TPU v7x, 32 devices: a whole 2x2x4 slice. The times are simulated.
32 devices in a mesh: angle: 4 (over y, core), tile: 8 (over z, x).
Axes of the slice: x: 2, y: 2, z: 4, core: 2. Of those that a mesh axis runs over, the one named last changes fastest.
Arguments:
- psi: float32 [2, 4, 160, 1024], P(None, 'angle', None, 'tile'), may hold values from -6 to 6
- target: float32 [2, 4, 160, 1024], P(None, 'angle', None, 'tile'), may hold values from -6 to 6
- probe: float32 [2, 128, 128], replicated, may hold values from -4.2 to 4.2
- data: float32 [4, 8, 16, 128, 128], P('angle', 'tile'), may hold values from 0.1 to 10
- pos_z: int32 [4, 8, 16], P('angle', 'tile'), may hold values from 0 to 32
- pos_x: int32 [4, 8, 16], P('angle', 'tile'), may hold values from 0 to 127
- counts: int32 [4, 8], P('angle', 'tile'), may hold values from 1 to 16, as said below
- shears: float32 [4], P('angle'), may hold values from -1 to 1
Outputs:
- psi_new: float32 [2, 4, 160, 1024], P(None, 'angle', None, 'tile')
- probe_new: float32 [2, 128, 128], replicated
- tomo_grad: bfloat16 [2, 160, 128, 1024], P(None, 'tile', 'angle')
Inputs may be any that keep to these rules, and one draw needn't show every extreme that they name: counts[a, t] positions of angle a lie in tile t, in slots 0 to counts[a, t] - 1; later slots are unused. Some tile of some angle has exactly 16 in every draw.
All inputs are finite; a program needn't handle non-finite values.
Results may differ from a plain program's by a relative error of at most 0.001.
Values sent between devices are 32-bit elements; how exact they have to be, the bound alone decides.
No kernel may reach another device: no remote copies, remote signals or barrier semaphores. Data moves between devices by JAX's collectives and lax.ppermute only.
A program may use at most 192 MiB of HBM per device.

v0:
```python
import math

import jax
import jax.numpy as jnp
from jax import lax
from jax.sharding import PartitionSpec as P

YB = 32
ITERS = 2


ALPHA = 0.004
RHO = 5.0
PROBE_STEP = 0.02
HIGHEST = lax.Precision.HIGHEST


def extended_2(block, sides, width):
    for axis, dim in sides:
        count = lax.axis_size(axis)
        forward = [(i, i + 1) for i in range(count - 1)]
        backward = [(target, source) for source, target in forward]
        low = lax.ppermute(
            lax.slice_in_dim(block, block.shape[dim] - width, None, axis=dim), axis, forward
        )
        high = lax.ppermute(lax.slice_in_dim(block, 0, width, axis=dim), axis, backward)
        block = jnp.concatenate([low, block, high], axis=dim)
    return block


def twin_einsum(pattern, left_real, left_imag, right_real, right_imag):
    real_part = jnp.einsum(pattern, left_real, right_real, precision=HIGHEST) - jnp.einsum(
        pattern, left_imag, right_imag, precision=HIGHEST
    )
    imag_part = jnp.einsum(pattern, left_real, right_imag, precision=HIGHEST) + jnp.einsum(
        pattern, left_imag, right_real, precision=HIGHEST
    )
    return (real_part, imag_part)


def phase_table(integers, modulus, orient):
    radians = 2.0 * math.pi / modulus * (integers % modulus).astype(jnp.float32)
    return (jnp.cos(radians), orient * jnp.sin(radians))


def square_table(length, orient):
    counter = lax.iota(jnp.int32, length)
    return phase_table(counter[:, None] * counter[None, :], length, orient)


def twiddle_table(inner, outer, orient):
    coarse = lax.iota(jnp.int32, outer)
    fine = lax.iota(jnp.int32, inner)
    return phase_table(coarse[:, None] * fine[None, :], inner * outer, orient)


def forward_rows(values_real, values_imag, inner, outer):
    leading = values_real.shape[:-1]
    shaped_real = values_real.reshape(leading + (outer, inner))
    shaped_imag = values_imag.reshape(leading + (outer, inner))
    outer_real, outer_imag = square_table(outer, -1.0)
    inner_real, inner_imag = square_table(inner, -1.0)
    twist_real, twist_imag = twiddle_table(inner, outer, -1.0)
    first_real, first_imag = twin_einsum(
        "...ab,ac->...cb", shaped_real, shaped_imag, outer_real, outer_imag
    )
    turned_real = first_real * twist_real - first_imag * twist_imag
    turned_imag = first_real * twist_imag + first_imag * twist_real
    final_real, final_imag = twin_einsum(
        "...cb,bd->...cd", turned_real, turned_imag, inner_real, inner_imag
    )
    return (
        final_real.reshape(leading + (inner * outer,)),
        final_imag.reshape(leading + (inner * outer,)),
    )


def inverse_rows(values_real, values_imag, inner, outer):
    leading = values_real.shape[:-1]
    shaped_real = values_real.reshape(leading + (outer, inner))
    shaped_imag = values_imag.reshape(leading + (outer, inner))
    outer_real, outer_imag = square_table(outer, 1.0)
    inner_real, inner_imag = square_table(inner, 1.0)
    twist_real, twist_imag = twiddle_table(inner, outer, 1.0)
    first_real, first_imag = twin_einsum(
        "...ab,bc->...ac", shaped_real, shaped_imag, inner_real, inner_imag
    )
    turned_real = first_real * twist_real - first_imag * twist_imag
    turned_imag = first_real * twist_imag + first_imag * twist_real
    final_real, final_imag = twin_einsum(
        "...ac,ad->...dc", turned_real, turned_imag, outer_real, outer_imag
    )
    scale = 1.0 / (inner * outer)
    return (
        final_real.reshape(leading + (inner * outer,)) * scale,
        final_imag.reshape(leading + (inner * outer,)) * scale,
    )


def pattern_transform(field_real, field_imag, table_real, table_imag):
    middle_real, middle_imag = twin_einsum(
        "mn,pnq->pmq", table_real, table_imag, field_real, field_imag
    )
    return twin_einsum("pmq,qr->pmr", middle_real, middle_imag, table_real, table_imag)


def shards(psi, target, probe, data, pos_z, pos_x, counts, shears):
    angle_count = psi.shape[1]
    rows_total = psi.shape[2]
    tile_width = psi.shape[3]
    patch_side = probe.shape[1]
    half = patch_side // 2
    slot_count = data.shape[2]
    tiles = lax.axis_size("tile")
    wide_cols = tile_width + patch_side
    norm_factor = 1.0 / math.sqrt(patch_side)
    fwd_real, fwd_imag = square_table(patch_side, -1.0)
    inv_real, inv_imag = square_table(patch_side, 1.0)
    fwd_real, fwd_imag = (fwd_real * norm_factor, fwd_imag * norm_factor)
    inv_real, inv_imag = (inv_real * norm_factor, inv_imag * norm_factor)
    slot_mask = (
        (lax.iota(jnp.int32, slot_count)[None, :] < counts[:, 0][:, None])
        .astype(jnp.float32)
        .reshape(-1)
    )
    angle_ids = jnp.repeat(jnp.arange(angle_count, dtype=jnp.int32), slot_count)
    starts_z = pos_z.reshape(-1)
    starts_x = pos_x.reshape(-1)
    data_flat = data.reshape(-1, patch_side, patch_side)
    local_count = jnp.sum(counts).astype(jnp.float32)
    zero_index = jnp.zeros((), jnp.int32)
    window_index = lax.iota(jnp.int32, patch_side)
    place_cols = (
        lax.iota(jnp.int32, wide_cols)[None, None, :]
        == (starts_x[:, None] + window_index[None, :])[:, :, None]
    ).astype(jnp.float32)
    place_rows = (
        lax.iota(jnp.int32, rows_total)[None, None, :]
        == (starts_z[:, None] + window_index[None, :])[:, :, None]
    ).astype(jnp.float32)
    place_rows = place_rows.reshape(angle_count, slot_count, patch_side, rows_total)
    field = psi
    probe_now = probe
    for step in range(ITERS):
        extended = extended_2(field, (("tile", 3),), half)

        def cut_patch(angle_id, start_z, start_x):
            return lax.dynamic_slice(
                extended, (zero_index, angle_id, start_z, start_x), (2, 1, patch_side, patch_side)
            )[:, 0]

        patches = jax.vmap(cut_patch)(angle_ids, starts_z, starts_x)
        patch_real = patches[:, 0]
        patch_imag = patches[:, 1]
        exit_real = probe_now[0] * patch_real - probe_now[1] * patch_imag
        exit_imag = probe_now[0] * patch_imag + probe_now[1] * patch_real
        far_real, far_imag = pattern_transform(exit_real, exit_imag, fwd_real, fwd_imag)
        misfit = (far_real * far_real + far_imag * far_imag - data_flat) * slot_mask[:, None, None]
        back_real, back_imag = pattern_transform(
            misfit * far_real, misfit * far_imag, inv_real, inv_imag
        )
        grad_real = probe_now[0] * back_real + probe_now[1] * back_imag
        grad_imag = probe_now[0] * back_imag - probe_now[1] * back_real
        probe_part = jnp.stack(
            [
                jnp.sum(patch_real * back_real + patch_imag * back_imag, 0),
                jnp.sum(patch_real * back_imag - patch_imag * back_real, 0),
            ]
        )
        stacked_grad = jnp.stack([grad_real, grad_imag], 1)
        widened = jnp.einsum("spre,sew->psrw", stacked_grad, place_cols, precision=HIGHEST)
        widened = widened.reshape(2, angle_count, slot_count, patch_side, wide_cols)
        total = jnp.einsum("pasrw,asrz->pazw", widened, place_rows, precision=HIGHEST)
        own = total[:, :, :, half : half + tile_width]
        rims = jnp.concatenate([total[:, :, :, :half], total[:, :, :, half + tile_width :]], 3)
        returned = extended_2(rims, (("tile", 3),), half)
        own = own.at[:, :, :, :half].add(returned[:, :, :, :half])
        own = own.at[:, :, :, tile_width - half :].add(returned[:, :, :, half + patch_side :])
        probe_grad, count_total = lax.psum((probe_part, local_count), ("angle", "tile"))
        new_field = field - ALPHA * (own + RHO * (field - target))
        probe_now = probe_now - PROBE_STEP * probe_grad / count_total
        field = new_field
    misfit_rows = target - field
    slab = lax.all_to_all(misfit_rows, "tile", split_axis=2, concat_axis=3, tiled=True)
    spec_real, spec_imag = forward_rows(slab[0], slab[1], tile_width, tiles)
    spectra, all_shears = (
        lax.all_gather(jnp.stack([spec_real, spec_imag]), "angle", axis=1, tiled=True),
        lax.all_gather(shears, "angle", axis=0, tiled=True),
    )
    width = spectra.shape[-1]
    total_angles = all_shears.shape[0]
    band_rows = YB
    beam_rows = band_rows * lax.axis_size("angle")
    first_row = lax.axis_index("angle") * band_rows - beam_rows // 2
    offsets = first_row + lax.iota(jnp.int32, band_rows)
    position = lax.iota(jnp.int32, width)
    frequency = position // tile_width + tiles * (position % tile_width)
    signed = jnp.where(frequency < width // 2, frequency, frequency - width)
    product = (offsets[:, None] * signed[None, :]).astype(jnp.float32)
    theta = product[:, None, :] * all_shears[None, :, None] * (2.0 * math.pi / width)
    shift_real = jnp.cos(theta)
    shift_imag = jnp.sin(theta)
    summed_real, summed_imag = twin_einsum(
        "yak,azk->zyk", shift_real, shift_imag, spectra[0], spectra[1]
    )
    image_real, image_imag = inverse_rows(summed_real, summed_imag, tile_width, tiles)
    tomo = jnp.stack([image_real, image_imag]) / total_angles
    return (field, probe_now, tomo.astype(jnp.bfloat16))


def solution(mesh):
    in_specs = (
        P(None, "angle", None, "tile"),
        P(None, "angle", None, "tile"),
        P(),
        P("angle", "tile", None, None, None),
        P("angle", "tile", None),
        P("angle", "tile", None),
        P("angle", "tile"),
        P("angle"),
    )
    out_specs = (P(None, "angle", None, "tile"), P(), P(None, "tile", "angle", None))
    return jax.shard_map(shards, mesh=mesh, in_specs=in_specs, out_specs=out_specs, check_vma=False)
```

profile of v0, /device:TPU:0, one launch (start us, length us, event | category | flops | bytes accessed | tf_op | source)
XLA Modules:
  0.0 719.5 jit_solution(10539707067531472050)
XLA Ops:
  8.3 4.9 collective-permute-start
  16.1 41.7 %psum.25 = f32[]{:T(128)} all-reduce(f32[]{:T(128)S(6)} %convert_element_type.155), channel_id=1, replica_groups=mesh['angle'=4,'tile'=8] {'angle','tile'}, use_global_device_ids=true, to_apply=%region_3.4 | all-reduce | flops 1 | bytes 8 | tf_op jit(solution)/shard_map/psum | solution.py:179
  64.8 32.2 %while.6 = (s32[]{:T(128)}, f32[2,1,160,256]{3,2,1,0:T(8,128)S(1)}, s32[16,4]{0,1:T(4,128)S(1)}, f32[16,2,1,128,128]{4,3,0,1,2:T(8,128)S(1)}, s32[]{:T(128)}) while((s32[]{:T(128)}, f32[2,1,160,256]{3,2,1,0:T(8,128)S(1)}, s32[16,4]{0,1:T(4,128)S(1)}, f32[16,2,1,128,128]{4,3,0,1,2:T(8,128)S(1)}, s32[]{:T(128)}) %tuple.81), condition=%wide.while_cond.4, body=%wide.while_body.4.sunk | while | flops 2 | bytes 262269 | solution.py:148
  127.5 3.7 add_reduce_fusion.1
  132.0 3.7 fusion.5
  135.7 2.6 fusion.39
  138.5 4.2 collective-permute-start.2
  144.0 111.5 %all-reduce.4.cloned.1.call-done = f32[2,128,128]{2,1,0:T(8,128)} async-done(((f32[2,128,128]{2,1,0:T(8,128)}), f32[2,128,128]{2,1,0:T(8,128)}) %all-reduce.4.cloned.1.call-update) | async-done | bytes 131088 | tf_op jit(solution)/shard_map/psum | solution.py:179
  259.0 3.4 collective-permute-start.4
  263.7 3.2 collective-permute-done.4
  266.9 2.6 collective-permute-done.5
  270.8 48.7 %while.7 = (s32[]{:T(128)}, f32[2,1,160,256]{3,2,1,0:T(8,128)}, s32[16,4]{0,1:T(4,128)S(1)}, f32[16,2,1,128,128]{4,3,0,1,2:T(8,128)S(1)}, s32[]{:T(128)}) while((s32[]{:T(128)}, f32[2,1,160,256]{3,2,1,0:T(8,128)}, s32[16,4]{0,1:T(4,128)S(1)}, f32[16,2,1,128,128]{4,3,0,1,2:T(8,128)S(1)}, s32[]{:T(128)}) %tuple.91), condition=%wide.while_cond.5, body=%wide.while_body.5.sunk | while | flops 2 | bytes 262269 | solution.py:148
  271.4 2.3 bitcast_dynamic-update-slice_fusion.5
  277.5 2.3 bitcast_dynamic-update-slice_fusion.5
  280.5 2.3 bitcast_dynamic-update-slice_fusion.5
  286.6 2.3 bitcast_dynamic-update-slice_fusion.5
  289.6 2.3 bitcast_dynamic-update-slice_fusion.5
  295.7 2.3 bitcast_dynamic-update-slice_fusion.5
  298.7 2.3 bitcast_dynamic-update-slice_fusion.5
  304.8 2.3 bitcast_dynamic-update-slice_fusion.5
  307.8 2.3 bitcast_dynamic-update-slice_fusion.5
  343.7 2.4 fusion.131
  350.0 2.4 add_reduce_fusion
  354.6 2.9 fusion.44
  357.7 4.2 collective-permute-start.6
  364.0 2.6 collective-permute-done.6
  371.7 4.1 all-to-all-start
  375.9 6.9 all-reduce
  383.0 104.4 %all-reduce.6.cloned.1.call-done = f32[2,128,128]{2,1,0:T(8,128)} async-done(((f32[2,128,128]{2,1,0:T(8,128)}), f32[2,128,128]{2,1,0:T(8,128)}) %all-reduce.6.cloned.1.call-update) | async-done | bytes 131088 | tf_op jit(solution)/shard_map/psum | solution.py:179
  492.9 7.9 %all_gather.6 = f32[2,4,20,1024]{3,0,2,1:T(2,128)S(1)} all-gather(f32[2,1,20,1024]{3,0,2,1:T(2,128)S(1)} %pad_maximum_fusion.1), channel_id=1, replica_groups=mesh['angle'=4,'tile'=8] {'angle'}, dimensions={1}, use_global_device_ids=true | all-gather | bytes 819200 | tf_op jit(solution)/shard_map/all_gather | solution.py:187
  501.3 2.4 copy.260
  505.2 36.7 %fusion.13 = f32[1024,20,32]{2,1,0:T(8,128)} fusion(f32[1,4,20,1024]{2,1,3,0:T(4,128)} %copy.260, f32[4]{0:T(128)S(1)} %all-reduce, f32[32,1024]{0,1:T(8,128)S(1)} %copy.208), kind=kOutput, calls=%fused_computation.24 | convolution fusion | flops 31719424 | bytes 3080208 | tf_op jit(solution)/shard_map/yak,azk->zyk/dot_general | solution.py:35
  541.9 33.6 %fusion.17 = f32[1024,20,32]{2,1,0:T(8,128)S(1)} fusion(f32[1,4,20,1024]{2,1,3,0:T(4,128)S(1)} %copy.259, f32[4]{0:T(128)S(1)} %all-reduce, f32[32,1024]{0,1:T(8,128)S(1)} %copy.208), kind=kOutput, calls=%fused_computation.28 | convolution fusion | flops 31719424 | bytes 3080208 | tf_op jit(solution)/shard_map/yak,azk->zyk/dot_general | solution.py:32
  575.5 36.5 %convolution_subtract_fusion = f32[1024,20,32]{2,1,0:T(8,128)} fusion(f32[1024,20,32]{2,1,0:T(8,128)S(1)} %fusion.17, f32[1,4,20,1024]{2,1,3,0:T(4,128)S(1)} %copy-done.1, f32[4]{0:T(128)S(1)} %all-reduce, f32[32,1024]{0,1:T(8,128)S(1)} %copy.208), kind=kOutput, calls=%fused_computation.7 | convolution fusion | flops 32374784 | bytes 5701648 | tf_op jit(solution)/shard_map/yak,azk->zyk/dot_general | solution.py:32
  612.0 8.2 %copy.210 = f32[20,32,8,128]{3,2,1,0:T(8,128)} copy(f32[20,32,8,128]{1,0,3,2:T(8,128)} %bitcast.421) | data formatting | bytes 5242880 | tf_op jit(solution)/shard_map/reshape | solution.py:80
  620.2 5.8 fusion.99
  626.0 3.9 fusion.101
  630.0 37.4 %convolution_add_fusion = f32[1024,20,32]{2,1,0:T(8,128)} fusion(f32[1024,20,32]{2,1,0:T(8,128)} %fusion.13, f32[1,4,20,1024]{2,1,3,0:T(4,128)S(1)} %copy.259, f32[4]{0:T(128)S(1)} %all-reduce, f32[32,1024]{0,1:T(8,128)S(1)} %copy.208), kind=kOutput, calls=%fused_computation.6 | convolution fusion | flops 32374784 | bytes 5701648 | tf_op jit(solution)/shard_map/yak,azk->zyk/dot_general | solution.py:35
  667.4 8.4 %copy.211 = f32[20,32,8,128]{3,2,1,0:T(8,128)} copy(f32[20,32,8,128]{1,0,3,2:T(8,128)} %bitcast.420) | data formatting | bytes 5242880 | tf_op jit(solution)/shard_map/reshape | solution.py:81
  675.9 5.1 convolution_subtract_fusion.1
  681.0 2.5 convolution_add_fusion.1
  683.6 2.6 fusion.72
  686.2 3.9 fusion.71
  690.0 4.3 multiply_bitcast_fusion.1
  694.4 3.8 mul.1062
  698.1 6.5 multiply_bitcast_fusion
  704.6 3.9 mul.1065
  708.5 3.9 fusion
  (214 shorter events, 152.3 us)
Async XLA Ops:
  7.2 248.4 %all-reduce.4.cloned.1.call-start = ((), (), s32[]{:S(2)}) async-start(), calls=%async_computation.1 | async-start | bytes 262144 | tf_op jit(solution)/shard_map/psum | solution.py:179
  8.3 55.1 %collective-permute-start = (f32[2,1,160,64]{3,2,1,0:T(8,128)S(1)}, f32[2,1,160,64]{3,2,1,0:T(8,128)S(1)}, u32[]{:S(2)}, u32[]{:S(2)}) collective-permute-start(f32[2,1,160,64]{3,2,1,0:T(8,128)S(1)} %get-tuple-element.141), channel_id=1, source_target_pairs={{0,1},{1,2},{2,3},{3,4},{4,5},{5,6},{6,7},{8,9},{9,10},{10,11},{11... | collective-permute-start | bytes 245768 | tf_op jit(solution)/shard_map/ppermute | solution.py:23
  13.2 50.2 %collective-permute-start.1 = (f32[2,1,160,64]{3,2,1,0:T(8,128)S(1)}, f32[2,1,160,64]{3,2,1,0:T(8,128)S(1)}, u32[]{:S(2)}, u32[]{:S(2)}) collective-permute-start(f32[2,1,160,64]{3,2,1,0:T(8,128)S(1)} %get-tuple-element.142), channel_id=1, source_target_pairs={{1,0},{2,1},{3,2},{4,3},{5,4},{6,5},{7,6},{9,8},{10,9},{11,10},{12... | collective-permute-start | bytes 245768 | tf_op jit(solution)/shard_map/ppermute | solution.py:26
  107.0 4.2 copy-start.6
  131.9 355.5 %all-reduce.6.cloned.1.call-start = ((), (), s32[]{:S(2)}) async-start(), calls=%async_computation.2 | async-start | bytes 262144 | tf_op jit(solution)/shard_map/psum | solution.py:179
  135.7 119.8 %copy-start.13 = (f32[2,128,128]{2,1,0:T(8,128)S(1)}, f32[2,128,128]{2,1,0:T(8,128)}, u32[]{:S(2)}) copy-start(f32[2,128,128]{2,1,0:T(8,128)} %param.18) | copy-start | bytes 393220
  138.3 120.6 %copy-start.7 = (f32[2,1,160,128]{3,2,1,0:T(8,128)S(1)}, f32[2,1,160,128]{3,2,1,0:T(8,128)}, u32[]{:S(2)}) copy-start(f32[2,1,160,128]{3,2,1,0:T(8,128)} %param.16) | copy-start | bytes 491524
  138.3 120.6 %copy-start.10 = (f32[2,1,160,128]{3,2,1,0:T(8,128)S(1)}, f32[2,1,160,128]{3,2,1,0:T(8,128)}, u32[]{:S(2)}) copy-start(f32[2,1,160,128]{3,2,1,0:T(8,128)} %param.17) | copy-start | bytes 491524
  138.5 118.6 %collective-permute-start.2 = (f32[2,1,160,64]{3,2,0,1:T(8,128)S(1)}, f32[2,1,160,64]{3,2,0,1:T(8,128)S(1)}, u32[]{:S(2)}, u32[]{:S(2)}) collective-permute-start(f32[2,1,160,64]{3,2,0,1:T(8,128)S(1)} %get-tuple-element.138), channel_id=1, source_target_pairs={{0,1},{1,2},{2,3},{3,4},{4,5},{5,6},{6,7},{8,9},{9,10},{10,11},{11... | collective-permute-start | bytes 245768 | tf_op jit(solution)/shard_map/ppermute | solution.py:23
  142.7 115.1 %collective-permute-start.3 = (f32[2,1,160,64]{3,2,0,1:T(8,128)S(1)}, f32[2,1,160,64]{3,2,0,1:T(8,128)S(1)}, u32[]{:S(2)}, u32[]{:S(2)}) collective-permute-start(f32[2,1,160,64]{3,2,0,1:T(8,128)S(1)} %get-tuple-element.137), channel_id=1, source_target_pairs={{1,0},{2,1},{3,2},{4,3},{5,4},{6,5},{7,6},{9,8},{10,9},{11,10},{12... | collective-permute-start | bytes 245768 | tf_op jit(solution)/shard_map/ppermute | solution.py:26
  257.1 12.5 %copy-start.8 = (f32[2,128,128]{2,1,0:T(8,128)}, f32[2,128,128]{2,1,0:T(8,128)S(1)}, u32[]{:S(2)}) copy-start(f32[2,128,128]{2,1,0:T(8,128)S(1)} %divide_subtract_fusion.1) | copy-start | bytes 393220
  259.0 7.9 %collective-permute-start.4 = (f32[2,1,160,64]{3,2,0,1:T(8,128)S(1)}, f32[2,1,160,64]{3,2,0,1:T(8,128)S(1)}, u32[]{:S(2)}, u32[]{:S(2)}) collective-permute-start(f32[2,1,160,64]{3,2,0,1:T(8,128)S(1)} %get-tuple-element.139), channel_id=1, source_target_pairs={{0,1},{1,2},{2,3},{3,4},{4,5},{5,6},{6,7},{8,9},{9,10},{10,11},{11... | collective-permute-start | bytes 245768 | tf_op jit(solution)/shard_map/ppermute | solution.py:23
  262.4 7.2 %collective-permute-start.5 = (f32[2,1,160,64]{3,2,0,1:T(8,128)S(1)}, f32[2,1,160,64]{3,2,0,1:T(8,128)S(1)}, u32[]{:S(2)}, u32[]{:S(2)}) collective-permute-start(f32[2,1,160,64]{3,2,0,1:T(8,128)S(1)} %get-tuple-element.140), channel_id=1, source_target_pairs={{1,0},{2,1},{3,2},{4,3},{5,4},{6,5},{7,6},{9,8},{10,9},{11,10},{12... | collective-permute-start | bytes 245768 | tf_op jit(solution)/shard_map/ppermute | solution.py:26
  357.5 12.8 %copy-start.11 = (f32[2,1,160,128]{3,2,1,0:T(8,128)S(1)}, f32[2,1,160,128]{3,2,1,0:T(8,128)}, u32[]{:S(2)}) copy-start(f32[2,1,160,128]{3,2,1,0:T(8,128)} %param.17) | copy-start | bytes 491524
  357.5 25.3 %copy-start.12 = (f32[32,1024]{1,0:T(8,128)S(1)}, f32[32,1024]{1,0:T(8,128)}, u32[]{:S(2)}) copy-start(f32[32,1024]{1,0:T(8,128)} %multiply_convert_fusion) | copy-start | bytes 393220
  357.5 130.0 %copy-start.9 = (f32[2,128,128]{2,1,0:T(8,128)S(1)}, f32[2,128,128]{2,1,0:T(8,128)}, u32[]{:S(2)}) copy-start(f32[2,128,128]{2,1,0:T(8,128)} %copy-done.8) | copy-start | bytes 393220
  357.7 8.8 %collective-permute-start.6 = (f32[2,1,160,64]{3,2,0,1:T(8,128)S(1)}, f32[2,1,160,64]{3,2,0,1:T(8,128)S(1)}, u32[]{:S(2)}, u32[]{:S(2)}) collective-permute-start(f32[2,1,160,64]{3,2,0,1:T(8,128)S(1)} %get-tuple-element.136), channel_id=1, source_target_pairs={{0,1},{1,2},{2,3},{3,4},{4,5},{5,6},{6,7},{8,9},{9,10},{10,11},{11... | collective-permute-start | bytes 245768 | tf_op jit(solution)/shard_map/ppermute | solution.py:23
  362.0 7.2 %collective-permute-start.7 = (f32[2,1,160,64]{3,2,0,1:T(8,128)S(1)}, f32[2,1,160,64]{3,2,0,1:T(8,128)S(1)}, u32[]{:S(2)}, u32[]{:S(2)}) collective-permute-start(f32[2,1,160,64]{3,2,0,1:T(8,128)S(1)} %get-tuple-element.135), channel_id=1, source_target_pairs={{1,0},{2,1},{3,2},{4,3},{5,4},{6,5},{7,6},{9,8},{10,9},{11,10},{12... | collective-permute-start | bytes 245768 | tf_op jit(solution)/shard_map/ppermute | solution.py:26
  371.7 118.0 %all-to-all-start = ((f32[2,1,160,128]{3,0,1,2:T(2,128)}), f32[2,1,160,128]{3,0,1,2:T(2,128)S(1)}, u32[]{:S(2)}, u32[]{:S(2)}) async-start(f32[2,1,160,128]{3,0,1,2:T(2,128)} %copy.203), calls=%async_computation | async-start | bytes 327680 | tf_op jit(solution)/shard_map/all_to_all | solution.py:184
  541.9 33.6 %copy-start.1 = (f32[1,4,20,1024]{2,1,3,0:T(4,128)S(1)}, f32[1,4,20,1024]{2,1,3,0:T(4,128)}, u32[]{:S(2)}) copy-start(f32[1,4,20,1024]{2,1,3,0:T(4,128)} %copy.260) | copy-start | bytes 983044
  620.2 5.8 copy-start.2
  675.8 5.2 copy-start.3
  675.9 5.2 copy-start.4
  683.6 6.5 copy-start
  704.6 3.9 copy-start.5
Sparse Core Ops, SparseCore 0:
  132.0 123.4 all-reduce.3
  364.1 123.3 all-reduce.5
where the time goes:
time: 731 us; the launch traced here: 720 us
  matrix products  260 us (36%)
  waiting for transfers between devices  226 us (31%)
  local copies, waits for them, and re-layouts  118 us (16%)
  blocking collectives  56.5 us (8%)
  starting transfers between devices  26 us (4%)
  between operations  16.4 us (2%)
  other arithmetic  15.5 us (2%)
    psum x2, waiting for transfers between devices, shards(): lax.psum((probe_part, local_count), ('angle', 'tile'))  216 us
    gather x96, local copies, waits for them, and re-layouts  80.1 us
    dot_general x13, matrix products, twin_einsum(): jnp.einsum(pattern, left_imag, right_imag, precision=HIGHEST)  65 us
    dot_general x13, matrix products, twin_einsum(): jnp.einsum(pattern, left_imag, right_real, precision=HIGHEST)  63.6 us
    dot_general x13, matrix products, twin_einsum(): jnp.einsum(pattern, left_real, right_imag, precision=HIGHEST)  61 us
    dot_general x13, matrix products, twin_einsum(): jnp.einsum(pattern, left_real, right_real, precision=HIGHEST)  59.2 us
    psum x1, blocking collectives, shards(): lax.psum((probe_part, local_count), ('angle', 'tile'))  41.7 us
    ppermute x4, starting transfers between devices, extended_2(): lax.ppermute(lax.slice_in_dim(block, block.shape[dim] - width, None, axis...  16.7 us
  transfers between devices with their start and end apart: 11, of which 6 were waited for; matrix products, arithmetic and copies ran while one was open for 3% of the time, Pallas kernels for 0%

commit v1 on v0

v1 whole, which is shorter than its diff:
```python
import functools
import math

import jax
import jax.numpy as jnp
import ml_dtypes
import numpy as np
from jax import lax
from jax.experimental import pallas as pl
from jax.experimental.pallas import tpu as pltpu
from jax.sharding import PartitionSpec as P

ITERS = 2
ALPHA = 0.004
RHO = 5.0
PROBE_STEP = 0.02
GROUP = 4
VMEM_LIMIT = 40 * 1024 * 1024
BF16 = jnp.bfloat16
F32 = jnp.float32


def split_table(matrix, axis):
    high = matrix.astype(ml_dtypes.bfloat16)
    low = (matrix - high.astype(np.float64)).astype(ml_dtypes.bfloat16)
    return np.concatenate([high, high, low], axis)


def dft_parts(length, orient, scale):
    counter = np.arange(length)
    angle = 2.0 * math.pi / length * (np.outer(counter, counter) % length)
    return np.cos(angle) * scale, orient * np.sin(angle) * scale


def right_table(length, orient, scale):
    real, imag = dft_parts(length, orient, scale)
    return split_table(np.block([[real, imag], [-imag, real]]), 0)


def left_table(length, orient, scale):
    real, imag = dft_parts(length, orient, scale)
    return split_table(np.block([[real, -imag], [imag, real]]), 1)


def twiddles(tiles, inner, orient, scale):
    angle = 2.0 * math.pi / (tiles * inner) * np.outer(np.arange(tiles), np.arange(inner))
    return np.stack([np.cos(angle) * scale, orient * np.sin(angle) * scale]).astype(np.float32)


def halves(value):
    high = value.astype(BF16)
    low = (value - high.astype(F32)).astype(BF16)
    return high, low


def dot(left, right):
    return jnp.dot(left, right, preferred_element_type=F32)


def butterfly(parts, orient):
    count = len(parts)
    if count == 1:
        return parts
    even = butterfly(parts[0::2], orient)
    odd = butterfly(parts[1::2], orient)
    low, high = [], []
    for index in range(count // 2):
        angle = orient * 2.0 * math.pi * index / count
        real, imag = odd[index]
        if index == 0:
            turned = (real, imag)
        elif 4 * index == count:
            turned = (-imag, real) if orient > 0 else (imag, -real)
        else:
            cosine, sine = math.cos(angle), math.sin(angle)
            turned = (real * cosine - imag * sine, real * sine + imag * cosine)
        base_real, base_imag = even[index]
        low.append((base_real + turned[0], base_imag + turned[1]))
        high.append((base_real - turned[0], base_imag - turned[1]))
    return low + high


def lane_mask(shape, half):
    return lax.broadcasted_iota(jnp.int32, shape, len(shape) - 1) < half


def slot_loop(pos_z, pos_x, count, probe_real, probe_imag, data, tables, own, halo, work):
    right_fwd, left_fwd, left_inv, right_inv = tables
    grad_own, grad_halo, grad_probe, patches, high_rows, low_rows = work
    side = data.shape[-1]
    half = side // 2
    lanes = lax.broadcasted_iota(jnp.int32, (side, side), 1)
    grad_own[...] = jnp.zeros_like(grad_own)
    grad_halo[...] = jnp.zeros_like(grad_halo)
    grad_probe[...] = jnp.zeros_like(grad_probe)

    def place(slot):
        start = pos_x[0, 0, slot] - half
        back = jnp.where(start > 0, side - start, -start)
        forth = jnp.where(start < 0, side + start, start)
        inside = (lanes >= start) & (lanes < side + start)
        return pos_z[0, 0, slot], back, forth, inside

    def group(index, carry):
        first = index * GROUP
        for member in range(GROUP):
            row, back, _, inside = place(first + member)
            cut = []
            for part in range(2):
                mixed = jnp.where(
                    inside, own[part, pl.ds(row, side), :], halo[part, pl.ds(row, side), :]
                )
                cut.append(pltpu.roll(mixed, back, 1))
                patches[member, part] = cut[part]
            exit_wave = jnp.concatenate(
                [
                    probe_real[...] * cut[0] - probe_imag[...] * cut[1],
                    probe_real[...] * cut[1] + probe_imag[...] * cut[0],
                ],
                1,
            )
            high, low = halves(exit_wave)
            high_rows[pl.ds(member * side, side), :] = high
            low_rows[pl.ds(member * side, side), :] = low
        high, low = high_rows[...], low_rows[...]
        rows = dot(jnp.concatenate([high, low, high], 1), right_fwd[...])
        for pair in range(GROUP // 2):
            two = [rows[(2 * pair + k) * side : (2 * pair + k + 1) * side] for k in range(2)]
            stacked = jnp.concatenate(
                [
                    jnp.concatenate([block[:, :side] for block in two], 1),
                    jnp.concatenate([block[:, side:] for block in two], 1),
                ],
                0,
            )
            high, low = halves(stacked)
            far = dot(left_fwd[...], jnp.concatenate([high, low, high], 0))
            weights = []
            for k in range(2):
                slot = first + 2 * pair + k
                live = jnp.where(slot < count, 1.0, 0.0).astype(F32)
                far_real = far[:side, k * side : (k + 1) * side]
                far_imag = far[side:, k * side : (k + 1) * side]
                weights.append((far_real * far_real + far_imag * far_imag - data[0, 0, slot]) * live)
            weight = jnp.concatenate(weights, 1)
            high, low = halves(jnp.concatenate([far[:side] * weight, far[side:] * weight], 0))
            back_cols = dot(left_inv[...], jnp.concatenate([high, low, high], 0))
            for k in range(2):
                block = back_cols[:, k * side : (k + 1) * side]
                high, low = halves(jnp.concatenate([block[:side], block[side:]], 1))
                high_rows[pl.ds((2 * pair + k) * side, side), :] = high
                low_rows[pl.ds((2 * pair + k) * side, side), :] = low
        high, low = high_rows[...], low_rows[...]
        chi = dot(jnp.concatenate([high, low, high], 1), right_inv[...])
        sum_real, sum_imag = grad_probe[0], grad_probe[1]
        for member in range(GROUP):
            row, _, forth, inside = place(first + member)
            chi_real = chi[member * side : (member + 1) * side, :side]
            chi_imag = chi[member * side : (member + 1) * side, side:]
            cut_real, cut_imag = patches[member, 0], patches[member, 1]
            sum_real = sum_real + (cut_real * chi_real + cut_imag * chi_imag)
            sum_imag = sum_imag + (cut_real * chi_imag - cut_imag * chi_real)
            grads = (
                probe_real[...] * chi_real + probe_imag[...] * chi_imag,
                probe_real[...] * chi_imag - probe_imag[...] * chi_real,
            )
            for part in range(2):
                moved = pltpu.roll(grads[part], forth, 1)
                where = pl.ds(row, side)
                grad_own[part, where, :] += jnp.where(inside, moved, 0.0)
                grad_halo[part, where, :] += jnp.where(inside, 0.0, moved)
        grad_probe[0], grad_probe[1] = sum_real, sum_imag
        return carry

    lax.fori_loop(0, (count + GROUP - 1) // GROUP, group, 0)


def first_kernel(
    pos_z, pos_x, counts, shears, psi, target, left, right, probe, data, *rest
):
    tables = rest[:4]
    to_right, to_left, base_out, rim_out, sums_out = rest[4:9]
    halo, work = rest[9], rest[10:]
    grad_own, grad_halo, grad_probe = work[:3]
    side = data.shape[-1]
    mask = lane_mask(psi.shape[2:], side // 2)
    for part in range(2):
        halo[part] = jnp.where(mask, right[part, 0], left[part, 0])
    count = counts[0, 0]
    slot_loop(
        pos_z, pos_x, count, probe.at[0], probe.at[1], data, tables, psi.at[:, 0], halo, work
    )
    for part in range(2):
        field = psi[part, 0]
        base = field - ALPHA * (grad_own[part] + RHO * (field - target[part, 0]))
        rim = -ALPHA * grad_halo[part]
        base_out[part] = base
        rim_out[part] = rim
        to_right[part] = jnp.where(mask, rim, base)
        to_left[part] = jnp.where(mask, base, rim)
    devices, rows = sums_out.shape[0], sums_out.shape[1] - 8
    extra = jnp.where(
        lax.broadcasted_iota(jnp.int32, (8, side), 0) == 0,
        jnp.full((8, side), count.astype(F32)),
        jnp.full((8, side), shears[0]),
    )
    per_part = side // rows
    for device in range(devices):
        part, place = device // per_part, device % per_part
        sums_out[device, 0:rows] = grad_probe[part, place * rows : (place + 1) * rows]
        sums_out[device, rows : rows + 8] = extra


def chunk_kernel(received, probe, chunk_out, total_out):
    devices, rows = chunk_out.shape[0], chunk_out.shape[1]
    total = received[0]
    for device in range(1, devices):
        total = total + received[device]
    number = total[rows : rows + 1]
    me = lax.axis_index("angle") * lax.axis_size("tile") + lax.axis_index("tile")
    mine = probe[pl.ds(me, 1)][0] - PROBE_STEP * total[:rows] / number
    for device in range(devices):
        chunk_out[device] = mine
    total_out[...] = jnp.broadcast_to(number, total_out.shape)


def second_kernel(
    pos_z, pos_x, counts, base, rim, left, right, target, probe, data, *rest
):
    tables = rest[:4]
    slabs_out, base_out, rim_out = rest[4:7]
    own, halo, hold, work = rest[7], rest[8], rest[9], rest[10:]
    grad_own, grad_halo, grad_probe = work[:3]
    side = data.shape[-1]
    mask = lane_mask(base.shape[1:], side // 2)
    tile, tiles = lax.axis_index("tile"), lax.axis_size("tile")
    from_right = jnp.where(tile < tiles - 1, 1.0, 0.0).astype(F32)
    from_left = jnp.where(tile > 0, 1.0, 0.0).astype(F32)
    for part in range(2):
        own[part] = base[part] + jnp.where(mask, left[part], right[part])
        halo[part] = jnp.where(
            mask,
            (right[part] + rim[part]) * from_right,
            (left[part] + rim[part]) * from_left,
        )
    slot_loop(
        pos_z, pos_x, counts[0, 0], probe.at[0], probe.at[1], data, tables, own, halo, work
    )
    slabs, depth = slabs_out.shape[0], base.shape[1] // slabs_out.shape[0]
    chunk = slabs_out.shape[1] - 4 * depth
    for part in range(2):
        field = own[part]
        aim = target[part, 0]
        updated = field - ALPHA * (grad_own[part] + RHO * (field - aim))
        edge = -ALPHA * grad_halo[part]
        base_out[part] = updated
        rim_out[part] = edge
        hold[part] = aim - updated
    per_part = side // chunk
    for slab in range(slabs):
        rows = pl.ds(slab * depth, depth)
        for part in range(2):
            slabs_out[slab, part * depth : (part + 1) * depth] = hold[part, rows]
            slabs_out[slab, (2 + part) * depth : (3 + part) * depth] = rim_out[part, rows]
        part, place = slab // per_part, slab % per_part
        slabs_out[slab, 4 * depth : 4 * depth + chunk] = grad_probe[
            part, place * chunk : (place + 1) * chunk
        ]


def forward_kernel(slabs, turn, table, spectrum_out, rows_scratch):
    tiles, height, width = slabs.shape
    depth = rows_scratch.shape[0] // tiles
    chunk = height - 4 * depth
    mask = lane_mask((depth, width), width // 2)
    blocks = []
    for tile in range(tiles):
        block = []
        for part in range(2):
            rows = slice((2 + part) * depth, (3 + part) * depth)
            zero = jnp.zeros((depth, width), F32)
            before = slabs[tile - 1, rows] if tile > 0 else zero
            after = slabs[tile + 1, rows] if tile < tiles - 1 else zero
            block.append(
                slabs[tile, part * depth : (part + 1) * depth] - jnp.where(mask, before, after)
            )
        blocks.append(tuple(block))
    for index, (real, imag) in enumerate(butterfly(blocks, -1)):
        cosine, sine = turn[0, index : index + 1], turn[1, index : index + 1]
        rows = slice(index * depth, (index + 1) * depth)
        rows_scratch[rows, :width] = real * cosine - imag * sine
        rows_scratch[rows, width:] = real * sine + imag * cosine
    high, low = halves(rows_scratch[...])
    spectrum = dot(jnp.concatenate([high, low, high], 1), table[...])
    count = rows_scratch.shape[0]
    spectrum_out[0:count] = spectrum[:, :width]
    spectrum_out[count : 2 * count] = spectrum[:, width:]
    total = slabs[0, 4 * depth : 4 * depth + chunk]
    for tile in range(1, tiles):
        total = total + slabs[tile, 4 * depth : 4 * depth + chunk]
    spectrum_out[2 * count : 2 * count + chunk] = total


def phase_kernel(tiles, received, table_out):
    angles, _, _, beam, width = table_out.shape
    rows = received.shape[1] - 8
    total = tiles * width
    first = lax.axis_index("angle") * beam - (beam * lax.axis_size("angle")) // 2
    offsets = (lax.broadcasted_iota(jnp.int32, (beam, width), 0) + first).astype(F32)
    column = lax.broadcasted_iota(jnp.int32, (beam, width), 1)
    for angle in range(angles):
        shear = received[angle * tiles, rows + 1 : rows + 2]
        for block in range(tiles):
            frequency = block + tiles * column
            signed = jnp.where(frequency < total // 2, frequency, frequency - total).astype(F32)
            turns = (offsets * signed * shear) * (1.0 / total)
            turns = turns - jnp.floor(turns + 0.5)
            x = turns * math.pi
            square = x * x
            sine = x * (
                1.0 + square * (-1 / 6 + square * (1 / 120 + square * (-1 / 5040 + square * (
                    1 / 362880 + square * (-1 / 39916800 + square * (1.0 / 6227020800.0))))))
            )
            cosine = 1.0 + square * (-1 / 2 + square * (1 / 24 + square * (-1 / 720 + square * (
                1 / 40320 + square * (-1 / 3628800 + square * (1.0 / 479001600.0))))))
            table_out[angle, 0, block] = 1.0 - 2.0 * sine * sine
            table_out[angle, 1, block] = 2.0 * sine * cosine


def inverse_kernel(depth, spectra, phases, turn, table, image_out, high_rows, low_rows):
    angles, _, tiles, beam, width = phases.shape
    row = pl.program_id(0)
    count = tiles * depth
    for block in range(tiles):
        real = jnp.zeros((beam, width), F32)
        imag = jnp.zeros((beam, width), F32)
        for angle in range(angles):
            spec_real = spectra[angle, pl.ds(block * depth + row, 1), :]
            spec_imag = spectra[angle, pl.ds(count + block * depth + row, 1), :]
            cosine, sine = phases[angle, 0, block], phases[angle, 1, block]
            real = real + (cosine * spec_real - sine * spec_imag)
            imag = imag + (cosine * spec_imag + sine * spec_real)
        rows = slice(block * beam, (block + 1) * beam)
        for part, value in enumerate((real, imag)):
            high, low = halves(value)
            high_rows[rows, part * width : (part + 1) * width] = high
            low_rows[rows, part * width : (part + 1) * width] = low
    high, low = high_rows[...], low_rows[...]
    image = dot(jnp.concatenate([high, low, high], 1), table[...])
    blocks = []
    for block in range(tiles):
        real = image[block * beam : (block + 1) * beam, :width]
        imag = image[block * beam : (block + 1) * beam, width:]
        cosine, sine = turn[0, block : block + 1], turn[1, block : block + 1]
        blocks.append((real * cosine - imag * sine, real * sine + imag * cosine))
    for index, (real, imag) in enumerate(butterfly(blocks, 1)):
        columns = slice(index * width, (index + 1) * width)
        image_out[0, 0, :, columns] = real.astype(BF16)
        image_out[1, 0, :, columns] = imag.astype(BF16)


def last_kernel(probe_rows, spectra, probe, number, base, left, right, chunk_out, psi_out):
    angles, tiles, rows = spectra.shape[0], chunk_out.shape[0], chunk_out.shape[1]
    total = spectra[0, probe_rows : probe_rows + rows]
    for angle in range(1, angles):
        total = total + spectra[angle, probe_rows : probe_rows + rows]
    tile = lax.axis_index("tile")
    mine = probe[pl.ds(tile, 1)][0] - PROBE_STEP * total / number[0:1]
    for place in range(tiles):
        chunk_out[place] = mine
    mask = lane_mask(base.shape[1:], base.shape[-1] // 2)
    for part in range(2):
        psi_out[part, 0] = base[part] + jnp.where(mask, left[part], right[part])


VMEM = pl.BlockSpec(memory_space=pltpu.VMEM)
SMEM = pl.BlockSpec(memory_space=pltpu.SMEM)


def call(body, name, out_shape, in_specs, scratch=(), flops=0, size=0, **more):
    return pl.pallas_call(
        body,
        name=name,
        out_shape=out_shape,
        in_specs=in_specs,
        scratch_shapes=list(scratch),
        compiler_params=pltpu.CompilerParams(vmem_limit_bytes=VMEM_LIMIT),
        cost_estimate=pl.CostEstimate(flops=flops, bytes_accessed=size, transcendentals=0),
        **more,
    )


def shape(*dims, dtype=F32):
    return jax.ShapeDtypeStruct(dims, dtype)


def shards(psi, target, probe, data, pos_z, pos_x, counts, shears):
    rows_total, width = psi.shape[2], psi.shape[3]
    side = probe.shape[1]
    angles, tiles = lax.axis_size("angle"), lax.axis_size("tile")
    devices = angles * tiles
    depth = rows_total // tiles
    beam = 32
    both = ("angle", "tile")
    forward = [(i, i + 1) for i in range(tiles - 1)]
    backward = [(i + 1, i) for i in range(tiles - 1)]
    norm = 1.0 / math.sqrt(side)
    tables = [
        jnp.asarray(right_table(side, -1.0, norm)),
        jnp.asarray(left_table(side, -1.0, norm)),
        jnp.asarray(left_table(side, 1.0, norm)),
        jnp.asarray(right_table(side, 1.0, norm)),
    ]
    block = (2, rows_total, width)
    work = [
        pltpu.VMEM(block, F32),
        pltpu.VMEM(block, F32),
        pltpu.VMEM((2, side, side), F32),
        pltpu.VMEM((GROUP, 2, side, side), F32),
        pltpu.VMEM((GROUP * side, 2 * side), BF16),
        pltpu.VMEM((GROUP * side, 2 * side), BF16),
    ]
    slots = data.shape[2]
    flops = slots * 4 * 2 * side * 6 * side * 2 * side
    left = lax.ppermute(psi, "tile", forward)
    right = lax.ppermute(psi, "tile", backward)
    chunk = 2 * side // devices
    to_right, to_left, base, rim, sums = call(
        first_kernel,
        "ptycho_first",
        [shape(*block)] * 4 + [shape(devices, chunk + 8, side)],
        [SMEM] * 4 + [VMEM] * 10,
        [pltpu.VMEM(block, F32)] + work,
        flops,
    )(pos_z, pos_x, counts, shears, psi, target, left, right, probe, data, *tables)
    left = lax.ppermute(to_right, "tile", forward)
    right = lax.ppermute(to_left, "tile", backward)
    received = lax.all_to_all(sums, both, 0, 0, tiled=True)
    chunks, number = call(
        chunk_kernel,
        "probe_chunk",
        [shape(devices, chunk, side), shape(8, side)],
        [VMEM] * 2,
    )(received, probe.reshape(devices, chunk, side))
    probe_one = lax.all_to_all(chunks, both, 0, 0, tiled=True).reshape(2, side, side)
    phases = call(
        functools.partial(phase_kernel, tiles),
        "phase_table",
        shape(angles, 2, tiles, beam, width),
        [VMEM],
        (),
        angles * tiles * beam * width * 40,
    )(received)
    piece = 2 * side // tiles
    slabs, base, rim = call(
        second_kernel,
        "ptycho_second",
        [shape(tiles, 4 * depth + piece, width), shape(*block), shape(*block)],
        [SMEM] * 3 + [VMEM] * 11,
        [pltpu.VMEM(block, F32)] * 3 + work,
        flops,
    )(pos_z, pos_x, counts, base, rim, left, right, target, probe_one, data, *tables)
    slabs = lax.all_to_all(slabs, "tile", 0, 0, tiled=True)
    left = lax.ppermute(rim, "tile", forward)
    right = lax.ppermute(rim, "tile", backward)
    count = tiles * depth
    spectrum = call(
        forward_kernel,
        "slab_spectrum",
        shape(2 * count + piece, width),
        [VMEM] * 3,
        [pltpu.VMEM((count, 2 * width), F32)],
    )(slabs, jnp.asarray(twiddles(tiles, width, -1.0, 1.0)), jnp.asarray(right_table(width, -1.0, 1.0)))
    spectra = lax.all_gather(spectrum, "angle", axis=0, tiled=False)
    chunks, psi_new = call(
        functools.partial(last_kernel, 2 * count),
        "probe_last",
        [shape(tiles, piece, side), shape(2, 1, rows_total, width)],
        [VMEM] * 6,
    )(spectra, probe_one.reshape(tiles, piece, side), number, base, left, right)
    probe_new = lax.all_to_all(chunks, "tile", 0, 0, tiled=True).reshape(2, side, side)
    scale = 1.0 / (angles * tiles * width)
    tomo = call(
        functools.partial(inverse_kernel, depth),
        "slab_image",
        shape(2, depth, beam, tiles * width, dtype=BF16),
        [VMEM] * 4,
        [pltpu.VMEM((tiles * beam, 2 * width), BF16)] * 2,
        depth * tiles * beam * 2 * 6 * width * 2 * width,
        grid=(depth,),
        out_specs=pl.BlockSpec((2, 1, beam, tiles * width), lambda row: (0, row, 0, 0)),
    )(
        spectra,
        phases,
        jnp.asarray(twiddles(tiles, width, 1.0, scale)),
        jnp.asarray(right_table(width, 1.0, 1.0)),
    )
    return psi_new, probe_new, tomo


def solution(mesh):
    in_specs = (
        P(None, "angle", None, "tile"),
        P(None, "angle", None, "tile"),
        P(),
        P("angle", "tile", None, None, None),
        P("angle", "tile", None),
        P("angle", "tile", None),
        P("angle", "tile"),
        P("angle"),
    )
    out_specs = (P(None, "angle", None, "tile"), P(), P(None, "tile", "angle", None))
    return jax.shard_map(shards, mesh=mesh, in_specs=in_specs, out_specs=out_specs, check_vma=False)
```

time: 731 us -> 116 us (0.16); the launches traced: 720 us -> 116 us
  matrix products: 260 us -> 0 us
  waiting for transfers between devices: 226 us -> 20.2 us
  local copies, waits for them, and re-layouts: 118 us -> 13.9 us
  blocking collectives: 56.5 us -> 23.8 us
  Pallas kernels: 0 us -> 26.9 us
  other arithmetic: 15.5 us -> 0 us
  between operations: 16.4 us -> 2.12 us
    dot_general x56 -> x0, matrix products: 260 us -> none  [the longest x13 65 us: twin_einsum(): jnp.einsum(pattern, left_imag, right_imag, precision=HIGHEST)]
    psum x2 -> x0, waiting for transfers between devices: 216 us -> none  [shards(): lax.psum((probe_part, local_count), ('angle', 'tile'))]
    gather x96 -> x0, local copies, waits for them, and re-layouts: 80.1 us -> none
    psum x1 -> x0, blocking collectives: 41.7 us -> none  [shards(): lax.psum((probe_part, local_count), ('angle', 'tile'))]
    pallas_call x0 -> x7, Pallas kernels: none -> 26.9 us  [the longest x1 11.2 us: shards(): call(functools.partial(inverse_kernel, depth), 'slab_image', shape(2, dep...]
    reshape x2 -> x0, local copies, waits for them, and re-layouts: 16.7 us -> none  [the longest x1 8.44 us: inverse_rows(): shaped_imag = values_imag.reshape(leading + (outer, inner))]
    all_to_all x0 -> x1, blocking collectives: none -> 16.2 us  [shards(): received = lax.all_to_all(sums, both, 0, 0, tiled=True)]
    mul x4 -> x0, local copies, waits for them, and re-layouts: 8.54 us -> none  [the longest x1 3.89 us: inverse_rows(): final_imag.reshape(leading + (inner * outer,)) * scale]
  transfers between devices with their start and end apart: 11 -> 9, of which waited for: 6 -> 5; matrix products, arithmetic and copies ran while one was open for 3% -> 0% of each run, Pallas kernels for 0% -> 10%
where the time goes in v1:
time: 116 us
  starting transfers between devices  29 us (25%)
  Pallas kernels  26.9 us (23%)
  blocking collectives  23.8 us (21%)
  waiting for transfers between devices  20.2 us (17%)
  local copies, waits for them, and re-layouts  13.9 us (12%)
  between operations  2.12 us (2%)
    all_to_all x1, blocking collectives, shards(): received = lax.all_to_all(sums, both, 0, 0, tiled=True)  16.2 us
    unnamed x45, local copies, waits for them, and re-layouts  13.9 us
    pallas_call x1, Pallas kernels, shards(): call(functools.partial(inverse_kernel, depth), 'slab_image', shape(2, dep...  11.2 us
    all_to_all x1, waiting for transfers between devices, shards(): slabs = lax.all_to_all(slabs, 'tile', 0, 0, tiled=True)  8.5 us
    all_gather x1, blocking collectives, shards(): spectra = lax.all_gather(spectrum, 'angle', axis=0, tiled=False)  7.63 us
    pallas_call x1, Pallas kernels, shards(): call(second_kernel, 'ptycho_second', [shape(tiles, 4 * depth + piece, wid...  7.07 us
    pallas_call x1, Pallas kernels, shards(): call(first_kernel, 'ptycho_first', [shape(*block)] * 4 + [shape(devices,...  6.27 us
    all_to_all x1, starting transfers between devices, shards(): slabs = lax.all_to_all(slabs, 'tile', 0, 0, tiled=True)  6.12 us
  transfers between devices with their start and end apart: 9, of which 5 were waited for; matrix products, arithmetic and copies ran while one was open for 0% of the time, Pallas kernels for 10%

profile of v1, /device:TPU:0, one launch (start us, length us, event | category | flops | bytes accessed | tf_op | source)
XLA Modules:
  0.0 116.0 jit_solution(4190480494105158411)
XLA Ops:
  0.6 4.9 %collective-permute-start = (f32[2,1,160,128]{3,2,1,0:T(8,128)}, f32[2,1,160,128]{3,2,1,0:T(8,128)S(1)}, u32[]{:S(2)}, u32[]{:S(2)}) collective-permute-start(f32[2,1,160,128]{3,2,1,0:T(8,128)} %psi.1), channel_id=1, source_target_pairs={{0,1},{1,2},{2,3},{3,4},{4,5},{5,6},{6,7},{8,9},{9,10},{10,11},{11... | collective-permute-start | bytes 491528 | tf_op jit(solution)/shard_map/ppermute | solution.py:425
  5.5 1.3 %collective-permute-start.1 = (f32[2,1,160,128]{3,2,1,0:T(8,128)}, f32[2,1,160,128]{3,2,1,0:T(8,128)S(1)}, u32[]{:S(2)}, u32[]{:S(2)}) collective-permute-start(f32[2,1,160,128]{3,2,1,0:T(8,128)} %psi.1), channel_id=1, source_target_pairs={{1,0},{2,1},{3,2},{4,3},{5,4},{6,5},{7,6},{9,8},{10,9},{11,10},{12... | collective-permute-start | bytes 491528 | tf_op jit(solution)/shard_map/ppermute | solution.py:426
  7.4 0.0 copy-start.9
  7.4 0.0 copy-start.11
  8.1 1.1 collective-permute-done.left
  9.2 4.0 %collective-permute-done.1.right = f32[2,1,160,128]{3,2,1,0:T(8,128)S(1)} collective-permute-done((f32[2,1,160,128]{3,2,1,0:T(8,128)}, f32[2,1,160,128]{3,2,1,0:T(8,128)S(1)}, u32[]{:S(2)}, u32[]{:S(2)}) %collective-permute-start.1) | collective-permute-done | bytes 163872 | tf_op jit(solution)/shard_map/ppermute | solution.py:426
  13.3 0.9 copy-done.1
  14.2 1.2 %copy-done.3 = f32[1,1,16,128,128]{4,3,2,1,0:T(8,128)S(1)} copy-done((f32[1,1,16,128,128]{4,3,2,1,0:T(8,128)S(1)}, f32[1,1,16,128,128]{4,3,2,1,0:T(8,128)}, u32[]{:S(2)}) %copy-start.3) | copy-done | bytes 1048600
  15.4 0.9 copy-done.5
  16.3 0.9 copy-done.6
  17.2 0.7 copy-done.8
  17.9 0.7 copy-done.10
  18.5 1.0 copy-done.13
  19.5 1.0 copy-done.15
  20.5 1.0 copy-done.17
  21.5 1.0 copy-done.19
  22.5 6.3 %ptycho_first.1 = (f32[2,160,128]{2,1,0:T(8,128)S(1)}, f32[2,160,128]{2,1,0:T(8,128)S(1)}, f32[2,160,128]{2,1,0:T(8,128)S(1)}, f32[2,160,128]{2,1,0:T(8,128)S(1)}, f32[32,16,128]{2,1,0:T(8,128)S(1)}) custom-call(s32[1,1,16]{2,1,0:T(1,128)S(1)} %copy-done.8, s32[1,1,16]{2,1,0:T(1,128)S(1)} %copy-done.10, s32[1,1]{1,0:T(1,128)S(6)} %copy.20.counts, ...), custom_call_target="tpu_custom_call" | custom-call | flops 3221225472 | tf_op jit(solution)/shard_map/ptycho_first/pallas_call | solution.py:428
  28.8 16.2 %all_to_all.20.received = f32[32,16,128]{2,1,0:T(8,128)S(1)} all-to-all(f32[32,16,128]{2,1,0:T(8,128)S(1)} %get-tuple-element.19), channel_id=1, replica_groups=mesh['angle'=4,'tile'=8] {'angle','tile'}, dimensions={0} | all-to-all | bytes 524288 | tf_op jit(solution)/shard_map/all_to_all | solution.py:438
  45.0 0.7 probe_chunk.1
  45.7 2.6 %all-to-all-start.1 = ((f32[32,8,128]{2,1,0:T(8,128)}), f32[32,8,128]{2,1,0:T(8,128)S(1)}, u32[]{:S(2)}, u32[]{:S(2)}) async-start(f32[32,8,128]{2,1,0:T(8,128)} %get-tuple-element.20), calls=%async_computation.1 | async-start | bytes 262144 | tf_op jit(solution)/shard_map/all_to_all | solution.py:445
  48.3 3.5 %collective-permute-start.2 = (f32[2,160,128]{2,1,0:T(8,128)S(1)}, f32[2,160,128]{2,1,0:T(8,128)S(1)}, u32[]{:S(2)}, u32[]{:S(2)}) collective-permute-start(f32[2,160,128]{2,1,0:T(8,128)S(1)} %get-tuple-element.17), channel_id=1, source_target_pairs={{0,1},{1,2},{2,3},{3,4},{4,5},{5,6},{6,7},{8,9},{9,10},{10,11},{11... | collective-permute-start | bytes 491528 | tf_op jit(solution)/shard_map/ppermute | solution.py:436
  51.9 1.3 %collective-permute-start.3 = (f32[2,160,128]{2,1,0:T(8,128)S(1)}, f32[2,160,128]{2,1,0:T(8,128)S(1)}, u32[]{:S(2)}, u32[]{:S(2)}) collective-permute-start(f32[2,160,128]{2,1,0:T(8,128)S(1)} %get-tuple-element.18), channel_id=1, source_target_pairs={{1,0},{2,1},{3,2},{4,3},{5,4},{6,5},{7,6},{9,8},{10,9},{11,10},{12... | collective-permute-start | bytes 491528 | tf_op jit(solution)/shard_map/ppermute | solution.py:437
  53.2 2.9 %collective-permute-done.2.left = f32[2,160,128]{2,1,0:T(8,128)S(1)} collective-permute-done((f32[2,160,128]{2,1,0:T(8,128)S(1)}, f32[2,160,128]{2,1,0:T(8,128)S(1)}, u32[]{:S(2)}, u32[]{:S(2)}) %collective-permute-start.2) | collective-permute-done | bytes 163872 | tf_op jit(solution)/shard_map/ppermute | solution.py:436
  56.1 3.6 %collective-permute-done.3.right = f32[2,160,128]{2,1,0:T(8,128)S(1)} collective-permute-done((f32[2,160,128]{2,1,0:T(8,128)S(1)}, f32[2,160,128]{2,1,0:T(8,128)S(1)}, u32[]{:S(2)}, u32[]{:S(2)}) %collective-permute-start.3) | collective-permute-done | bytes 163872 | tf_op jit(solution)/shard_map/ppermute | solution.py:437
  59.7 0.0 all-to-all-done.1
  59.7 0.0 copy-done.9
  59.8 0.0 copy-start.14
  59.8 1.0 copy-done.14
  60.8 1.0 copy-done.16
  61.8 1.0 copy-done.18
  62.8 1.0 copy-done.20
  63.8 7.1 %ptycho_second.1 = (f32[8,112,128]{2,1,0:T(8,128)}, f32[2,160,128]{2,1,0:T(8,128)S(1)}, f32[2,160,128]{2,1,0:T(8,128)S(1)}) custom-call(s32[1,1,16]{2,1,0:T(1,128)S(1)} %copy-done.9, s32[1,1,16]{2,1,0:T(1,128)S(1)} %copy-done.11, s32[1,1]{1,0:T(1,128)S(6)} %copy.20.counts, f32[2,160,128]{2,1,0:T(8,128)S(1)} %get-tuple-element.15.base, ...), custom_call_target="tpu_custom_call" | custom-call | flops 3221225472 | tf_op jit(solution)/shard_map/ptycho_second/pallas_call | solution.py:455
  70.8 6.1 %all-to-all-start.2 = ((f32[8,112,128]{2,1,0:T(8,128)}), f32[8,112,128]{2,1,0:T(8,128)S(1)}, u32[]{:S(2)}, u32[]{:S(2)}) async-start(f32[8,112,128]{2,1,0:T(8,128)} %get-tuple-element.21), calls=%async_computation.2 | async-start | bytes 917504 | tf_op jit(solution)/shard_map/all_to_all | solution.py:463
  77.0 0.0 copy-start.21
  77.0 1.4 %collective-permute-start.5 = (f32[2,160,128]{2,1,0:T(8,128)S(1)}, f32[2,160,128]{2,1,0:T(8,128)S(1)}, u32[]{:S(2)}, u32[]{:S(2)}) collective-permute-start(f32[2,160,128]{2,1,0:T(8,128)S(1)} %get-tuple-element.24), channel_id=1, source_target_pairs={{1,0},{2,1},{3,2},{4,3},{5,4},{6,5},{7,6},{9,8},{10,9},{11,10},{12... | collective-permute-start | bytes 491528 | tf_op jit(solution)/shard_map/ppermute | solution.py:465
  78.4 4.6 %collective-permute-start.4 = (f32[2,160,128]{2,1,0:T(8,128)S(1)}, f32[2,160,128]{2,1,0:T(8,128)S(1)}, u32[]{:S(2)}, u32[]{:S(2)}) collective-permute-start(f32[2,160,128]{2,1,0:T(8,128)S(1)} %get-tuple-element.24), channel_id=1, source_target_pairs={{0,1},{1,2},{2,3},{3,4},{4,5},{5,6},{6,7},{8,9},{9,10},{10,11},{11... | collective-permute-start | bytes 491528 | tf_op jit(solution)/shard_map/ppermute | solution.py:464
  83.0 8.5 %all-to-all-done.2.slabs = f32[8,112,128]{2,1,0:T(8,128)S(1)} async-done(((f32[8,112,128]{2,1,0:T(8,128)}), f32[8,112,128]{2,1,0:T(8,128)S(1)}, u32[]{:S(2)}, u32[]{:S(2)}) %all-to-all-start.2) | async-done | bytes 458784 | tf_op jit(solution)/shard_map/all_to_all | solution.py:463
  91.5 0.0 copy-done.2
  91.5 0.3 slab_spectrum.1
  91.7 7.6 %all-gather = f32[1408,128]{1,0:T(8,128)S(1)} all-gather(f32[352,128]{1,0:T(8,128)S(1)} %slab_spectrum.1), channel_id=2, replica_groups=mesh['angle'=4,'tile'=8] {'angle'}, dimensions={0}, use_global_device_ids=true | all-gather | bytes 901120 | tf_op jit(solution)/shard_map/all_gather | solution.py:474
  99.4 0.0 collective-permute-done.5.right
  99.4 0.0 collective-permute-done.4.left
  99.4 0.7 probe_last.1
  100.1 3.4 %all-to-all-start.3 = ((f32[8,32,128]{2,1,0:T(8,128)}), f32[8,32,128]{2,1,0:T(8,128)S(1)}, u32[]{:S(2)}, u32[]{:S(2)}) async-start(f32[8,32,128]{2,1,0:T(8,128)} %get-tuple-element.26), calls=%async_computation.3 | async-start | bytes 262144 | tf_op jit(solution)/shard_map/all_to_all | solution.py:481
  103.5 0.6 phase_table.1.phases
  104.2 11.2 %slab_image.1 = bf16[2,20,32,1024]{3,2,1,0:T(8,128)(2,1)} custom-call(f32[4,352,128]{2,1,0:T(8,128)S(1)} %bitcast.6, f32[4,2,8,32,128]{4,3,2,1,0:T(8,128)S(1)} %phase_table.1.phases, f32[2,8,128]{2,1,0:T(8,128)S(1)} %copy-done.21, bf16[768,256]{1,0:T(8,128)(2,1)S(1)} %copy-done.12), custom_call_target="tpu_custom_call" | custom-call | flops 2013265920 | tf_op jit(solution)/shard_map/slab_image/pallas_call | solution.py:483
  115.4 0.0 all-to-all-done.3
  115.4 0.7 copy.22
  (24 shorter events, 0.0 us)
Async XLA Ops:
  0.6 8.6 %collective-permute-start = (f32[2,1,160,128]{3,2,1,0:T(8,128)}, f32[2,1,160,128]{3,2,1,0:T(8,128)S(1)}, u32[]{:S(2)}, u32[]{:S(2)}) collective-permute-start(f32[2,1,160,128]{3,2,1,0:T(8,128)} %psi.1), channel_id=1, source_target_pairs={{0,1},{1,2},{2,3},{3,4},{4,5},{5,6},{6,7},{8,9},{9,10},{10,11},{11... | collective-permute-start | bytes 491528 | tf_op jit(solution)/shard_map/ppermute | solution.py:425
  5.5 7.8 %collective-permute-start.1 = (f32[2,1,160,128]{3,2,1,0:T(8,128)}, f32[2,1,160,128]{3,2,1,0:T(8,128)S(1)}, u32[]{:S(2)}, u32[]{:S(2)}) collective-permute-start(f32[2,1,160,128]{3,2,1,0:T(8,128)} %psi.1), channel_id=1, source_target_pairs={{1,0},{2,1},{3,2},{4,3},{5,4},{6,5},{7,6},{9,8},{10,9},{11,10},{12... | collective-permute-start | bytes 491528 | tf_op jit(solution)/shard_map/ppermute | solution.py:426
  7.4 52.3 %copy-start.9 = (s32[1,1,16]{2,1,0:T(1,128)S(1)}, s32[1,1,16]{2,1,0:T(1,128)}, u32[]{:S(2)}) copy-start(s32[1,1,16]{2,1,0:T(1,128)} %pos_z.3) | copy-start | bytes 196
  7.4 52.3 %copy-start.11 = (s32[1,1,16]{2,1,0:T(1,128)S(1)}, s32[1,1,16]{2,1,0:T(1,128)}, u32[]{:S(2)}) copy-start(s32[1,1,16]{2,1,0:T(1,128)} %pos_x.3) | copy-start | bytes 196
  13.3 0.9 copy-start.1
  14.2 1.2 %copy-start.3 = (f32[1,1,16,128,128]{4,3,2,1,0:T(8,128)S(1)}, f32[1,1,16,128,128]{4,3,2,1,0:T(8,128)}, u32[]{:S(2)}) copy-start(f32[1,1,16,128,128]{4,3,2,1,0:T(8,128)} %data.3) | copy-start | bytes 3145732
  15.4 0.9 copy-start.5
  16.3 0.9 copy-start.6
  17.2 0.7 copy-start.8
  17.9 0.7 copy-start.10
  18.5 1.0 copy-start.13
  19.5 1.0 copy-start.15
  20.5 1.0 copy-start.17
  21.5 1.0 copy-start.19
  22.5 37.2 %copy-start.4 = (f32[1,1,16,128,128]{4,3,2,1,0:T(8,128)S(1)}, f32[1,1,16,128,128]{4,3,2,1,0:T(8,128)}, u32[]{:S(2)}) copy-start(f32[1,1,16,128,128]{4,3,2,1,0:T(8,128)} %data.3) | copy-start | bytes 3145732
  22.5 37.2 %copy-start.7 = (f32[2,1,160,128]{3,2,1,0:T(8,128)S(1)}, f32[2,1,160,128]{3,2,1,0:T(8,128)}, u32[]{:S(2)}) copy-start(f32[2,1,160,128]{3,2,1,0:T(8,128)} %target.3) | copy-start | bytes 491524
  45.7 14.0 %all-to-all-start.1 = ((f32[32,8,128]{2,1,0:T(8,128)}), f32[32,8,128]{2,1,0:T(8,128)S(1)}, u32[]{:S(2)}, u32[]{:S(2)}) async-start(f32[32,8,128]{2,1,0:T(8,128)} %get-tuple-element.20), calls=%async_computation.1 | async-start | bytes 262144 | tf_op jit(solution)/shard_map/all_to_all | solution.py:445
  48.3 7.8 %collective-permute-start.2 = (f32[2,160,128]{2,1,0:T(8,128)S(1)}, f32[2,160,128]{2,1,0:T(8,128)S(1)}, u32[]{:S(2)}, u32[]{:S(2)}) collective-permute-start(f32[2,160,128]{2,1,0:T(8,128)S(1)} %get-tuple-element.17), channel_id=1, source_target_pairs={{0,1},{1,2},{2,3},{3,4},{4,5},{5,6},{6,7},{8,9},{9,10},{10,11},{11... | collective-permute-start | bytes 491528 | tf_op jit(solution)/shard_map/ppermute | solution.py:436
  51.9 7.9 %collective-permute-start.3 = (f32[2,160,128]{2,1,0:T(8,128)S(1)}, f32[2,160,128]{2,1,0:T(8,128)S(1)}, u32[]{:S(2)}, u32[]{:S(2)}) collective-permute-start(f32[2,160,128]{2,1,0:T(8,128)S(1)} %get-tuple-element.18), channel_id=1, source_target_pairs={{1,0},{2,1},{3,2},{4,3},{5,4},{6,5},{7,6},{9,8},{10,9},{11,10},{12... | collective-permute-start | bytes 491528 | tf_op jit(solution)/shard_map/ppermute | solution.py:437
  59.8 1.0 copy-start.14
  60.8 1.0 copy-start.16
  61.8 1.0 copy-start.18
  62.8 1.0 copy-start.20
  63.8 27.7 %copy-start = (bf16[768,256]{1,0:T(8,128)(2,1)S(1)}, bf16[768,256]{1,0:T(8,128)(2,1)}, u32[]{:S(2)}) copy-start(bf16[768,256]{1,0:T(8,128)(2,1)} %constant.21.clone.table) | copy-start | bytes 1179652
  63.8 27.7 %copy-start.2 = (f32[2,8,128]{2,1,0:T(8,128)S(1)}, f32[2,8,128]{2,1,0:T(8,128)}, u32[]{:S(2)}) copy-start(f32[2,8,128]{2,1,0:T(8,128)} %constant.20.clone.turn) | copy-start | bytes 24580
  70.8 20.6 %all-to-all-start.2 = ((f32[8,112,128]{2,1,0:T(8,128)}), f32[8,112,128]{2,1,0:T(8,128)S(1)}, u32[]{:S(2)}, u32[]{:S(2)}) async-start(f32[8,112,128]{2,1,0:T(8,128)} %get-tuple-element.21), calls=%async_computation.2 | async-start | bytes 917504 | tf_op jit(solution)/shard_map/all_to_all | solution.py:463
  76.9 27.2 %copy-start.12 = (bf16[768,256]{1,0:T(8,128)(2,1)S(1)}, bf16[768,256]{1,0:T(8,128)(2,1)}, u32[]{:S(2)}) copy-start(bf16[768,256]{1,0:T(8,128)(2,1)} %constant.23.clone.table) | copy-start | bytes 1179652
  77.0 27.2 %copy-start.21 = (f32[2,8,128]{2,1,0:T(8,128)S(1)}, f32[2,8,128]{2,1,0:T(8,128)}, u32[]{:S(2)}) copy-start(f32[2,8,128]{2,1,0:T(8,128)} %constant.22.clone.turn) | copy-start | bytes 24580
  77.0 22.4 %collective-permute-start.5 = (f32[2,160,128]{2,1,0:T(8,128)S(1)}, f32[2,160,128]{2,1,0:T(8,128)S(1)}, u32[]{:S(2)}, u32[]{:S(2)}) collective-permute-start(f32[2,160,128]{2,1,0:T(8,128)S(1)} %get-tuple-element.24), channel_id=1, source_target_pairs={{1,0},{2,1},{3,2},{4,3},{5,4},{6,5},{7,6},{9,8},{10,9},{11,10},{12... | collective-permute-start | bytes 491528 | tf_op jit(solution)/shard_map/ppermute | solution.py:465
  78.4 21.0 %collective-permute-start.4 = (f32[2,160,128]{2,1,0:T(8,128)S(1)}, f32[2,160,128]{2,1,0:T(8,128)S(1)}, u32[]{:S(2)}, u32[]{:S(2)}) collective-permute-start(f32[2,160,128]{2,1,0:T(8,128)S(1)} %get-tuple-element.24), channel_id=1, source_target_pairs={{0,1},{1,2},{2,3},{3,4},{4,5},{5,6},{6,7},{8,9},{9,10},{10,11},{11... | collective-permute-start | bytes 491528 | tf_op jit(solution)/shard_map/ppermute | solution.py:464
  100.1 15.2 %all-to-all-start.3 = ((f32[8,32,128]{2,1,0:T(8,128)}), f32[8,32,128]{2,1,0:T(8,128)S(1)}, u32[]{:S(2)}, u32[]{:S(2)}) async-start(f32[8,32,128]{2,1,0:T(8,128)} %get-tuple-element.26), calls=%async_computation.3 | async-start | bytes 262144 | tf_op jit(solution)/shard_map/all_to_all | solution.py:481

commit v2 on v1

v2 whole, which is shorter than its diff:
```python
import functools
import math

import jax
import jax.numpy as jnp
import ml_dtypes
import numpy as np
from jax import lax
from jax.experimental import pallas as pl
from jax.experimental.pallas import tpu as pltpu
from jax.sharding import PartitionSpec as P

ITERS = 2
ALPHA = 0.004
RHO = 5.0
PROBE_STEP = 0.02
GROUP = 4
VMEM_LIMIT = 40 * 1024 * 1024
BF16 = jnp.bfloat16
F32 = jnp.float32


def split_table(matrix, axis):
    high = matrix.astype(ml_dtypes.bfloat16)
    low = (matrix - high.astype(np.float64)).astype(ml_dtypes.bfloat16)
    return np.concatenate([high, high, low], axis)


def dft_parts(length, orient, scale):
    counter = np.arange(length)
    angle = 2.0 * math.pi / length * (np.outer(counter, counter) % length)
    return np.cos(angle) * scale, orient * np.sin(angle) * scale


def right_table(length, orient, scale):
    real, imag = dft_parts(length, orient, scale)
    return split_table(np.block([[real, imag], [-imag, real]]), 0)


def left_table(length, orient, scale):
    real, imag = dft_parts(length, orient, scale)
    matrix = np.block([[real, -imag], [imag, real]])
    high = matrix.astype(ml_dtypes.bfloat16)
    return np.concatenate([high, (matrix - high.astype(np.float64)).astype(ml_dtypes.bfloat16)], 0)


def twiddles(tiles, inner, orient, scale):
    angle = 2.0 * math.pi / (tiles * inner) * np.outer(np.arange(tiles), np.arange(inner))
    return np.stack([np.cos(angle) * scale, orient * np.sin(angle) * scale]).astype(np.float32)


def halves(value):
    high = value.astype(BF16)
    low = (value - high.astype(F32)).astype(BF16)
    return high, low


def dot(left, right):
    return jnp.dot(left, right, preferred_element_type=F32)


def tall(table, high, low):
    size = high.shape[0]
    both = dot(table[...], high)
    return both[:size] + both[size:] + dot(table[0:size], low)


def butterfly(parts, orient):
    count = len(parts)
    if count == 1:
        return parts
    even = butterfly(parts[0::2], orient)
    odd = butterfly(parts[1::2], orient)
    low, high = [], []
    for index in range(count // 2):
        angle = orient * 2.0 * math.pi * index / count
        real, imag = odd[index]
        if index == 0:
            turned = (real, imag)
        elif 4 * index == count:
            turned = (-imag, real) if orient > 0 else (imag, -real)
        else:
            cosine, sine = math.cos(angle), math.sin(angle)
            turned = (real * cosine - imag * sine, real * sine + imag * cosine)
        base_real, base_imag = even[index]
        low.append((base_real + turned[0], base_imag + turned[1]))
        high.append((base_real - turned[0], base_imag - turned[1]))
    return low + high


def lane_mask(shape, half):
    return lax.broadcasted_iota(jnp.int32, shape, len(shape) - 1) < half


def side_by_side(stages, count, group):
    groups = count // group
    held = [None] * groups
    for turn in range(groups + len(stages) - 1):
        for number in reversed(range(len(stages))):
            at = turn - number
            if 0 <= at < groups:
                held[at] = stages[number](at * group, held[at])


def slot_loop(pos_z, pos_x, count, probe_real, probe_imag, data, tables, own, halo, work):
    right_fwd, left_fwd, left_inv, right_inv = tables
    grad_own, grad_halo, grad_probe, patches = work
    side = data.shape[-1]
    half = side // 2
    slots = data.shape[2]
    group = math.gcd(slots, GROUP)
    wide = math.gcd(group, 2)
    lanes = lax.broadcasted_iota(jnp.int32, (side, side), 1)
    grad_own[...] = jnp.zeros_like(grad_own)
    grad_halo[...] = jnp.zeros_like(grad_halo)
    grad_probe[...] = jnp.zeros_like(grad_probe)

    def place(slot):
        start = pos_x[0, 0, slot] - half
        back = jnp.where(start > 0, side - start, -start)
        forth = jnp.where(start < 0, side + start, start)
        inside = (lanes >= start) & (lanes < side + start)
        return pl.ds(pos_z[0, 0, slot], side), back, forth, inside

    def cut_out(first, _):
        waves = []
        for slot in range(first, first + group):
            where, back, _, inside = place(slot)
            cut = []
            for part in range(2):
                mixed = jnp.where(inside, own[part, where, :], halo[part, where, :])
                cut.append(pltpu.roll(mixed, back, 1))
                patches[slot, part] = cut[part]
            waves.append(
                jnp.concatenate(
                    [
                        probe_real[...] * cut[0] - probe_imag[...] * cut[1],
                        probe_real[...] * cut[1] + probe_imag[...] * cut[0],
                    ],
                    1,
                )
            )
        return halves(jnp.concatenate(waves, 0))

    def rows_forward(first, split):
        high, low = split
        rows = dot(jnp.concatenate([high, low, high], 1), right_fwd[...])
        stacks = []
        for at in range(0, group, wide):
            some = [rows[(at + k) * side : (at + k + 1) * side] for k in range(wide)]
            stacked = jnp.concatenate(
                [
                    jnp.concatenate([block[:, :side] for block in some], 1),
                    jnp.concatenate([block[:, side:] for block in some], 1),
                ],
                0,
            )
            stacks.append(halves(stacked))
        return stacks

    def columns_forward(first, stacks):
        results = []
        for index, (high, low) in enumerate(stacks):
            far = tall(left_fwd, high, low)
            weights = []
            for k in range(wide):
                slot = first + index * wide + k
                live = jnp.where(slot < count, 1.0, 0.0).astype(F32)
                far_real = far[:side, k * side : (k + 1) * side]
                far_imag = far[side:, k * side : (k + 1) * side]
                weights.append((far_real * far_real + far_imag * far_imag - data[0, 0, slot]) * live)
            weight = jnp.concatenate(weights, 1)
            results.append(halves(jnp.concatenate([far[:side] * weight, far[side:] * weight], 0)))
        return results

    def columns_inverse(first, stacks):
        blocks = []
        for high, low in stacks:
            back_cols = tall(left_inv, high, low)
            for k in range(wide):
                block = back_cols[:, k * side : (k + 1) * side]
                blocks.append(jnp.concatenate([block[:side], block[side:]], 1))
        return halves(jnp.concatenate(blocks, 0))

    def rows_inverse(first, split):
        high, low = split
        return dot(jnp.concatenate([high, low, high], 1), right_inv[...])

    def add_back(first, chi):
        sum_real, sum_imag = grad_probe[0], grad_probe[1]
        for member in range(group):
            slot = first + member
            where, _, forth, inside = place(slot)
            chi_real = chi[member * side : (member + 1) * side, :side]
            chi_imag = chi[member * side : (member + 1) * side, side:]
            cut_real, cut_imag = patches[slot, 0], patches[slot, 1]
            sum_real = sum_real + (cut_real * chi_real + cut_imag * chi_imag)
            sum_imag = sum_imag + (cut_real * chi_imag - cut_imag * chi_real)
            grads = (
                probe_real[...] * chi_real + probe_imag[...] * chi_imag,
                probe_real[...] * chi_imag - probe_imag[...] * chi_real,
            )
            for part in range(2):
                moved = pltpu.roll(grads[part], forth, 1)
                grad_own[part, where, :] += jnp.where(inside, moved, 0.0)
                grad_halo[part, where, :] += jnp.where(inside, 0.0, moved)
        grad_probe[0], grad_probe[1] = sum_real, sum_imag

    side_by_side(
        [cut_out, rows_forward, columns_forward, columns_inverse, rows_inverse, add_back], slots, group
    )


def stage_kernel(*refs):
    count = (len(refs) - 1) // 2
    copies = [
        pltpu.make_async_copy(refs[index], refs[count + index], refs[-1].at[index])
        for index in range(count)
    ]
    for copy in copies:
        copy.start()
    for copy in copies:
        copy.wait()


def sides(partner, other, part, even):
    first, second = partner[part], other[part]
    return jnp.where(even, second, first), jnp.where(even, first, second)


def is_even():
    return lax.axis_index("tile") % 2 == 0


def load_places(sources, targets, sems):
    copies = [
        pltpu.make_async_copy(source, target, sems.at[index])
        for index, (source, target) in enumerate(zip(sources, targets))
    ]
    for copy in copies:
        copy.start()
    return copies


def fold(kept, turned, mask):
    return jnp.where(mask, kept, pltpu.roll(turned, mask.shape[-1] // 2, 1))


def pack_kernel(psi, to_partner, to_other, held, sems):
    copies = [pltpu.make_async_copy(psi.at[part, 0], held.at[part], sems.at[part]) for part in range(2)]
    for copy in copies:
        copy.start()
    mask = lane_mask(to_partner.shape, to_partner.shape[-1] // 2)
    even = is_even()
    for copy in copies:
        copy.wait()
    to_left = fold(held[0], held[1], mask)
    to_right = fold(held[0], held[1], ~mask)
    to_partner[...] = jnp.where(even, to_right, to_left)
    to_other[...] = jnp.where(even, to_left, to_right)


def unfold(low_source, high_source, mask):
    real = jnp.where(mask, low_source, high_source)
    imag = pltpu.roll(jnp.where(mask, high_source, low_source), mask.shape[-1] // 2, 1)
    return real, imag


def packed_sides(partner, other, even):
    first, second = partner[...], other[...]
    return jnp.where(even, second, first), jnp.where(even, first, second)


def first_kernel(
    pos_z, pos_x, counts, shears, psi, target, partner, other, probe, data, *rest
):
    tables = rest[:4]
    to_partner, to_other, base_out, rim_out, keep_out, send_out = rest[4:10]
    held, sems, halo, work = rest[10:12], rest[12], rest[13], rest[14:]
    copies = load_places((pos_z, pos_x), held, sems)
    pos_z, pos_x = held
    grad_own, grad_halo, grad_probe = work[:3]
    side = data.shape[-1]
    mask = lane_mask(psi.shape[2:], side // 2)
    even = is_even()
    left, right = packed_sides(partner, other, even)
    halo[0], halo[1] = unfold(right, left, mask)
    for copy in copies:
        copy.wait()
    count = counts[0, 0]
    slot_loop(
        pos_z, pos_x, count, probe.at[0], probe.at[1], data, tables, psi.at[:, 0], halo, work
    )
    for part in range(2):
        field = psi[part, 0]
        base = field - ALPHA * (grad_own[part] + RHO * (field - target[part, 0]))
        rim = -ALPHA * grad_halo[part]
        base_out[part] = base
        rim_out[part] = rim
        to_right, to_left = jnp.where(mask, rim, base), jnp.where(mask, base, rim)
        to_partner[part] = jnp.where(even, to_right, to_left)
        to_other[part] = jnp.where(even, to_left, to_right)
    row = lax.broadcasted_iota(jnp.int32, (8, side), 0)
    lane = lax.broadcasted_iota(jnp.int32, (8, side), 1)
    angle, tile = lax.axis_index("angle"), lax.axis_index("tile")
    mine = (row == 1) & (lane == angle) & (tile == 0)
    extra = jnp.where(row == 0, count.astype(F32), jnp.where(mine, shears[0], 0.0))
    core = angle % 2
    for out, part in ((keep_out, core), (send_out, 1 - core)):
        out[0:side] = grad_probe[part]
        out[side : side + 8] = extra


def sum_kernel(*refs):
    terms = [ref[...] for ref in refs[:-1]]
    while len(terms) > 1:
        terms = [terms[at] + terms[at + 1] for at in range(0, len(terms), 2)]
    refs[-1][...] = terms[0]


def probe_kernel(probe, *refs):
    total, probe_out, extra_out = refs[-1], refs[-3], refs[-2]
    sum_kernel(*refs[:-3], total)
    side = probe.shape[-1]
    extra = total[side : side + 8]
    part = lax.axis_index("angle") % 2
    probe_out[...] = probe[part] - PROBE_STEP * total[0:side] / extra[0:1]
    extra_out[...] = extra


def second_kernel(
    pos_z, pos_x, counts, base, rim, partner, other, target, probe_mine, probe_theirs, data, *rest
):
    tables = rest[:4]
    slabs_out, base_out, to_partner, to_other, probe = rest[5:10]
    held, sems, own, halo, hold, edge, work = rest[10:12], *rest[12:17], rest[17:]
    copies = load_places((pos_z, pos_x), held, sems)
    pos_z, pos_x = held
    grad_own, grad_halo, grad_probe = work[:3]
    side = data.shape[-1]
    mask = lane_mask(base.shape[1:], side // 2)
    tile, tiles = lax.axis_index("tile"), lax.axis_size("tile")
    from_right = jnp.where(tile < tiles - 1, 1.0, 0.0).astype(F32)
    from_left = jnp.where(tile > 0, 1.0, 0.0).astype(F32)
    core = lax.axis_index("angle") % 2
    probe[core] = probe_mine[...]
    probe[1 - core] = probe_theirs[...]
    even = is_even()
    for part in range(2):
        left, right = sides(partner, other, part, even)
        own[part] = base[part] + jnp.where(mask, left, right)
        halo[part] = jnp.where(
            mask, (right + rim[part]) * from_right, (left + rim[part]) * from_left
        )
    for copy in copies:
        copy.wait()
    slot_loop(
        pos_z, pos_x, counts[0, 0], probe.at[0], probe.at[1], data, tables, own, halo, work
    )
    slabs, depth = slabs_out.shape[0], base.shape[1] // slabs_out.shape[0]
    chunk = slabs_out.shape[1] - 4 * depth
    for part in range(2):
        field = own[part]
        aim = target[part, 0]
        updated = field - ALPHA * (grad_own[part] + RHO * (field - aim))
        edge[part] = -ALPHA * grad_halo[part]
        base_out[part] = updated
        hold[part] = aim - updated
    to_right = fold(edge[0], edge[1], mask)
    to_left = fold(edge[0], edge[1], ~mask)
    to_partner[...] = jnp.where(even, to_right, to_left)
    to_other[...] = jnp.where(even, to_left, to_right)
    per_part = side // chunk
    for slab in range(slabs):
        rows = pl.ds(slab * depth, depth)
        for part in range(2):
            slabs_out[slab, part * depth : (part + 1) * depth] = hold[part, rows]
            slabs_out[slab, (2 + part) * depth : (3 + part) * depth] = edge[part, rows]
        part, place = slab // per_part, slab % per_part
        slabs_out[slab, 4 * depth : 4 * depth + chunk] = grad_probe[
            part, place * chunk : (place + 1) * chunk
        ]


def forward_kernel(slabs, turn, table, spectrum_out, rows_scratch):
    tiles, height, width = slabs.shape
    depth = rows_scratch.shape[0] // tiles
    chunk = height - 4 * depth
    mask = lane_mask((depth, width), width // 2)
    blocks = []
    for tile in range(tiles):
        block = []
        for part in range(2):
            rows = slice((2 + part) * depth, (3 + part) * depth)
            zero = jnp.zeros((depth, width), F32)
            before = slabs[tile - 1, rows] if tile > 0 else zero
            after = slabs[tile + 1, rows] if tile < tiles - 1 else zero
            block.append(
                slabs[tile, part * depth : (part + 1) * depth] - jnp.where(mask, before, after)
            )
        blocks.append(tuple(block))
    for index, (real, imag) in enumerate(butterfly(blocks, -1)):
        cosine, sine = turn[0, index : index + 1], turn[1, index : index + 1]
        rows = slice(index * depth, (index + 1) * depth)
        rows_scratch[rows, :width] = real * cosine - imag * sine
        rows_scratch[rows, width:] = real * sine + imag * cosine
    high, low = halves(rows_scratch[...])
    spectrum = dot(jnp.concatenate([high, low, high], 1), table[...])
    count = rows_scratch.shape[0]
    spectrum_out[0:count] = spectrum[:, :width]
    spectrum_out[count : 2 * count] = spectrum[:, width:]
    total = slabs[0, 4 * depth : 4 * depth + chunk]
    for tile in range(1, tiles):
        total = total + slabs[tile, 4 * depth : 4 * depth + chunk]
    spectrum_out[2 * count : 2 * count + chunk] = total


def phase_kernel(tiles, extra, table_out):
    angles, _, _, beam, width = table_out.shape
    total = tiles * width
    first = lax.axis_index("angle") * beam - (beam * lax.axis_size("angle")) // 2
    offsets = (lax.broadcasted_iota(jnp.int32, (beam, width), 0) + first).astype(F32)
    column = lax.broadcasted_iota(jnp.int32, (beam, width), 1)
    for angle in range(angles):
        shear = extra[1:2, angle : angle + 1]
        for block in range(tiles):
            frequency = block + tiles * column
            signed = jnp.where(frequency < total // 2, frequency, frequency - total).astype(F32)
            turns = (offsets * signed * shear) * (1.0 / total)
            turns = turns - jnp.floor(turns + 0.5)
            x = turns * math.pi
            square = x * x
            sine = x * (
                1.0 + square * (-1 / 6 + square * (1 / 120 + square * (-1 / 5040 + square * (
                    1 / 362880 + square * (-1 / 39916800 + square * (1.0 / 6227020800.0))))))
            )
            cosine = 1.0 + square * (-1 / 2 + square * (1 / 24 + square * (-1 / 720 + square * (
                1 / 40320 + square * (-1 / 3628800 + square * (1.0 / 479001600.0))))))
            table_out[angle, 0, block] = 1.0 - 2.0 * sine * sine
            table_out[angle, 1, block] = 2.0 * sine * cosine


def inverse_kernel(depth, spectra, phases, turn, table, image_out):
    angles, _, tiles, beam, width = phases.shape
    group = image_out.shape[1]
    wide = math.gcd(group, 2)
    first = pl.program_id(0) * group
    count = tiles * depth

    def sum_angles(start, _):
        rows = [[] for _ in range(wide)]
        for block in range(tiles):
            cosines = [phases[angle, 0, block] for angle in range(angles)]
            sines = [phases[angle, 1, block] for angle in range(angles)]
            for member in range(wide):
                real = imag = None
                for angle in range(angles):
                    at = block * depth + first + start + member
                    spec_real = spectra[angle, pl.ds(at, 1), :]
                    spec_imag = spectra[angle, pl.ds(count + at, 1), :]
                    add_real = cosines[angle] * spec_real - sines[angle] * spec_imag
                    add_imag = cosines[angle] * spec_imag + sines[angle] * spec_real
                    real = add_real if angle == 0 else real + add_real
                    imag = add_imag if angle == 0 else imag + add_imag
                rows[member].append(jnp.concatenate([real, imag], 1))
        return [halves(jnp.concatenate(blocks, 0)) for blocks in rows]

    def transform(start, splits):
        return [dot(jnp.concatenate([high, low, high], 1), table[...]) for high, low in splits]

    def finish(start, images):
        for member, image in enumerate(images):
            blocks = []
            for block in range(tiles):
                real = image[block * beam : (block + 1) * beam, :width]
                imag = image[block * beam : (block + 1) * beam, width:]
                cosine, sine = turn[0, block : block + 1], turn[1, block : block + 1]
                blocks.append((real * cosine - imag * sine, real * sine + imag * cosine))
            for index, (real, imag) in enumerate(butterfly(blocks, 1)):
                columns = slice(index * width, (index + 1) * width)
                image_out[0, start + member, :, columns] = real.astype(BF16)
                image_out[1, start + member, :, columns] = imag.astype(BF16)

    side_by_side([sum_angles, transform, finish], group, wide)


def last_kernel(probe_rows, spectra, probe, extra, base, partner, other, chunk_out, psi_out):
    angles, tiles, rows = spectra.shape[0], chunk_out.shape[0], chunk_out.shape[1]
    total = spectra[0, probe_rows : probe_rows + rows]
    for angle in range(1, angles):
        total = total + spectra[angle, probe_rows : probe_rows + rows]
    tile = lax.axis_index("tile")
    mine = probe[pl.ds(tile, 1)][0] - PROBE_STEP * total / extra[0:1]
    for place in range(tiles):
        chunk_out[place] = mine
    mask = lane_mask(base.shape[1:], base.shape[-1] // 2)
    even = is_even()
    left, right = packed_sides(partner, other, even)
    real, imag = unfold(left, right, mask)
    psi_out[0, 0] = base[0] + real
    psi_out[1, 0] = base[1] + imag


VMEM = pl.BlockSpec(memory_space=pltpu.VMEM)
SMEM = pl.BlockSpec(memory_space=pltpu.SMEM)
HBM = pl.BlockSpec(memory_space=pltpu.HBM)
ANY = pl.BlockSpec(memory_space=pl.ANY)


def call(body, name, out_shape, in_specs, scratch=(), flops=0, size=0, **more):
    return pl.pallas_call(
        body,
        name=name,
        out_shape=out_shape,
        in_specs=in_specs,
        scratch_shapes=list(scratch),
        compiler_params=pltpu.CompilerParams(vmem_limit_bytes=VMEM_LIMIT),
        cost_estimate=pl.CostEstimate(flops=flops, bytes_accessed=size, transcendentals=0),
        **more,
    )


def shape(*dims, dtype=F32):
    return jax.ShapeDtypeStruct(dims, dtype)


def exchange(to_partner, to_other, tiles):
    def pairs(start):
        low = range(start, tiles - 1, 2)
        return [(i, i + 1) for i in low] + [(i + 1, i) for i in low]

    return (
        lax.ppermute(to_partner, "tile", pairs(0)),
        lax.ppermute(to_other, "tile", pairs(1)),
    )


def swap(array, mask, devices):
    return lax.ppermute(array, ("angle", "tile"), [(i, i ^ mask) for i in range(devices)])


def hypercube(angles, tiles):
    bits = [tiles << at for at in range(1, angles.bit_length() - 1)]
    bits += [1 << at for at in range(tiles.bit_length() - 1)]
    rounds = []
    while bits:
        two, bits = bits[:2], bits[2:]
        rounds.append(two if len(two) == 1 else [two[0], two[1], two[0] ^ two[1]])
    return rounds


def shards(psi, target, probe, data, pos_z, pos_x, counts, shears):
    rows_total, width = psi.shape[2], psi.shape[3]
    side = probe.shape[1]
    angles, tiles = lax.axis_size("angle"), lax.axis_size("tile")
    devices = angles * tiles
    depth = rows_total // tiles
    beam = 32
    norm = 1.0 / math.sqrt(side)
    tables = [
        jnp.asarray(right_table(side, -1.0, norm)),
        jnp.asarray(left_table(side, -1.0, norm)),
        jnp.asarray(left_table(side, 1.0, norm)),
        jnp.asarray(right_table(side, 1.0, norm)),
    ]
    block = (2, rows_total, width)
    work = [
        pltpu.VMEM(block, F32),
        pltpu.VMEM(block, F32),
        pltpu.VMEM((2, side, side), F32),
        pltpu.VMEM((data.shape[2], 2, side, side), F32),
    ]
    slots = data.shape[2]
    flops = slots * 4 * 2 * side * 6 * side * 2 * side
    slot_places = [pltpu.with_memory_space_constraint(x, pltpu.HBM) for x in (pos_z, pos_x)]
    places = [pltpu.SMEM(x.shape, x.dtype) for x in slot_places] + [pltpu.SemaphoreType.DMA((2,))]
    psi = pltpu.with_memory_space_constraint(psi, pltpu.HBM)
    flat = shape(rows_total, width)
    to_partner, to_other = call(
        pack_kernel,
        "psi_pack",
        [flat] * 2,
        [HBM],
        [pltpu.VMEM(block, F32), pltpu.SemaphoreType.DMA((2,))],
    )(psi)
    partner, other = exchange(to_partner, to_other, tiles)
    operands = [
        pltpu.with_memory_space_constraint(x, pltpu.HBM)
        for x in [psi, target, probe, data] + tables
    ]
    psi_in, target_in, probe_in, data_in, *tables = call(
        stage_kernel,
        "stage_operands",
        [pltpu.VMEM(x.shape, x.dtype) for x in operands],
        [HBM] * len(operands),
        [pltpu.SemaphoreType.DMA((len(operands),))],
        0,
        3_000_000,
        out_specs=[VMEM] * len(operands),
    )(*operands)
    target_in, data_in, *tables = [
        pltpu.with_memory_space_constraint(x, pltpu.VMEM) for x in [target_in, data_in] + tables
    ]
    half = shape(side + 8, side)
    to_partner, to_other, base, rim, keep, send = call(
        first_kernel,
        "ptycho_first",
        [shape(*block)] * 4 + [half] * 2,
        [HBM] * 2 + [SMEM] * 2 + [VMEM] * 10,
        places + [pltpu.VMEM(block, F32)] + work,
        flops,
    )(*slot_places, counts, shears, psi_in, target_in, partner, other, probe_in, data_in, *tables)
    rounds = hypercube(angles, tiles)
    total = call(sum_kernel, "probe_sum", half, [VMEM] * 2)(keep, swap(send, tiles, devices))
    for masks in rounds[:-1]:
        terms = [total] + [swap(total, mask, devices) for mask in masks]
        total = call(sum_kernel, "probe_sum", half, [VMEM] * len(terms))(*terms)
    partner, other = exchange(to_partner, to_other, tiles)
    terms = [total] + [swap(total, mask, devices) for mask in rounds[-1]]
    probe_mine, extra = call(
        probe_kernel,
        "probe_step",
        [shape(side, side), shape(8, side)],
        [VMEM] * (1 + len(terms)),
        [pltpu.VMEM((side + 8, side), F32)],
    )(probe_in, *terms)
    probe_theirs = swap(probe_mine, tiles, devices)
    phases = call(
        functools.partial(phase_kernel, tiles),
        "phase_table",
        shape(angles, 2, tiles, beam, width),
        [VMEM],
        (),
        angles * tiles * beam * width * 40,
    )(extra)
    piece = 2 * side // tiles
    slabs, base, to_partner, to_other, probe_one = call(
        second_kernel,
        "ptycho_second",
        [shape(tiles, 4 * depth + piece, width), shape(*block), flat, flat, shape(2, side, side)],
        [HBM] * 2 + [SMEM] + [VMEM] * 12 + [ANY],
        places + [pltpu.VMEM(block, F32)] * 4 + work,
        flops,
    )(
        *(*slot_places, counts, base, rim, partner, other, target_in),
        *(probe_mine, probe_theirs, data_in, *tables, phases),
    )
    slabs = lax.all_to_all(slabs, "tile", 0, 0, tiled=True)
    partner, other = exchange(to_partner, to_other, tiles)
    count = tiles * depth
    spectrum = call(
        forward_kernel,
        "slab_spectrum",
        shape(2 * count + piece, width),
        [VMEM] * 3,
        [pltpu.VMEM((count, 2 * width), F32)],
    )(slabs, jnp.asarray(twiddles(tiles, width, -1.0, 1.0)), jnp.asarray(right_table(width, -1.0, 1.0)))
    spectra = lax.all_gather(spectrum, "angle", axis=0, tiled=False)
    chunks, psi_new = call(
        functools.partial(last_kernel, 2 * count),
        "probe_last",
        [shape(tiles, piece, side), shape(2, 1, rows_total, width)],
        [VMEM] * 6,
    )(spectra, probe_one.reshape(tiles, piece, side), extra, base, partner, other)
    probe_new = lax.all_to_all(chunks, "tile", 0, 0, tiled=True).reshape(2, side, side)
    scale = 1.0 / (angles * tiles * width)
    group = max(size for size in (1, 2, 4, 10) if depth % size == 0)
    tomo = call(
        functools.partial(inverse_kernel, depth),
        "slab_image",
        shape(2, depth, beam, tiles * width, dtype=BF16),
        [VMEM] * 4,
        [],
        depth * tiles * beam * 2 * 6 * width * 2 * width,
        grid=(depth // group,),
        out_specs=pl.BlockSpec((2, group, beam, tiles * width), lambda row: (0, row, 0, 0)),
    )(
        spectra,
        phases,
        jnp.asarray(twiddles(tiles, width, 1.0, scale)),
        jnp.asarray(right_table(width, 1.0, 1.0)),
    )
    return psi_new, probe_new, tomo


def solution(mesh):
    in_specs = (
        P(None, "angle", None, "tile"),
        P(None, "angle", None, "tile"),
        P(),
        P("angle", "tile", None, None, None),
        P("angle", "tile", None),
        P("angle", "tile", None),
        P("angle", "tile"),
        P("angle"),
    )
    out_specs = (P(None, "angle", None, "tile"), P(), P(None, "tile", "angle", None))
    return jax.shard_map(shards, mesh=mesh, in_specs=in_specs, out_specs=out_specs, check_vma=False)
```

time: 116 us -> 86.1 us (0.74)
  blocking collectives: 23.8 us -> 8.25 us
  local copies, waits for them, and re-layouts: 13.9 us -> 0.68 us
  Pallas kernels: 26.9 us -> 23.6 us
  waiting for transfers between devices: 20.2 us -> 23.4 us
  starting transfers between devices: 29 us -> 27.6 us
    all_to_all x1 -> x0, blocking collectives: 16.2 us -> none  [shards(): received = lax.all_to_all(sums, both, 0, 0, tiled=True)]
    unnamed x45 -> x9, local copies, waits for them, and re-layouts: 13.9 us -> 0.68 us
    pallas_call x1, Pallas kernels: 11.2 us -> 6.58 us  [shards(): call(functools.partial(inverse_kernel, depth), 'slab_image', shape(2, dep...]
    all_to_all x1, waiting for transfers between devices: 8.5 us -> 11.6 us  [shards(): slabs = lax.all_to_all(slabs, 'tile', 0, 0, tiled=True)]
    ppermute x6 -> x14, starting transfers between devices: 17 us -> 19.7 us  [the longest x8 10.9 us: swap(): lax.ppermute(array, ('angle', 'tile'), [(i, i ^ mask) for i in range(devi...]
    all_to_all x1 -> x0, starting transfers between devices: 2.58 us -> none  [shards(): lax.all_to_all(chunks, both, 0, 0, tiled=True).reshape(2, side, side)]
    all_to_all x1, starting transfers between devices: 6.12 us -> 4.27 us  [shards(): slabs = lax.all_to_all(slabs, 'tile', 0, 0, tiled=True)]
    pallas_call x2 -> x6, Pallas kernels: 6.98 us -> 8.75 us  [the longest x1 5.77 us: shards(): call(first_kernel, 'ptycho_first', [shape(*block)] * 4 + [half] * 2, [HBM...]
  transfers between devices with their start and end apart: 9 -> 16, of which waited for: 5 -> 7; matrix products, arithmetic and copies ran while one was open for 0% -> 0% of each run, Pallas kernels for 10% -> 11%
where the time goes in v2:
time: 86.1 us; the launch traced here: 85.6 us
  starting transfers between devices  27.6 us (32%)
  Pallas kernels  23.6 us (27%)
  waiting for transfers between devices  23.4 us (27%)
  blocking collectives  8.25 us (10%)
  between operations  2.11 us (2%)
    all_to_all x1, waiting for transfers between devices, shards(): slabs = lax.all_to_all(slabs, 'tile', 0, 0, tiled=True)  11.6 us
    ppermute x8, starting transfers between devices, swap(): lax.ppermute(array, ('angle', 'tile'), [(i, i ^ mask) for i in range(devi...  10.9 us
    ppermute x8, waiting for transfers between devices, swap(): lax.ppermute(array, ('angle', 'tile'), [(i, i ^ mask) for i in range(devi...  10.9 us
    all_gather x1, blocking collectives, shards(): spectra = lax.all_gather(spectrum, 'angle', axis=0, tiled=False)  8.25 us
    ppermute x3, starting transfers between devices, exchange(): lax.ppermute(to_partner, 'tile', pairs(0))  6.9 us
    pallas_call x1, Pallas kernels, shards(): call(second_kernel, 'ptycho_second', [shape(tiles, 4 * depth + piece, wid...  6.58 us
    pallas_call x1, Pallas kernels, shards(): call(functools.partial(inverse_kernel, depth), 'slab_image', shape(2, dep...  6.58 us
    pallas_call x1, Pallas kernels, shards(): call(first_kernel, 'ptycho_first', [shape(*block)] * 4 + [half] * 2, [HBM...  5.77 us
  transfers between devices with their start and end apart: 16, of which 7 were waited for; matrix products, arithmetic and copies ran while one was open for 0% of the time, Pallas kernels for 11%

profile of v2, /device:TPU:0, one launch (start us, length us, event | category | flops | bytes accessed | tf_op | source)
XLA Modules:
  0.0 85.6 jit_solution(13706281498828129041)
XLA Ops:
  0.6 1.0 %psi_pack.1 = (f32[160,128]{1,0:T(8,128)S(1)}, f32[160,128]{1,0:T(8,128)S(1)}) custom-call(f32[2,1,160,128]{3,2,1,0:T(8,128)} %psi.1), custom_call_target="tpu_custom_call" | custom-call | tf_op jit(solution)/shard_map/psi_pack/pallas_call | solution.py:579
  1.7 3.0 %collective-permute-start = (f32[160,128]{1,0:T(8,128)S(1)}, f32[160,128]{1,0:T(8,128)S(1)}, u32[]{:S(2)}, u32[]{:S(2)}) collective-permute-start(f32[160,128]{1,0:T(8,128)S(1)} %get-tuple-element.30), channel_id=1, source_target_pairs={{0,1},{2,3},{4,5},{6,7},{1,0},{3,2},{5,4},{7,6},{8,9},{10,11},{12,... | collective-permute-start | bytes 245768 | tf_op jit(solution)/shard_map/ppermute | solution.py:533
  4.7 0.7 collective-permute-start.1
  6.6 1.9 %stage_operands.1 = (f32[2,1,160,128]{3,2,1,0:T(8,128)S(1)}, f32[2,1,160,128]{3,2,1,0:T(8,128)S(1)}, f32[2,128,128]{2,1,0:T(8,128)S(1)}, f32[1,1,16,128,128]{4,3...) custom-call(f32[2,1,160,128]{3,2,1,0:T(8,128)} %psi.1, ...), custom_call_target="tpu_custom_call" | custom-call | bytes 3000000 | tf_op jit(solution)/shard_map/stage_operands/pallas_call | solution.py:591
  8.5 0.0 collective-permute-done.partner
  8.5 0.0 collective-permute-done.1.other
  8.6 5.8 %ptycho_first.1 = (f32[2,160,128]{2,1,0:T(8,128)S(1)}, f32[2,160,128]{2,1,0:T(8,128)S(1)}, f32[2,160,128]{2,1,0:T(8,128)S(1)}, f32[2,160,128]{2,1,0:T(8,128)S(1)...) custom-call(s32[1,1,16]{2,1,0:T(1,128)} %pos_z.3, s32[1,1,16]{2,1,0:T(1,128)} %pos_x.3, s32[1,1]{1,0:T(1,128)S(6)} %copy.20.counts, ...), custom_call_target="tpu_custom_call" | custom-call | flops 3221225472 | tf_op jit(solution)/shard_map/ptycho_first/pallas_call | solution.py:605
  14.3 0.1 collective-permute-start.4
  14.4 1.2 %collective-permute-done.4.refs_1_ = f32[136,128]{1,0:T(8,128)S(1)} collective-permute-done((f32[136,128]{1,0:T(8,128)S(1)}, f32[136,128]{1,0:T(8,128)S(1)}, u32[]{:S(2)}, u32[]{:S(2)}) %collective-permute-start.4) | collective-permute-done | bytes 69664 | tf_op jit(solution)/shard_map/ppermute | solution.py:539
  15.7 5.3 %collective-permute-start.7 = (f32[136,128]{1,0:T(8,128)S(1)}, f32[136,128]{1,0:T(8,128)S(1)}, u32[]{:S(2)}, u32[]{:S(2)}) collective-permute-start(f32[136,128]{1,0:T(8,128)S(1)} %probe_sum.2.refs_0_), channel_id=1, source_target_pairs={{0,17},{1,16},{2,19},{3,18},{4,21},{5,20},{6,23},{7,22},{8,25},{9,... | collective-permute-start | bytes 208904 | tf_op jit(solution)/shard_map/ppermute | solution.py:539
  20.9 0.0 collective-permute-start.6
  21.0 0.6 collective-permute-start.5
  21.6 1.9 %collective-permute-start.2 = (f32[2,160,128]{2,1,0:T(8,128)S(1)}, f32[2,160,128]{2,1,0:T(8,128)S(1)}, u32[]{:S(2)}, u32[]{:S(2)}) collective-permute-start(f32[2,160,128]{2,1,0:T(8,128)S(1)} %get-tuple-element.40), channel_id=1, source_target_pairs={{0,1},{2,3},{4,5},{6,7},{1,0},{3,2},{5,4},{7,6},{8,9},{10,11},{12,... | collective-permute-start | bytes 491528 | tf_op jit(solution)/shard_map/ppermute | solution.py:533
  23.5 0.7 collective-permute-start.3
  24.1 0.0 collective-permute-done.7.refs_3_
  24.1 1.9 %collective-permute-done.6.refs_2_ = f32[136,128]{1,0:T(8,128)S(1)} collective-permute-done((f32[136,128]{1,0:T(8,128)S(1)}, f32[136,128]{1,0:T(8,128)S(1)}, u32[]{:S(2)}, u32[]{:S(2)}) %collective-permute-start.6) | collective-permute-done | bytes 69664 | tf_op jit(solution)/shard_map/ppermute | solution.py:539
  26.0 0.0 collective-permute-done.5.refs_1_
  26.0 4.2 %collective-permute-start.10 = (f32[136,128]{1,0:T(8,128)S(1)}, f32[136,128]{1,0:T(8,128)S(1)}, u32[]{:S(2)}, u32[]{:S(2)}) collective-permute-start(f32[136,128]{1,0:T(8,128)S(1)} %probe_sum.3.refs_0_), channel_id=1, source_target_pairs={{0,6},{1,7},{2,4},{3,5},{4,2},{5,3},{6,0},{7,1},{8,14},{9,15},{10,... | collective-permute-start | bytes 208904 | tf_op jit(solution)/shard_map/ppermute | solution.py:539
  30.2 0.0 collective-permute-start.9
  30.2 0.6 collective-permute-start.8
  30.9 5.3 %collective-permute-done.10.refs_3_ = f32[136,128]{1,0:T(8,128)S(1)} collective-permute-done((f32[136,128]{1,0:T(8,128)S(1)}, f32[136,128]{1,0:T(8,128)S(1)}, u32[]{:S(2)}, u32[]{:S(2)}) %collective-permute-start.10) | collective-permute-done | bytes 69664 | tf_op jit(solution)/shard_map/ppermute | solution.py:539
  36.2 1.9 %collective-permute-done.9.refs_2_ = f32[136,128]{1,0:T(8,128)S(1)} collective-permute-done((f32[136,128]{1,0:T(8,128)S(1)}, f32[136,128]{1,0:T(8,128)S(1)}, u32[]{:S(2)}, u32[]{:S(2)}) %collective-permute-start.9) | collective-permute-done | bytes 69664 | tf_op jit(solution)/shard_map/ppermute | solution.py:539
  38.1 0.0 collective-permute-done.8.refs_1_
  38.1 0.1 collective-permute-start.11
  38.2 0.7 phase_table.1.rest_4_.phases
  38.8 0.0 collective-permute-done.2.partner
  38.9 0.0 collective-permute-done.3.other
  38.9 0.5 collective-permute-done.11.probe_theirs
  39.4 6.6 %ptycho_second.1 = (f32[8,112,128]{2,1,0:T(8,128)}, f32[2,160,128]{2,1,0:T(8,128)S(1)}, f32[160,128]{1,0:T(8,128)S(1)}, f32[160,128]{1,0:T(8,128)S(1)}, f32[2,128,128]{2,1,0:T(8,128)S(1)}) custom-call(s32[1,1,16]{2,1,0:T(1,128)} %pos_z.3, s32[1,1,16]{2,1,0:T(1,128)} %pos_x.3, s32[1,1]{1,0:T(1,128)S(6)} %copy.20.counts, ...), custom_call_target="tpu_custom_call" | custom-call | flops 3221225472 | tf_op jit(solution)/shard_map/ptycho_second/pallas_call | solution.py:637
  46.0 0.0 copy-start.2
  46.0 0.0 copy-start.3
  46.0 4.3 %all-to-all-start = ((f32[8,112,128]{2,1,0:T(8,128)}), f32[8,112,128]{2,1,0:T(8,128)S(1)}, u32[]{:S(2)}, u32[]{:S(2)}) async-start(f32[8,112,128]{2,1,0:T(8,128)} %get-tuple-element.46), calls=%async_computation | async-start | bytes 917504 | tf_op jit(solution)/shard_map/all_to_all | solution.py:648
  50.3 2.0 %collective-permute-start.12 = (f32[160,128]{1,0:T(8,128)S(1)}, f32[160,128]{1,0:T(8,128)S(1)}, u32[]{:S(2)}, u32[]{:S(2)}) collective-permute-start(f32[160,128]{1,0:T(8,128)S(1)} %get-tuple-element.49), channel_id=1, source_target_pairs={{0,1},{2,3},{4,5},{6,7},{1,0},{3,2},{5,4},{7,6},{8,9},{10,11},{12,... | collective-permute-start | bytes 245768 | tf_op jit(solution)/shard_map/ppermute | solution.py:533
  52.3 0.7 collective-permute-start.13
  53.0 11.6 %all-to-all-done.slabs = f32[8,112,128]{2,1,0:T(8,128)S(1)} async-done(((f32[8,112,128]{2,1,0:T(8,128)}), f32[8,112,128]{2,1,0:T(8,128)S(1)}, u32[]{:S(2)}, u32[]{:S(2)}) %all-to-all-start) | async-done | bytes 458784 | tf_op jit(solution)/shard_map/all_to_all | solution.py:648
  64.6 0.0 copy-done
  64.6 0.0 copy-done.1
  64.6 0.3 slab_spectrum.1
  64.9 8.3 %all-gather = f32[1408,128]{1,0:T(8,128)S(1)} all-gather(f32[352,128]{1,0:T(8,128)S(1)} %slab_spectrum.1), channel_id=2, replica_groups=mesh['angle'=4,'tile'=8] {'angle'}, dimensions={0}, use_global_device_ids=true | all-gather | bytes 901120 | tf_op jit(solution)/shard_map/all_gather | solution.py:658
  73.1 0.0 collective-permute-done.12.partner
  73.1 0.0 collective-permute-done.13.other
  73.1 0.8 probe_last.1
  73.9 3.6 %all-to-all-start.1 = ((f32[8,32,128]{2,1,0:T(8,128)}), f32[8,32,128]{2,1,0:T(8,128)S(1)}, u32[]{:S(2)}, u32[]{:S(2)}) async-start(f32[8,32,128]{2,1,0:T(8,128)} %get-tuple-element.52), calls=%async_computation.1 | async-start | bytes 262144 | tf_op jit(solution)/shard_map/all_to_all | solution.py:665
  77.5 0.0 copy-done.2
  77.5 0.0 copy-done.3
  77.5 6.6 %slab_image.1 = bf16[2,20,32,1024]{3,2,1,0:T(8,128)(2,1)} custom-call(f32[4,352,128]{2,1,0:T(8,128)S(1)} %bitcast.4, f32[4,2,8,32,128]{4,3,2,1,0:T(8,128)S(1)} %phase_table.1.rest_4_.phases, f32[2,8,128]{2,1,0:T(8,128)S(1)} %copy-done.3, bf16[768,256]{1,0:T(8,128)(2,1)S(1)} %copy-done.2), custom_call_target="tpu_custom_call" | custom-call | flops 2013265920 | tf_op jit(solution)/shard_map/slab_image/pallas_call | solution.py:668
  84.1 0.9 %all-to-all-done.1 = f32[8,32,128]{2,1,0:T(8,128)S(1)} async-done(((f32[8,32,128]{2,1,0:T(8,128)}), f32[8,32,128]{2,1,0:T(8,128)S(1)}, u32[]{:S(2)}, u32[]{:S(2)}) %all-to-all-start.1) | async-done | bytes 131104 | tf_op jit(solution)/shard_map/all_to_all | solution.py:665
  85.0 0.7 copy.22
  (5 shorter events, 0.1 us)
Async XLA Ops:
  1.7 6.9 %collective-permute-start = (f32[160,128]{1,0:T(8,128)S(1)}, f32[160,128]{1,0:T(8,128)S(1)}, u32[]{:S(2)}, u32[]{:S(2)}) collective-permute-start(f32[160,128]{1,0:T(8,128)S(1)} %get-tuple-element.30), channel_id=1, source_target_pairs={{0,1},{2,3},{4,5},{6,7},{1,0},{3,2},{5,4},{7,6},{8,9},{10,11},{12,... | collective-permute-start | bytes 245768 | tf_op jit(solution)/shard_map/ppermute | solution.py:533
  4.7 3.9 %collective-permute-start.1 = (f32[160,128]{1,0:T(8,128)S(1)}, f32[160,128]{1,0:T(8,128)S(1)}, u32[]{:S(2)}, u32[]{:S(2)}) collective-permute-start(f32[160,128]{1,0:T(8,128)S(1)} %get-tuple-element.31), channel_id=1, source_target_pairs={{1,2},{3,4},{5,6},{2,1},{4,3},{6,5},{9,10},{11,12},{13,14},{10,9},... | collective-permute-start | bytes 245768 | tf_op jit(solution)/shard_map/ppermute | solution.py:534
  14.3 1.3 %collective-permute-start.4 = (f32[136,128]{1,0:T(8,128)S(1)}, f32[136,128]{1,0:T(8,128)S(1)}, u32[]{:S(2)}, u32[]{:S(2)}) collective-permute-start(f32[136,128]{1,0:T(8,128)S(1)} %get-tuple-element.43), channel_id=1, source_target_pairs={{0,8},{1,9},{2,10},{3,11},{4,12},{5,13},{6,14},{7,15},{8,0},{9,1},... | collective-permute-start | bytes 208904 | tf_op jit(solution)/shard_map/ppermute | solution.py:539
  15.7 8.5 %collective-permute-start.7 = (f32[136,128]{1,0:T(8,128)S(1)}, f32[136,128]{1,0:T(8,128)S(1)}, u32[]{:S(2)}, u32[]{:S(2)}) collective-permute-start(f32[136,128]{1,0:T(8,128)S(1)} %probe_sum.2.refs_0_), channel_id=1, source_target_pairs={{0,17},{1,16},{2,19},{3,18},{4,21},{5,20},{6,23},{7,22},{8,25},{9,... | collective-permute-start | bytes 208904 | tf_op jit(solution)/shard_map/ppermute | solution.py:539
  20.9 5.1 %collective-permute-start.6 = (f32[136,128]{1,0:T(8,128)S(1)}, f32[136,128]{1,0:T(8,128)S(1)}, u32[]{:S(2)}, u32[]{:S(2)}) collective-permute-start(f32[136,128]{1,0:T(8,128)S(1)} %probe_sum.2.refs_0_), channel_id=1, source_target_pairs={{0,1},{1,0},{2,3},{3,2},{4,5},{5,4},{6,7},{7,6},{8,9},{9,8},{10,11... | collective-permute-start | bytes 208904 | tf_op jit(solution)/shard_map/ppermute | solution.py:539
  21.0 5.1 %collective-permute-start.5 = (f32[136,128]{1,0:T(8,128)S(1)}, f32[136,128]{1,0:T(8,128)S(1)}, u32[]{:S(2)}, u32[]{:S(2)}) collective-permute-start(f32[136,128]{1,0:T(8,128)S(1)} %probe_sum.2.refs_0_), channel_id=1, source_target_pairs={{0,16},{1,17},{2,18},{3,19},{4,20},{5,21},{6,22},{7,23},{8,24},{9,... | collective-permute-start | bytes 208904 | tf_op jit(solution)/shard_map/ppermute | solution.py:539
  21.6 17.3 %collective-permute-start.2 = (f32[2,160,128]{2,1,0:T(8,128)S(1)}, f32[2,160,128]{2,1,0:T(8,128)S(1)}, u32[]{:S(2)}, u32[]{:S(2)}) collective-permute-start(f32[2,160,128]{2,1,0:T(8,128)S(1)} %get-tuple-element.40), channel_id=1, source_target_pairs={{0,1},{2,3},{4,5},{6,7},{1,0},{3,2},{5,4},{7,6},{8,9},{10,11},{12,... | collective-permute-start | bytes 491528 | tf_op jit(solution)/shard_map/ppermute | solution.py:533
  23.5 15.4 %collective-permute-start.3 = (f32[2,160,128]{2,1,0:T(8,128)S(1)}, f32[2,160,128]{2,1,0:T(8,128)S(1)}, u32[]{:S(2)}, u32[]{:S(2)}) collective-permute-start(f32[2,160,128]{2,1,0:T(8,128)S(1)} %get-tuple-element.41), channel_id=1, source_target_pairs={{1,2},{3,4},{5,6},{2,1},{4,3},{6,5},{9,10},{11,12},{13,14},{10,9},... | collective-permute-start | bytes 491528 | tf_op jit(solution)/shard_map/ppermute | solution.py:534
  26.0 10.1 %collective-permute-start.10 = (f32[136,128]{1,0:T(8,128)S(1)}, f32[136,128]{1,0:T(8,128)S(1)}, u32[]{:S(2)}, u32[]{:S(2)}) collective-permute-start(f32[136,128]{1,0:T(8,128)S(1)} %probe_sum.3.refs_0_), channel_id=1, source_target_pairs={{0,6},{1,7},{2,4},{3,5},{4,2},{5,3},{6,0},{7,1},{8,14},{9,15},{10,... | collective-permute-start | bytes 208904 | tf_op jit(solution)/shard_map/ppermute | solution.py:539
  30.2 7.8 %collective-permute-start.9 = (f32[136,128]{1,0:T(8,128)S(1)}, f32[136,128]{1,0:T(8,128)S(1)}, u32[]{:S(2)}, u32[]{:S(2)}) collective-permute-start(f32[136,128]{1,0:T(8,128)S(1)} %probe_sum.3.refs_0_), channel_id=1, source_target_pairs={{0,4},{1,5},{2,6},{3,7},{4,0},{5,1},{6,2},{7,3},{8,12},{9,13},{10,... | collective-permute-start | bytes 208904 | tf_op jit(solution)/shard_map/ppermute | solution.py:539
  30.2 7.8 %collective-permute-start.8 = (f32[136,128]{1,0:T(8,128)S(1)}, f32[136,128]{1,0:T(8,128)S(1)}, u32[]{:S(2)}, u32[]{:S(2)}) collective-permute-start(f32[136,128]{1,0:T(8,128)S(1)} %probe_sum.3.refs_0_), channel_id=1, source_target_pairs={{0,2},{1,3},{2,0},{3,1},{4,6},{5,7},{6,4},{7,5},{8,10},{9,11},{10,... | collective-permute-start | bytes 208904 | tf_op jit(solution)/shard_map/ppermute | solution.py:539
  38.1 1.3 %collective-permute-start.11 = (f32[128,128]{1,0:T(8,128)S(1)}, f32[128,128]{1,0:T(8,128)S(1)}, u32[]{:S(2)}, u32[]{:S(2)}) collective-permute-start(f32[128,128]{1,0:T(8,128)S(1)} %get-tuple-element.44.probe_mine), channel_id=1, source_target_pairs={{0,8},{1,9},{2,10},{3,11},{4,12},{5,13},{6,14},{7,15},{8,0},{9,1},... | collective-permute-start | bytes 196616 | tf_op jit(solution)/shard_map/ppermute | solution.py:539
  39.4 25.2 %copy-start = (bf16[768,256]{1,0:T(8,128)(2,1)S(1)}, bf16[768,256]{1,0:T(8,128)(2,1)}, u32[]{:S(2)}) copy-start(bf16[768,256]{1,0:T(8,128)(2,1)} %constant.21.clone.table) | copy-start | bytes 1179652
  39.4 25.2 %copy-start.1 = (f32[2,8,128]{2,1,0:T(8,128)S(1)}, f32[2,8,128]{2,1,0:T(8,128)}, u32[]{:S(2)}) copy-start(f32[2,8,128]{2,1,0:T(8,128)} %constant.20.clone.turn) | copy-start | bytes 24580
  46.0 31.4 %copy-start.2 = (bf16[768,256]{1,0:T(8,128)(2,1)S(1)}, bf16[768,256]{1,0:T(8,128)(2,1)}, u32[]{:S(2)}) copy-start(bf16[768,256]{1,0:T(8,128)(2,1)} %constant.23.clone.table) | copy-start | bytes 1179652
  46.0 31.4 %copy-start.3 = (f32[2,8,128]{2,1,0:T(8,128)S(1)}, f32[2,8,128]{2,1,0:T(8,128)}, u32[]{:S(2)}) copy-start(f32[2,8,128]{2,1,0:T(8,128)} %constant.22.clone.turn) | copy-start | bytes 24580
  46.0 18.6 %all-to-all-start = ((f32[8,112,128]{2,1,0:T(8,128)}), f32[8,112,128]{2,1,0:T(8,128)S(1)}, u32[]{:S(2)}, u32[]{:S(2)}) async-start(f32[8,112,128]{2,1,0:T(8,128)} %get-tuple-element.46), calls=%async_computation | async-start | bytes 917504 | tf_op jit(solution)/shard_map/all_to_all | solution.py:648
  50.3 22.8 %collective-permute-start.12 = (f32[160,128]{1,0:T(8,128)S(1)}, f32[160,128]{1,0:T(8,128)S(1)}, u32[]{:S(2)}, u32[]{:S(2)}) collective-permute-start(f32[160,128]{1,0:T(8,128)S(1)} %get-tuple-element.49), channel_id=1, source_target_pairs={{0,1},{2,3},{4,5},{6,7},{1,0},{3,2},{5,4},{7,6},{8,9},{10,11},{12,... | collective-permute-start | bytes 245768 | tf_op jit(solution)/shard_map/ppermute | solution.py:533
  52.3 20.8 %collective-permute-start.13 = (f32[160,128]{1,0:T(8,128)S(1)}, f32[160,128]{1,0:T(8,128)S(1)}, u32[]{:S(2)}, u32[]{:S(2)}) collective-permute-start(f32[160,128]{1,0:T(8,128)S(1)} %get-tuple-element.50), channel_id=1, source_target_pairs={{1,2},{3,4},{5,6},{2,1},{4,3},{6,5},{9,10},{11,12},{13,14},{10,9},... | collective-permute-start | bytes 245768 | tf_op jit(solution)/shard_map/ppermute | solution.py:534
  73.9 11.1 %all-to-all-start.1 = ((f32[8,32,128]{2,1,0:T(8,128)}), f32[8,32,128]{2,1,0:T(8,128)S(1)}, u32[]{:S(2)}, u32[]{:S(2)}) async-start(f32[8,32,128]{2,1,0:T(8,128)} %get-tuple-element.52), calls=%async_computation.1 | async-start | bytes 262144 | tf_op jit(solution)/shard_map/all_to_all | solution.py:665

commit v3 on v2

--- a/solution.py
+++ b/solution.py
@@ -328,12 +328,18 @@
     extra_out[...] = extra
 
 
+def last_probe_kernel(probe_mine, extra, *refs):
+    total, probe_out = refs[-1], refs[-2]
+    sum_kernel(*refs[:-2], total)
+    probe_out[...] = probe_mine[...] - PROBE_STEP * total[...] / extra[0:1]
+
+
 def second_kernel(
     pos_z, pos_x, counts, base, rim, partner, other, target, probe_mine, probe_theirs, data, *rest
 ):
     tables = rest[:4]
-    slabs_out, base_out, to_partner, to_other, probe = rest[5:10]
-    held, sems, own, halo, hold, edge, work = rest[10:12], *rest[12:17], rest[17:]
+    slabs_out, base_out, to_partner, to_other, keep_out, send_out = rest[5:11]
+    held, sems, own, halo, hold, edge, probe, work = rest[11:13], *rest[13:19], rest[19:]
     copies = load_places((pos_z, pos_x), held, sems)
     pos_z, pos_x = held
     grad_own, grad_halo, grad_probe = work[:3]
@@ -358,7 +364,6 @@
         pos_z, pos_x, counts[0, 0], probe.at[0], probe.at[1], data, tables, own, halo, work
     )
     slabs, depth = slabs_out.shape[0], base.shape[1] // slabs_out.shape[0]
-    chunk = slabs_out.shape[1] - 4 * depth
     for part in range(2):
         field = own[part]
         aim = target[part, 0]
@@ -370,22 +375,19 @@
     to_left = fold(edge[0], edge[1], ~mask)
     to_partner[...] = jnp.where(even, to_right, to_left)
     to_other[...] = jnp.where(even, to_left, to_right)
-    per_part = side // chunk
+    keep_out[...] = grad_probe[core]
+    send_out[...] = grad_probe[1 - core]
     for slab in range(slabs):
         rows = pl.ds(slab * depth, depth)
         for part in range(2):
             slabs_out[slab, part * depth : (part + 1) * depth] = hold[part, rows]
             slabs_out[slab, (2 + part) * depth : (3 + part) * depth] = edge[part, rows]
-        part, place = slab // per_part, slab % per_part
-        slabs_out[slab, 4 * depth : 4 * depth + chunk] = grad_probe[
-            part, place * chunk : (place + 1) * chunk
-        ]
-
-
-def forward_kernel(slabs, turn, table, spectrum_out, rows_scratch):
-    tiles, height, width = slabs.shape
+
+
+def forward_kernel(slabs, turn, table, *rest):
+    spectrum_out, rows_scratch = rest[-2:]
+    tiles, _, width = slabs.shape
     depth = rows_scratch.shape[0] // tiles
-    chunk = height - 4 * depth
     mask = lane_mask((depth, width), width // 2)
     blocks = []
     for tile in range(tiles):
@@ -409,10 +411,6 @@
     count = rows_scratch.shape[0]
     spectrum_out[0:count] = spectrum[:, :width]
     spectrum_out[count : 2 * count] = spectrum[:, width:]
-    total = slabs[0, 4 * depth : 4 * depth + chunk]
-    for tile in range(1, tiles):
-        total = total + slabs[tile, 4 * depth : 4 * depth + chunk]
-    spectrum_out[2 * count : 2 * count + chunk] = total
 
 
 def phase_kernel(tiles, extra, table_out):
@@ -440,8 +438,11 @@
             table_out[angle, 1, block] = 2.0 * sine * cosine
 
 
-def inverse_kernel(depth, spectra, phases, turn, table, image_out):
-    angles, _, tiles, beam, width = phases.shape
+def inverse_kernel(depth, masks, phases, turn, table, *rest):
+    spectra, image_out, token = rest[: len(masks)], rest[-2], rest[-1]
+    token[...] = jnp.zeros_like(token)
+    _, _, tiles, beam, width = phases.shape
+    angles = [lax.axis_index("angle") ^ mask for mask in masks]
     group = image_out.shape[1]
     wide = math.gcd(group, 2)
     first = pl.program_id(0) * group
@@ -450,18 +451,18 @@
     def sum_angles(start, _):
         rows = [[] for _ in range(wide)]
         for block in range(tiles):
-            cosines = [phases[angle, 0, block] for angle in range(angles)]
-            sines = [phases[angle, 1, block] for angle in range(angles)]
+            cosines = [phases[angle, 0, block] for angle in angles]
+            sines = [phases[angle, 1, block] for angle in angles]
             for member in range(wide):
                 real = imag = None
-                for angle in range(angles):
+                for spectrum, cosine, sine in zip(spectra, cosines, sines):
                     at = block * depth + first + start + member
-                    spec_real = spectra[angle, pl.ds(at, 1), :]
-                    spec_imag = spectra[angle, pl.ds(count + at, 1), :]
-                    add_real = cosines[angle] * spec_real - sines[angle] * spec_imag
-                    add_imag = cosines[angle] * spec_imag + sines[angle] * spec_real
-                    real = add_real if angle == 0 else real + add_real
-                    imag = add_imag if angle == 0 else imag + add_imag
+                    spec_real = spectrum[pl.ds(at, 1), :]
+                    spec_imag = spectrum[pl.ds(count + at, 1), :]
+                    add_real = cosine * spec_real - sine * spec_imag
+                    add_imag = cosine * spec_imag + sine * spec_real
+                    real = add_real if real is None else real + add_real
+                    imag = add_imag if imag is None else imag + add_imag
                 rows[member].append(jnp.concatenate([real, imag], 1))
         return [halves(jnp.concatenate(blocks, 0)) for blocks in rows]
 
@@ -484,21 +485,15 @@
     side_by_side([sum_angles, transform, finish], group, wide)
 
 
-def last_kernel(probe_rows, spectra, probe, extra, base, partner, other, chunk_out, psi_out):
-    angles, tiles, rows = spectra.shape[0], chunk_out.shape[0], chunk_out.shape[1]
-    total = spectra[0, probe_rows : probe_rows + rows]
-    for angle in range(1, angles):
-        total = total + spectra[angle, probe_rows : probe_rows + rows]
-    tile = lax.axis_index("tile")
-    mine = probe[pl.ds(tile, 1)][0] - PROBE_STEP * total / extra[0:1]
-    for place in range(tiles):
-        chunk_out[place] = mine
+def finish_kernel(base, partner, other, probe_mine, probe_theirs, _, psi_out, probe_out):
     mask = lane_mask(base.shape[1:], base.shape[-1] // 2)
-    even = is_even()
-    left, right = packed_sides(partner, other, even)
+    left, right = packed_sides(partner, other, is_even())
     real, imag = unfold(left, right, mask)
     psi_out[0, 0] = base[0] + real
     psi_out[1, 0] = base[1] + imag
+    core = lax.axis_index("angle") % 2
+    probe_out[core] = probe_mine[...]
+    probe_out[1 - core] = probe_theirs[...]
 
 
 VMEM = pl.BlockSpec(memory_space=pltpu.VMEM)
@@ -611,12 +606,20 @@
         flops,
     )(*slot_places, counts, shears, psi_in, target_in, partner, other, probe_in, data_in, *tables)
     rounds = hypercube(angles, tiles)
-    total = call(sum_kernel, "probe_sum", half, [VMEM] * 2)(keep, swap(send, tiles, devices))
-    for masks in rounds[:-1]:
-        terms = [total] + [swap(total, mask, devices) for mask in masks]
-        total = call(sum_kernel, "probe_sum", half, [VMEM] * len(terms))(*terms)
+
+    def all_but_last(keep, send, rounds):
+        piece = shape(*keep.shape)
+        total = call(sum_kernel, "probe_sum", piece, [VMEM] * 2)(keep, swap(send, tiles, devices))
+        for masks in rounds[:-1]:
+            terms = [total] + [swap(total, mask, devices) for mask in masks]
+            total = call(sum_kernel, "probe_sum", piece, [VMEM] * len(terms))(*terms)
+        return total
+
+    def last_round(total, rounds):
+        return [total] + [swap(total, mask, devices) for mask in rounds[-1]]
+
+    terms = last_round(all_but_last(keep, send, rounds), rounds)
     partner, other = exchange(to_partner, to_other, tiles)
-    terms = [total] + [swap(total, mask, devices) for mask in rounds[-1]]
     probe_mine, extra = call(
         probe_kernel,
         "probe_step",
@@ -633,53 +636,79 @@
         (),
         angles * tiles * beam * width * 40,
     )(extra)
-    piece = 2 * side // tiles
-    slabs, base, to_partner, to_other, probe_one = call(
+    slabs, base, to_partner, to_other, keep, send = call(
         second_kernel,
         "ptycho_second",
-        [shape(tiles, 4 * depth + piece, width), shape(*block), flat, flat, shape(2, side, side)],
+        [shape(tiles, 4 * depth, width), shape(*block), flat, flat] + [shape(side, side)] * 2,
         [HBM] * 2 + [SMEM] + [VMEM] * 12 + [ANY],
-        places + [pltpu.VMEM(block, F32)] * 4 + work,
+        places + [pltpu.VMEM(block, F32)] * 4 + [pltpu.VMEM((2, side, side), F32)] + work,
         flops,
     )(
         *(*slot_places, counts, base, rim, partner, other, target_in),
         *(probe_mine, probe_theirs, data_in, *tables, phases),
     )
     slabs = lax.all_to_all(slabs, "tile", 0, 0, tiled=True)
-    partner, other = exchange(to_partner, to_other, tiles)
+    total = all_but_last(keep, send, rounds)
+    late = total
+    for mask in rounds[-1][: 1 if len(rounds[-1]) > 1 else 0]:
+        late = call(sum_kernel, "probe_sum", shape(*late.shape), [VMEM] * 2)(
+            late, swap(late, mask, devices)
+        )
     count = tiles * depth
     spectrum = call(
         forward_kernel,
         "slab_spectrum",
-        shape(2 * count + piece, width),
-        [VMEM] * 3,
+        shape(2 * count, width),
+        [VMEM] * 3 + [ANY],
         [pltpu.VMEM((count, 2 * width), F32)],
-    )(slabs, jnp.asarray(twiddles(tiles, width, -1.0, 1.0)), jnp.asarray(right_table(width, -1.0, 1.0)))
-    spectra = lax.all_gather(spectrum, "angle", axis=0, tiled=False)
-    chunks, psi_new = call(
-        functools.partial(last_kernel, 2 * count),
+    )(
+        slabs,
+        jnp.asarray(twiddles(tiles, width, -1.0, 1.0)),
+        jnp.asarray(right_table(width, -1.0, 1.0)),
+        total,
+    )
+    masks = list(range(angles))
+    spectra = [spectrum] + [swap(spectrum, mask * tiles, devices) for mask in masks[1:]]
+    late, spectra[1], to_partner, to_other = lax.optimization_barrier(
+        (late, spectra[1], to_partner, to_other)
+    )
+    terms = [late, swap(late, rounds[-1][min(1, len(rounds[-1]) - 1)], devices)]
+    partner, other = exchange(to_partner, to_other, tiles)
+    probe_mine = call(
+        last_probe_kernel,
         "probe_last",
-        [shape(tiles, piece, side), shape(2, 1, rows_total, width)],
-        [VMEM] * 6,
-    )(spectra, probe_one.reshape(tiles, piece, side), extra, base, partner, other)
-    probe_new = lax.all_to_all(chunks, "tile", 0, 0, tiled=True).reshape(2, side, side)
+        shape(side, side),
+        [VMEM] * (2 + len(terms)),
+        [pltpu.VMEM((side, side), F32)],
+    )(probe_mine, extra, *terms)
+    probe_theirs = swap(probe_mine, tiles, devices)
     scale = 1.0 / (angles * tiles * width)
     group = max(size for size in (1, 2, 4, 10) if depth % size == 0)
-    tomo = call(
-        functools.partial(inverse_kernel, depth),
+    tomo, token = call(
+        functools.partial(inverse_kernel, depth, masks),
         "slab_image",
-        shape(2, depth, beam, tiles * width, dtype=BF16),
-        [VMEM] * 4,
+        [shape(2, depth, beam, tiles * width, dtype=BF16), shape(8, width)],
+        [VMEM] * (3 + angles) + [ANY],
         [],
         depth * tiles * beam * 2 * 6 * width * 2 * width,
         grid=(depth // group,),
-        out_specs=pl.BlockSpec((2, group, beam, tiles * width), lambda row: (0, row, 0, 0)),
+        out_specs=[
+            pl.BlockSpec((2, group, beam, tiles * width), lambda row: (0, row, 0, 0)),
+            pl.BlockSpec((8, width), lambda row: (0, 0)),
+        ],
     )(
-        spectra,
         phases,
         jnp.asarray(twiddles(tiles, width, 1.0, scale)),
         jnp.asarray(right_table(width, 1.0, 1.0)),
-    )
+        *spectra,
+        probe_mine,
+    )
+    psi_new, probe_new = call(
+        finish_kernel,
+        "field_probe",
+        [shape(2, 1, rows_total, width), shape(2, side, side)],
+        [VMEM] * 5 + [ANY],
+    )(base, partner, other, probe_mine, probe_theirs, token)
     return psi_new, probe_new, tomo
 
 

time: 86.1 us -> 81.5 us (0.947)
  blocking collectives: 8.25 us -> 0 us
  starting transfers between devices: 27.6 us -> 31.5 us
    ppermute x8 -> x18, waiting for transfers between devices: 10.9 us -> 22.3 us  [swap(): lax.ppermute(array, ('angle', 'tile'), [(i, i ^ mask) for i in range(devi...]
    all_to_all x1, waiting for transfers between devices: 11.6 us -> 1.34 us  [shards(): slabs = lax.all_to_all(slabs, 'tile', 0, 0, tiled=True)]
    ppermute x8 -> x18, starting transfers between devices: 10.9 us -> 19.7 us  [swap(): lax.ppermute(array, ('angle', 'tile'), [(i, i ^ mask) for i in range(devi...]
    all_gather x1 -> x0, blocking collectives: 8.25 us -> none  [shards(): spectra = lax.all_gather(spectrum, 'angle', axis=0, tiled=False)]
    all_to_all x1 -> x0, starting transfers between devices: 3.55 us -> none  [shards(): lax.all_to_all(chunks, 'tile', 0, 0, tiled=True).reshape(2, side, side)]
    ppermute x3, starting transfers between devices: 6.9 us -> 5.51 us  [exchange(): lax.ppermute(to_partner, 'tile', pairs(0))]
    all_to_all x1 -> x0, waiting for transfers between devices: 0.94 us -> none  [shards(): lax.all_to_all(chunks, 'tile', 0, 0, tiled=True).reshape(2, side, side)]
    pallas_call x6 -> x10, Pallas kernels: 14.2 us -> 14.4 us  [the longest x1 6.64 us: shards(): call(functools.partial(inverse_kernel, depth, masks), 'slab_image', [shap...]
  transfers between devices with their start and end apart: 16 -> 25, of which waited for: 7 -> 12; matrix products, arithmetic and copies ran while one was open for 0% -> 0% of each run, Pallas kernels for 11% -> 11%
where the time goes in v3:
time: 81.5 us; the launch traced here: 81.1 us
  starting transfers between devices  31.5 us (39%)
  Pallas kernels  23.7 us (29%)
  waiting for transfers between devices  23.7 us (29%)
  between operations  2.16 us (3%)
    ppermute x18, waiting for transfers between devices, swap(): lax.ppermute(array, ('angle', 'tile'), [(i, i ^ mask) for i in range(devi...  22.3 us
    ppermute x18, starting transfers between devices, swap(): lax.ppermute(array, ('angle', 'tile'), [(i, i ^ mask) for i in range(devi...  19.7 us
    pallas_call x1, Pallas kernels, shards(): call(functools.partial(inverse_kernel, depth, masks), 'slab_image', [shap...  6.64 us
    pallas_call x1, Pallas kernels, shards(): call(second_kernel, 'ptycho_second', [shape(tiles, 4 * depth, width), sha...  6.61 us
    pallas_call x1, Pallas kernels, shards(): call(first_kernel, 'ptycho_first', [shape(*block)] * 4 + [half] * 2, [HBM...  5.72 us
    ppermute x3, starting transfers between devices, exchange(): lax.ppermute(to_partner, 'tile', pairs(0))  5.51 us
    all_to_all x1, starting transfers between devices, shards(): slabs = lax.all_to_all(slabs, 'tile', 0, 0, tiled=True)  4.17 us
    ppermute x3, starting transfers between devices, exchange(): lax.ppermute(to_other, 'tile', pairs(1))  2.15 us
  transfers between devices with their start and end apart: 25, of which 12 were waited for; matrix products, arithmetic and copies ran while one was open for 0% of the time, Pallas kernels for 11%

profile of v3, /device:TPU:0, one launch (start us, length us, event | category | flops | bytes accessed | tf_op | source)
XLA Modules:
  0.0 81.1 jit_solution(8430151721001048284)
XLA Ops:
  0.6 1.0 %psi_pack.1 = (f32[160,128]{1,0:T(8,128)S(1)}, f32[160,128]{1,0:T(8,128)S(1)}) custom-call(f32[2,1,160,128]{3,2,1,0:T(8,128)} %psi.1), custom_call_target="tpu_custom_call" | custom-call | tf_op jit(solution)/shard_map/psi_pack/pallas_call | solution.py:574
  1.7 3.0 %collective-permute-start = (f32[160,128]{1,0:T(8,128)S(1)}, f32[160,128]{1,0:T(8,128)S(1)}, u32[]{:S(2)}, u32[]{:S(2)}) collective-permute-start(f32[160,128]{1,0:T(8,128)S(1)} %get-tuple-element.37), channel_id=1, source_target_pairs={{0,1},{2,3},{4,5},{6,7},{1,0},{3,2},{5,4},{7,6},{8,9},{10,11},{12,... | collective-permute-start | bytes 245768 | tf_op jit(solution)/shard_map/ppermute | solution.py:528
  4.7 0.7 collective-permute-start.1
  6.6 1.9 %stage_operands.1 = (f32[2,1,160,128]{3,2,1,0:T(8,128)S(1)}, f32[2,1,160,128]{3,2,1,0:T(8,128)S(1)}, f32[2,128,128]{2,1,0:T(8,128)S(1)}, f32[1,1,16,128,128]{4,3...) custom-call(f32[2,1,160,128]{3,2,1,0:T(8,128)} %psi.1, ...), custom_call_target="tpu_custom_call" | custom-call | bytes 3000000 | tf_op jit(solution)/shard_map/stage_operands/pallas_call | solution.py:586
  8.5 0.0 collective-permute-done.partner
  8.6 5.7 %ptycho_first.1 = (f32[2,160,128]{2,1,0:T(8,128)S(1)}, f32[2,160,128]{2,1,0:T(8,128)S(1)}, f32[2,160,128]{2,1,0:T(8,128)S(1)}, f32[2,160,128]{2,1,0:T(8,128)S(1)...) custom-call(s32[1,1,16]{2,1,0:T(1,128)} %pos_z.3, s32[1,1,16]{2,1,0:T(1,128)} %pos_x.3, s32[1,1]{1,0:T(1,128)S(6)} %copy.19.counts, ...), custom_call_target="tpu_custom_call" | custom-call | flops 3221225472 | tf_op jit(solution)/shard_map/ptycho_first/pallas_call | solution.py:600
  14.3 0.1 collective-permute-start.4
  14.4 1.2 %collective-permute-done.4.refs_1_ = f32[136,128]{1,0:T(8,128)S(1)} collective-permute-done((f32[136,128]{1,0:T(8,128)S(1)}, f32[136,128]{1,0:T(8,128)S(1)}, u32[]{:S(2)}, u32[]{:S(2)}) %collective-permute-start.4) | collective-permute-done | bytes 69664 | tf_op jit(solution)/shard_map/ppermute | solution.py:534
  15.6 5.3 %collective-permute-start.7 = (f32[136,128]{1,0:T(8,128)S(1)}, f32[136,128]{1,0:T(8,128)S(1)}, u32[]{:S(2)}, u32[]{:S(2)}) collective-permute-start(f32[136,128]{1,0:T(8,128)S(1)} %probe_sum.5.refs_0_), channel_id=1, source_target_pairs={{0,17},{1,16},{2,19},{3,18},{4,21},{5,20},{6,23},{7,22},{8,25},{9,... | collective-permute-start | bytes 208904 | tf_op jit(solution)/shard_map/ppermute | solution.py:534
  21.0 0.0 collective-permute-start.6
  21.0 0.6 collective-permute-start.5
  21.6 1.9 %collective-permute-start.2 = (f32[2,160,128]{2,1,0:T(8,128)S(1)}, f32[2,160,128]{2,1,0:T(8,128)S(1)}, u32[]{:S(2)}, u32[]{:S(2)}) collective-permute-start(f32[2,160,128]{2,1,0:T(8,128)S(1)} %get-tuple-element.47), channel_id=1, source_target_pairs={{0,1},{2,3},{4,5},{6,7},{1,0},{3,2},{5,4},{7,6},{8,9},{10,11},{12,... | collective-permute-start | bytes 491528 | tf_op jit(solution)/shard_map/ppermute | solution.py:528
  23.5 0.7 collective-permute-start.3
  24.2 0.0 collective-permute-done.7.refs_3_
  24.2 1.9 %collective-permute-done.6.refs_2_ = f32[136,128]{1,0:T(8,128)S(1)} collective-permute-done((f32[136,128]{1,0:T(8,128)S(1)}, f32[136,128]{1,0:T(8,128)S(1)}, u32[]{:S(2)}, u32[]{:S(2)}) %collective-permute-start.6) | collective-permute-done | bytes 69664 | tf_op jit(solution)/shard_map/ppermute | solution.py:534
  26.0 0.0 collective-permute-done.5.refs_1_
  26.1 4.2 %collective-permute-start.10 = (f32[136,128]{1,0:T(8,128)S(1)}, f32[136,128]{1,0:T(8,128)S(1)}, u32[]{:S(2)}, u32[]{:S(2)}) collective-permute-start(f32[136,128]{1,0:T(8,128)S(1)} %probe_sum.6.refs_0_), channel_id=1, source_target_pairs={{0,6},{1,7},{2,4},{3,5},{4,2},{5,3},{6,0},{7,1},{8,14},{9,15},{10,... | collective-permute-start | bytes 208904 | tf_op jit(solution)/shard_map/ppermute | solution.py:534
  30.2 0.6 collective-permute-start.8
  30.9 5.3 %collective-permute-done.10.refs_3_ = f32[136,128]{1,0:T(8,128)S(1)} collective-permute-done((f32[136,128]{1,0:T(8,128)S(1)}, f32[136,128]{1,0:T(8,128)S(1)}, u32[]{:S(2)}, u32[]{:S(2)}) %collective-permute-start.10) | collective-permute-done | bytes 69664 | tf_op jit(solution)/shard_map/ppermute | solution.py:534
  36.2 1.8 %collective-permute-done.9.refs_2_ = f32[136,128]{1,0:T(8,128)S(1)} collective-permute-done((f32[136,128]{1,0:T(8,128)S(1)}, f32[136,128]{1,0:T(8,128)S(1)}, u32[]{:S(2)}, u32[]{:S(2)}) %collective-permute-start.9) | collective-permute-done | bytes 69664 | tf_op jit(solution)/shard_map/ppermute | solution.py:534
  38.0 0.1 collective-permute-start.11
  38.1 0.7 phase_table.1.rest_4_.phases
  38.8 0.0 collective-permute-done.2.partner
  38.8 0.0 collective-permute-done.3.other
  38.8 0.5 collective-permute-done.11.probe_theirs
  39.4 6.6 %ptycho_second.1 = (f32[8,80,128]{2,1,0:T(8,128)}, f32[2,160,128]{2,1,0:T(8,128)S(1)}, f32[160,128]{1,0:T(8,128)S(1)}, f32[160,128]{1,0:T(8,128)S(1)}, f32[128,128]{1,0:T(8,128)S(1)}, /*index=5*/f32[128,128]{1,0:T(8,128)S(1)}) custom-call(s32[1,1,16]{2,1,0:T(1,128)} %pos_z.3, s32[1,1,16]{2,1,0:T(1,128)} %pos_x.3, s32[1,1]{1,0:T(1,128)S(6)} %copy.19.counts, ...), custom_call_target="tpu_custom_call" | custom-call | flops 3221225472 | tf_op jit(solution)/shard_map/ptycho_second/pallas_call | solution.py:639
  46.0 4.2 %all-to-all-start = ((f32[8,80,128]{2,1,0:T(8,128)}), f32[8,80,128]{2,1,0:T(8,128)S(1)}, u32[]{:S(2)}, u32[]{:S(2)}) async-start(f32[8,80,128]{2,1,0:T(8,128)} %get-tuple-element.56), calls=%async_computation | async-start | bytes 655360 | tf_op jit(solution)/shard_map/all_to_all | solution.py:650
  50.2 1.2 %collective-permute-done.12.refs_1_ = f32[128,128]{1,0:T(8,128)S(1)} collective-permute-done((f32[128,128]{1,0:T(8,128)S(1)}, f32[128,128]{1,0:T(8,128)S(1)}, u32[]{:S(2)}, u32[]{:S(2)}) %collective-permute-start.12) | collective-permute-done | bytes 65568 | tf_op jit(solution)/shard_map/ppermute | solution.py:534
  51.4 3.0 %collective-permute-start.15 = (f32[128,128]{1,0:T(8,128)S(1)}, f32[128,128]{1,0:T(8,128)S(1)}, u32[]{:S(2)}, u32[]{:S(2)}) collective-permute-start(f32[128,128]{1,0:T(8,128)S(1)} %probe_sum.7.refs_0_), channel_id=1, source_target_pairs={{0,17},{1,16},{2,19},{3,18},{4,21},{5,20},{6,23},{7,22},{8,25},{9,... | collective-permute-start | bytes 196616 | tf_op jit(solution)/shard_map/ppermute | solution.py:534
  54.4 0.0 collective-permute-start.14
  54.4 0.6 collective-permute-start.13
  55.1 3.3 %collective-permute-done.15.refs_3_ = f32[128,128]{1,0:T(8,128)S(1)} collective-permute-done((f32[128,128]{1,0:T(8,128)S(1)}, f32[128,128]{1,0:T(8,128)S(1)}, u32[]{:S(2)}, u32[]{:S(2)}) %collective-permute-start.15) | collective-permute-done | bytes 65568 | tf_op jit(solution)/shard_map/ppermute | solution.py:534
  58.4 0.9 %collective-permute-done.14.refs_2_ = f32[128,128]{1,0:T(8,128)S(1)} collective-permute-done((f32[128,128]{1,0:T(8,128)S(1)}, f32[128,128]{1,0:T(8,128)S(1)}, u32[]{:S(2)}, u32[]{:S(2)}) %collective-permute-start.14) | collective-permute-done | bytes 65568 | tf_op jit(solution)/shard_map/ppermute | solution.py:534
  59.4 0.1 collective-permute-done.13.refs_1_
  59.4 1.3 %all-to-all-done.slabs = f32[8,80,128]{2,1,0:T(8,128)S(1)} async-done(((f32[8,80,128]{2,1,0:T(8,128)}), f32[8,80,128]{2,1,0:T(8,128)S(1)}, u32[]{:S(2)}, u32[]{:S(2)}) %all-to-all-start) | async-done | bytes 327712 | tf_op jit(solution)/shard_map/all_to_all | solution.py:650
  60.8 0.3 slab_spectrum.1.rest_0_
  61.0 0.1 collective-permute-start.17
  61.1 1.5 %collective-permute-start.23 = (f32[320,128]{1,0:T(8,128)S(1)}, f32[320,128]{1,0:T(8,128)S(1)}, u32[]{:S(2)}, u32[]{:S(2)}) collective-permute-start(f32[320,128]{1,0:T(8,128)S(1)} %slab_spectrum.1.rest_0_), channel_id=1, source_target_pairs={{0,24},{1,25},{2,26},{3,27},{4,28},{5,29},{6,30},{7,31},{8,16},{9,... | collective-permute-start | bytes 491528 | tf_op jit(solution)/shard_map/ppermute | solution.py:534
  62.7 0.6 collective-permute-start.22
  63.3 1.0 %collective-permute-start.16 = (f32[128,128]{1,0:T(8,128)S(1)}, f32[128,128]{1,0:T(8,128)S(1)}, u32[]{:S(2)}, u32[]{:S(2)}) collective-permute-start(f32[128,128]{1,0:T(8,128)S(1)} %probe_sum.8.refs_0_.rest_0_), channel_id=1, source_target_pairs={{0,2},{1,3},{2,0},{3,1},{4,6},{5,7},{6,4},{7,5},{8,10},{9,11},{10,... | collective-permute-start | bytes 196616 | tf_op jit(solution)/shard_map/ppermute | solution.py:534
  64.3 3.2 %collective-permute-done.16.refs_1_ = f32[128,128]{1,0:T(8,128)S(1)} collective-permute-done((f32[128,128]{1,0:T(8,128)S(1)}, f32[128,128]{1,0:T(8,128)S(1)}, u32[]{:S(2)}, u32[]{:S(2)}) %collective-permute-start.16) | collective-permute-done | bytes 65568 | tf_op jit(solution)/shard_map/ppermute | solution.py:534
  67.6 1.8 %collective-permute-start.20 = (f32[128,128]{1,0:T(8,128)S(1)}, f32[128,128]{1,0:T(8,128)S(1)}, u32[]{:S(2)}, u32[]{:S(2)}) collective-permute-start(f32[128,128]{1,0:T(8,128)S(1)} %probe_sum.9.refs_0_), channel_id=1, source_target_pairs={{0,4},{1,5},{2,6},{3,7},{4,0},{5,1},{6,2},{7,3},{8,12},{9,13},{10,... | collective-permute-start | bytes 196616 | tf_op jit(solution)/shard_map/ppermute | solution.py:534
  69.4 0.6 collective-permute-start.18
  70.0 0.8 %collective-permute-start.19 = (f32[160,128]{1,0:T(8,128)S(1)}, f32[160,128]{1,0:T(8,128)S(1)}, u32[]{:S(2)}, u32[]{:S(2)}) collective-permute-start(f32[160,128]{1,0:T(8,128)S(1)} %get-tuple-element.60), channel_id=1, source_target_pairs={{1,2},{3,4},{5,6},{2,1},{4,3},{6,5},{9,10},{11,12},{13,14},{10,9},... | collective-permute-start | bytes 245768 | tf_op jit(solution)/shard_map/ppermute | solution.py:529
  70.8 2.7 %collective-permute-done.20.refs_1_ = f32[128,128]{1,0:T(8,128)S(1)} collective-permute-done((f32[128,128]{1,0:T(8,128)S(1)}, f32[128,128]{1,0:T(8,128)S(1)}, u32[]{:S(2)}, u32[]{:S(2)}) %collective-permute-start.20) | collective-permute-done | bytes 65568 | tf_op jit(solution)/shard_map/ppermute | solution.py:534
  73.5 0.1 collective-permute-start.21
  73.6 6.6 %slab_image.1 = (bf16[2,20,32,1024]{3,2,1,0:T(8,128)(2,1)}, f32[8,128]{1,0:T(8,128)S(1)}) custom-call(f32[4,2,8,32,128]{4,3,2,1,0:T(8,128)S(1)} %phase_table.1.rest_4_.phases, f32[2,8,128]{2,1,0:T(8,128)S(1)} %copy-done.3, bf16[768,256]{1,0:T(8,128)(2,1)S(1)} %copy-done.2, f32[320,128]{1,0:T(8,128)S(1)} %slab_spectrum.1.rest_0_, ...), custom_call_target="tpu_custom_call" | custom-call | flops 2013265920 | tf_op jit(solution)/shard_map/slab_image/pallas_call | solution.py:687
  80.3 0.8 field_probe.1
  (25 shorter events, 0.1 us)
Async XLA Ops:
  1.7 6.9 %collective-permute-start = (f32[160,128]{1,0:T(8,128)S(1)}, f32[160,128]{1,0:T(8,128)S(1)}, u32[]{:S(2)}, u32[]{:S(2)}) collective-permute-start(f32[160,128]{1,0:T(8,128)S(1)} %get-tuple-element.37), channel_id=1, source_target_pairs={{0,1},{2,3},{4,5},{6,7},{1,0},{3,2},{5,4},{7,6},{8,9},{10,11},{12,... | collective-permute-start | bytes 245768 | tf_op jit(solution)/shard_map/ppermute | solution.py:528
  4.7 3.9 %collective-permute-start.1 = (f32[160,128]{1,0:T(8,128)S(1)}, f32[160,128]{1,0:T(8,128)S(1)}, u32[]{:S(2)}, u32[]{:S(2)}) collective-permute-start(f32[160,128]{1,0:T(8,128)S(1)} %get-tuple-element.38), channel_id=1, source_target_pairs={{1,2},{3,4},{5,6},{2,1},{4,3},{6,5},{9,10},{11,12},{13,14},{10,9},... | collective-permute-start | bytes 245768 | tf_op jit(solution)/shard_map/ppermute | solution.py:529
  14.3 1.3 %collective-permute-start.4 = (f32[136,128]{1,0:T(8,128)S(1)}, f32[136,128]{1,0:T(8,128)S(1)}, u32[]{:S(2)}, u32[]{:S(2)}) collective-permute-start(f32[136,128]{1,0:T(8,128)S(1)} %get-tuple-element.50), channel_id=1, source_target_pairs={{0,8},{1,9},{2,10},{3,11},{4,12},{5,13},{6,14},{7,15},{8,0},{9,1},... | collective-permute-start | bytes 208904 | tf_op jit(solution)/shard_map/ppermute | solution.py:534
  15.6 8.5 %collective-permute-start.7 = (f32[136,128]{1,0:T(8,128)S(1)}, f32[136,128]{1,0:T(8,128)S(1)}, u32[]{:S(2)}, u32[]{:S(2)}) collective-permute-start(f32[136,128]{1,0:T(8,128)S(1)} %probe_sum.5.refs_0_), channel_id=1, source_target_pairs={{0,17},{1,16},{2,19},{3,18},{4,21},{5,20},{6,23},{7,22},{8,25},{9,... | collective-permute-start | bytes 208904 | tf_op jit(solution)/shard_map/ppermute | solution.py:534
  21.0 5.1 %collective-permute-start.6 = (f32[136,128]{1,0:T(8,128)S(1)}, f32[136,128]{1,0:T(8,128)S(1)}, u32[]{:S(2)}, u32[]{:S(2)}) collective-permute-start(f32[136,128]{1,0:T(8,128)S(1)} %probe_sum.5.refs_0_), channel_id=1, source_target_pairs={{0,1},{1,0},{2,3},{3,2},{4,5},{5,4},{6,7},{7,6},{8,9},{9,8},{10,11... | collective-permute-start | bytes 208904 | tf_op jit(solution)/shard_map/ppermute | solution.py:534
  21.0 5.1 %collective-permute-start.5 = (f32[136,128]{1,0:T(8,128)S(1)}, f32[136,128]{1,0:T(8,128)S(1)}, u32[]{:S(2)}, u32[]{:S(2)}) collective-permute-start(f32[136,128]{1,0:T(8,128)S(1)} %probe_sum.5.refs_0_), channel_id=1, source_target_pairs={{0,16},{1,17},{2,18},{3,19},{4,20},{5,21},{6,22},{7,23},{8,24},{9,... | collective-permute-start | bytes 208904 | tf_op jit(solution)/shard_map/ppermute | solution.py:534
  21.6 17.2 %collective-permute-start.2 = (f32[2,160,128]{2,1,0:T(8,128)S(1)}, f32[2,160,128]{2,1,0:T(8,128)S(1)}, u32[]{:S(2)}, u32[]{:S(2)}) collective-permute-start(f32[2,160,128]{2,1,0:T(8,128)S(1)} %get-tuple-element.47), channel_id=1, source_target_pairs={{0,1},{2,3},{4,5},{6,7},{1,0},{3,2},{5,4},{7,6},{8,9},{10,11},{12,... | collective-permute-start | bytes 491528 | tf_op jit(solution)/shard_map/ppermute | solution.py:528
  23.5 15.3 %collective-permute-start.3 = (f32[2,160,128]{2,1,0:T(8,128)S(1)}, f32[2,160,128]{2,1,0:T(8,128)S(1)}, u32[]{:S(2)}, u32[]{:S(2)}) collective-permute-start(f32[2,160,128]{2,1,0:T(8,128)S(1)} %get-tuple-element.48), channel_id=1, source_target_pairs={{1,2},{3,4},{5,6},{2,1},{4,3},{6,5},{9,10},{11,12},{13,14},{10,9},... | collective-permute-start | bytes 491528 | tf_op jit(solution)/shard_map/ppermute | solution.py:529
  26.1 10.1 %collective-permute-start.10 = (f32[136,128]{1,0:T(8,128)S(1)}, f32[136,128]{1,0:T(8,128)S(1)}, u32[]{:S(2)}, u32[]{:S(2)}) collective-permute-start(f32[136,128]{1,0:T(8,128)S(1)} %probe_sum.6.refs_0_), channel_id=1, source_target_pairs={{0,6},{1,7},{2,4},{3,5},{4,2},{5,3},{6,0},{7,1},{8,14},{9,15},{10,... | collective-permute-start | bytes 208904 | tf_op jit(solution)/shard_map/ppermute | solution.py:534
  30.2 7.8 %collective-permute-start.9 = (f32[136,128]{1,0:T(8,128)S(1)}, f32[136,128]{1,0:T(8,128)S(1)}, u32[]{:S(2)}, u32[]{:S(2)}) collective-permute-start(f32[136,128]{1,0:T(8,128)S(1)} %probe_sum.6.refs_0_), channel_id=1, source_target_pairs={{0,4},{1,5},{2,6},{3,7},{4,0},{5,1},{6,2},{7,3},{8,12},{9,13},{10,... | collective-permute-start | bytes 208904 | tf_op jit(solution)/shard_map/ppermute | solution.py:534
  30.2 7.8 %collective-permute-start.8 = (f32[136,128]{1,0:T(8,128)S(1)}, f32[136,128]{1,0:T(8,128)S(1)}, u32[]{:S(2)}, u32[]{:S(2)}) collective-permute-start(f32[136,128]{1,0:T(8,128)S(1)} %probe_sum.6.refs_0_), channel_id=1, source_target_pairs={{0,2},{1,3},{2,0},{3,1},{4,6},{5,7},{6,4},{7,5},{8,10},{9,11},{10,... | collective-permute-start | bytes 208904 | tf_op jit(solution)/shard_map/ppermute | solution.py:534
  38.0 1.3 %collective-permute-start.11 = (f32[128,128]{1,0:T(8,128)S(1)}, f32[128,128]{1,0:T(8,128)S(1)}, u32[]{:S(2)}, u32[]{:S(2)}) collective-permute-start(f32[128,128]{1,0:T(8,128)S(1)} %get-tuple-element.51.probe_mine), channel_id=1, source_target_pairs={{0,8},{1,9},{2,10},{3,11},{4,12},{5,13},{6,14},{7,15},{8,0},{9,1},... | collective-permute-start | bytes 196616 | tf_op jit(solution)/shard_map/ppermute | solution.py:534
  39.4 21.4 %copy-start = (bf16[768,256]{1,0:T(8,128)(2,1)S(1)}, bf16[768,256]{1,0:T(8,128)(2,1)}, u32[]{:S(2)}) copy-start(bf16[768,256]{1,0:T(8,128)(2,1)} %constant.21.clone.table) | copy-start | bytes 1179652
  39.4 21.4 %copy-start.1 = (f32[2,8,128]{2,1,0:T(8,128)S(1)}, f32[2,8,128]{2,1,0:T(8,128)}, u32[]{:S(2)}) copy-start(f32[2,8,128]{2,1,0:T(8,128)} %constant.20.clone.turn) | copy-start | bytes 24580
  39.4 34.3 %copy-start.2 = (bf16[768,256]{1,0:T(8,128)(2,1)S(1)}, bf16[768,256]{1,0:T(8,128)(2,1)}, u32[]{:S(2)}) copy-start(bf16[768,256]{1,0:T(8,128)(2,1)} %constant.23.clone.table) | copy-start | bytes 1179652
  39.4 34.3 %copy-start.3 = (f32[2,8,128]{2,1,0:T(8,128)S(1)}, f32[2,8,128]{2,1,0:T(8,128)}, u32[]{:S(2)}) copy-start(f32[2,8,128]{2,1,0:T(8,128)} %constant.22.clone.turn) | copy-start | bytes 24580
  46.0 14.8 %all-to-all-start = ((f32[8,80,128]{2,1,0:T(8,128)}), f32[8,80,128]{2,1,0:T(8,128)S(1)}, u32[]{:S(2)}, u32[]{:S(2)}) async-start(f32[8,80,128]{2,1,0:T(8,128)} %get-tuple-element.56), calls=%async_computation | async-start | bytes 655360 | tf_op jit(solution)/shard_map/all_to_all | solution.py:650
  50.1 1.3 %collective-permute-start.12 = (f32[128,128]{1,0:T(8,128)S(1)}, f32[128,128]{1,0:T(8,128)S(1)}, u32[]{:S(2)}, u32[]{:S(2)}) collective-permute-start(f32[128,128]{1,0:T(8,128)S(1)} %get-tuple-element.55), channel_id=1, source_target_pairs={{0,8},{1,9},{2,10},{3,11},{4,12},{5,13},{6,14},{7,15},{8,0},{9,1},... | collective-permute-start | bytes 196616 | tf_op jit(solution)/shard_map/ppermute | solution.py:534
  51.4 7.0 %collective-permute-start.15 = (f32[128,128]{1,0:T(8,128)S(1)}, f32[128,128]{1,0:T(8,128)S(1)}, u32[]{:S(2)}, u32[]{:S(2)}) collective-permute-start(f32[128,128]{1,0:T(8,128)S(1)} %probe_sum.7.refs_0_), channel_id=1, source_target_pairs={{0,17},{1,16},{2,19},{3,18},{4,21},{5,20},{6,23},{7,22},{8,25},{9,... | collective-permute-start | bytes 196616 | tf_op jit(solution)/shard_map/ppermute | solution.py:534
  54.4 4.9 %collective-permute-start.14 = (f32[128,128]{1,0:T(8,128)S(1)}, f32[128,128]{1,0:T(8,128)S(1)}, u32[]{:S(2)}, u32[]{:S(2)}) collective-permute-start(f32[128,128]{1,0:T(8,128)S(1)} %probe_sum.7.refs_0_), channel_id=1, source_target_pairs={{0,1},{1,0},{2,3},{3,2},{4,5},{5,4},{6,7},{7,6},{8,9},{9,8},{10,11... | collective-permute-start | bytes 196616 | tf_op jit(solution)/shard_map/ppermute | solution.py:534
  54.4 5.0 %collective-permute-start.13 = (f32[128,128]{1,0:T(8,128)S(1)}, f32[128,128]{1,0:T(8,128)S(1)}, u32[]{:S(2)}, u32[]{:S(2)}) collective-permute-start(f32[128,128]{1,0:T(8,128)S(1)} %probe_sum.7.refs_0_), channel_id=1, source_target_pairs={{0,16},{1,17},{2,18},{3,19},{4,20},{5,21},{6,22},{7,23},{8,24},{9,... | collective-permute-start | bytes 196616 | tf_op jit(solution)/shard_map/ppermute | solution.py:534
  61.0 6.5 %collective-permute-start.17 = (f32[320,128]{1,0:T(8,128)S(1)}, f32[320,128]{1,0:T(8,128)S(1)}, u32[]{:S(2)}, u32[]{:S(2)}) collective-permute-start(f32[320,128]{1,0:T(8,128)S(1)} %slab_spectrum.1.rest_0_), channel_id=1, source_target_pairs={{0,8},{1,9},{2,10},{3,11},{4,12},{5,13},{6,14},{7,15},{8,0},{9,1},... | collective-permute-start | bytes 491528 | tf_op jit(solution)/shard_map/ppermute | solution.py:534
  61.1 12.5 %collective-permute-start.23 = (f32[320,128]{1,0:T(8,128)S(1)}, f32[320,128]{1,0:T(8,128)S(1)}, u32[]{:S(2)}, u32[]{:S(2)}) collective-permute-start(f32[320,128]{1,0:T(8,128)S(1)} %slab_spectrum.1.rest_0_), channel_id=1, source_target_pairs={{0,24},{1,25},{2,26},{3,27},{4,28},{5,29},{6,30},{7,31},{8,16},{9,... | collective-permute-start | bytes 491528 | tf_op jit(solution)/shard_map/ppermute | solution.py:534
  62.7 10.9 %collective-permute-start.22 = (f32[320,128]{1,0:T(8,128)S(1)}, f32[320,128]{1,0:T(8,128)S(1)}, u32[]{:S(2)}, u32[]{:S(2)}) collective-permute-start(f32[320,128]{1,0:T(8,128)S(1)} %slab_spectrum.1.rest_0_), channel_id=1, source_target_pairs={{0,16},{1,17},{2,18},{3,19},{4,20},{5,21},{6,22},{7,23},{8,24},{9,... | collective-permute-start | bytes 491528 | tf_op jit(solution)/shard_map/ppermute | solution.py:534
  63.3 4.3 %collective-permute-start.16 = (f32[128,128]{1,0:T(8,128)S(1)}, f32[128,128]{1,0:T(8,128)S(1)}, u32[]{:S(2)}, u32[]{:S(2)}) collective-permute-start(f32[128,128]{1,0:T(8,128)S(1)} %probe_sum.8.refs_0_.rest_0_), channel_id=1, source_target_pairs={{0,2},{1,3},{2,0},{3,1},{4,6},{5,7},{6,4},{7,5},{8,10},{9,11},{10,... | collective-permute-start | bytes 196616 | tf_op jit(solution)/shard_map/ppermute | solution.py:534
  67.6 5.9 %collective-permute-start.20 = (f32[128,128]{1,0:T(8,128)S(1)}, f32[128,128]{1,0:T(8,128)S(1)}, u32[]{:S(2)}, u32[]{:S(2)}) collective-permute-start(f32[128,128]{1,0:T(8,128)S(1)} %probe_sum.9.refs_0_), channel_id=1, source_target_pairs={{0,4},{1,5},{2,6},{3,7},{4,0},{5,1},{6,2},{7,3},{8,12},{9,13},{10,... | collective-permute-start | bytes 196616 | tf_op jit(solution)/shard_map/ppermute | solution.py:534
  69.4 10.9 %collective-permute-start.18 = (f32[160,128]{1,0:T(8,128)S(1)}, f32[160,128]{1,0:T(8,128)S(1)}, u32[]{:S(2)}, u32[]{:S(2)}) collective-permute-start(f32[160,128]{1,0:T(8,128)S(1)} %get-tuple-element.59), channel_id=1, source_target_pairs={{0,1},{2,3},{4,5},{6,7},{1,0},{3,2},{5,4},{7,6},{8,9},{10,11},{12,... | collective-permute-start | bytes 245768 | tf_op jit(solution)/shard_map/ppermute | solution.py:528
  70.0 10.3 %collective-permute-start.19 = (f32[160,128]{1,0:T(8,128)S(1)}, f32[160,128]{1,0:T(8,128)S(1)}, u32[]{:S(2)}, u32[]{:S(2)}) collective-permute-start(f32[160,128]{1,0:T(8,128)S(1)} %get-tuple-element.60), channel_id=1, source_target_pairs={{1,2},{3,4},{5,6},{2,1},{4,3},{6,5},{9,10},{11,12},{13,14},{10,9},... | collective-permute-start | bytes 245768 | tf_op jit(solution)/shard_map/ppermute | solution.py:529
  73.5 6.8 %collective-permute-start.21 = (f32[128,128]{1,0:T(8,128)S(1)}, f32[128,128]{1,0:T(8,128)S(1)}, u32[]{:S(2)}, u32[]{:S(2)}) collective-permute-start(f32[128,128]{1,0:T(8,128)S(1)} %probe_last.1.rest_4_.probe_mine), channel_id=1, source_target_pairs={{0,8},{1,9},{2,10},{3,11},{4,12},{5,13},{6,14},{7,15},{8,0},{9,1},... | collective-permute-start | bytes 196616 | tf_op jit(solution)/shard_map/ppermute | solution.py:534

commit v4 on v3

--- a/solution.py
+++ b/solution.py
@@ -79,6 +79,11 @@
             turned = (real, imag)
         elif 4 * index == count:
             turned = (-imag, real) if orient > 0 else (imag, -real)
+        elif 8 * index in (count, 3 * count):
+            tangent = orient if 8 * index == count else -orient
+            plus, minus = (real + imag, imag - real)
+            turned = (-minus, plus) if tangent > 0 else (plus, minus)
+            turned = tuple(math.cos(angle) * value for value in turned)
         else:
             cosine, sine = math.cos(angle), math.sin(angle)
             turned = (real * cosine - imag * sine, real * sine + imag * cosine)
@@ -110,7 +115,7 @@
     slots = data.shape[2]
     group = math.gcd(slots, GROUP)
     wide = math.gcd(group, 2)
-    lanes = lax.broadcasted_iota(jnp.int32, (side, side), 1)
+    lanes = lax.broadcasted_iota(jnp.int32, (8, side), 1)
     grad_own[...] = jnp.zeros_like(grad_own)
     grad_halo[...] = jnp.zeros_like(grad_halo)
     grad_probe[...] = jnp.zeros_like(grad_probe)
@@ -122,13 +127,17 @@
         inside = (lanes >= start) & (lanes < side + start)
         return pl.ds(pos_z[0, 0, slot], side), back, forth, inside
 
+    def pick(inside, yes, no):
+        rows = (side // 8, 8, side)
+        return jnp.where(inside[None], yes.reshape(rows), no.reshape(rows)).reshape(side, side)
+
     def cut_out(first, _):
         waves = []
         for slot in range(first, first + group):
             where, back, _, inside = place(slot)
             cut = []
             for part in range(2):
-                mixed = jnp.where(inside, own[part, where, :], halo[part, where, :])
+                mixed = pick(inside, own[part, where, :], halo[part, where, :])
                 cut.append(pltpu.roll(mixed, back, 1))
                 patches[slot, part] = cut[part]
             waves.append(
@@ -202,8 +211,9 @@
             )
             for part in range(2):
                 moved = pltpu.roll(grads[part], forth, 1)
-                grad_own[part, where, :] += jnp.where(inside, moved, 0.0)
-                grad_halo[part, where, :] += jnp.where(inside, 0.0, moved)
+                zero = jnp.zeros_like(moved)
+                grad_own[part, where, :] += pick(inside, moved, zero)
+                grad_halo[part, where, :] += pick(inside, zero, moved)
         grad_probe[0], grad_probe[1] = sum_real, sum_imag
 
     side_by_side(
@@ -338,8 +348,10 @@
     pos_z, pos_x, counts, base, rim, partner, other, target, probe_mine, probe_theirs, data, *rest
 ):
     tables = rest[:4]
-    slabs_out, base_out, to_partner, to_other, keep_out, send_out = rest[5:11]
-    held, sems, own, halo, hold, edge, probe, work = rest[11:13], *rest[13:19], rest[19:]
+    base_out, to_partner, to_other, keep_out, send_out = rest[5:10]
+    inner = inner_count(lax.axis_size("tile"))
+    slab_outs, rest = rest[10 : 10 + inner], rest[10 + inner :]
+    held, sems, own, halo, hold, edge, probe, work = rest[:2], *rest[2:8], rest[8:]
     copies = load_places((pos_z, pos_x), held, sems)
     pos_z, pos_x = held
     grad_own, grad_halo, grad_probe = work[:3]
@@ -363,7 +375,6 @@
     slot_loop(
         pos_z, pos_x, counts[0, 0], probe.at[0], probe.at[1], data, tables, own, halo, work
     )
-    slabs, depth = slabs_out.shape[0], base.shape[1] // slabs_out.shape[0]
     for part in range(2):
         field = own[part]
         aim = target[part, 0]
@@ -377,17 +388,33 @@
     to_other[...] = jnp.where(even, to_left, to_right)
     keep_out[...] = grad_probe[core]
     send_out[...] = grad_probe[1 - core]
-    for slab in range(slabs):
-        rows = pl.ds(slab * depth, depth)
-        for part in range(2):
-            slabs_out[slab, part * depth : (part + 1) * depth] = hold[part, rows]
-            slabs_out[slab, (2 + part) * depth : (3 + part) * depth] = edge[part, rows]
-
-
-def forward_kernel(slabs, turn, table, *rest):
-    spectrum_out, rows_scratch = rest[-2:]
-    tiles, _, width = slabs.shape
+    outer, depth = slab_outs[0].shape[0], slab_outs[0].shape[1] // 4
+    for step, slab_out in enumerate(slab_outs):
+        for place in range(outer):
+            slab = place * inner + ((tile % inner) ^ step)
+            rows = pl.ds(slab * depth, depth)
+            for part in range(2):
+                slab_out[place, part * depth : (part + 1) * depth] = hold[part, rows]
+                slab_out[place, (2 + part) * depth : (3 + part) * depth] = edge[part, rows]
+
+
+def merge_kernel(*refs):
+    tile = lax.axis_index("tile")
+    inner = inner_count(lax.axis_size("tile"))
+    arrived, merged = refs[:inner], refs[inner:]
+    for step, source in enumerate(arrived):
+        for mask, out in enumerate(merged):
+            out[(tile % inner) ^ step] = source[(tile // inner) ^ mask]
+
+
+def forward_kernel(turn, table, _, *rest):
+    *arrived, spectrum_out, rows_scratch, slabs = rest
+    inner, _, width = arrived[0].shape
+    tiles = slabs.shape[0]
     depth = rows_scratch.shape[0] // tiles
+    outer = lax.axis_index("tile") // inner
+    for mask, source in enumerate(arrived):
+        slabs[pl.ds((outer ^ mask) * inner, inner)] = source[...]
     mask = lane_mask((depth, width), width // 2)
     blocks = []
     for tile in range(tiles):
@@ -434,16 +461,24 @@
             )
             cosine = 1.0 + square * (-1 / 2 + square * (1 / 24 + square * (-1 / 720 + square * (
                 1 / 40320 + square * (-1 / 3628800 + square * (1.0 / 479001600.0))))))
-            table_out[angle, 0, block] = 1.0 - 2.0 * sine * sine
-            table_out[angle, 1, block] = 2.0 * sine * cosine
+            real = 1.0 - 2.0 * sine * sine
+            imag = 2.0 * sine * cosine
+            table_out[angle, 0, block] = real
+            table_out[angle, 1, block] = imag - real
+            table_out[angle, 2, block] = real + imag
 
 
 def inverse_kernel(depth, masks, phases, turn, table, *rest):
-    spectra, image_out, token = rest[: len(masks)], rest[-2], rest[-1]
-    token[...] = jnp.zeros_like(token)
+    spectra = rest[: len(masks)]
+    last, (image_out, psi_out, probe_out) = rest[len(masks) : -3], rest[-3:]
     _, _, tiles, beam, width = phases.shape
     angles = [lax.axis_index("angle") ^ mask for mask in masks]
     group = image_out.shape[1]
+
+    @pl.when(pl.program_id(0) == 0)
+    def _():
+        finish(*last, psi_out, probe_out)
+
     wide = math.gcd(group, 2)
     first = pl.program_id(0) * group
     count = tiles * depth
@@ -451,25 +486,22 @@
     def sum_angles(start, _):
         rows = [[] for _ in range(wide)]
         for block in range(tiles):
-            cosines = [phases[angle, 0, block] for angle in angles]
-            sines = [phases[angle, 1, block] for angle in angles]
+            tables = [[phases[angle, which, block] for which in range(3)] for angle in angles]
             for member in range(wide):
-                real = imag = None
-                for spectrum, cosine, sine in zip(spectra, cosines, sines):
-                    at = block * depth + first + start + member
-                    spec_real = spectrum[pl.ds(at, 1), :]
-                    spec_imag = spectrum[pl.ds(count + at, 1), :]
-                    add_real = cosine * spec_real - sine * spec_imag
-                    add_imag = cosine * spec_imag + sine * spec_real
-                    real = add_real if real is None else real + add_real
-                    imag = add_imag if imag is None else imag + add_imag
-                rows[member].append(jnp.concatenate([real, imag], 1))
+                at = block * depth + first + start + member
+                sums = None
+                for spectrum, three in zip(spectra, tables):
+                    real = spectrum[pl.ds(at, 1), :]
+                    imag = spectrum[pl.ds(count + at, 1), :]
+                    terms = [factor * one for factor, one in zip((real + imag, real, imag), three)]
+                    sums = terms if sums is None else [x + y for x, y in zip(sums, terms)]
+                rows[member].append(jnp.concatenate([sums[0] - sums[2], sums[0] + sums[1]], 1))
         return [halves(jnp.concatenate(blocks, 0)) for blocks in rows]
 
     def transform(start, splits):
         return [dot(jnp.concatenate([high, low, high], 1), table[...]) for high, low in splits]
 
-    def finish(start, images):
+    def store(start, images):
         for member, image in enumerate(images):
             blocks = []
             for block in range(tiles):
@@ -482,10 +514,10 @@
                 image_out[0, start + member, :, columns] = real.astype(BF16)
                 image_out[1, start + member, :, columns] = imag.astype(BF16)
 
-    side_by_side([sum_angles, transform, finish], group, wide)
-
-
-def finish_kernel(base, partner, other, probe_mine, probe_theirs, _, psi_out, probe_out):
+    side_by_side([sum_angles, transform, store], group, wide)
+
+
+def finish(base, partner, other, probe_mine, probe_theirs, psi_out, probe_out):
     mask = lane_mask(base.shape[1:], base.shape[-1] // 2)
     left, right = packed_sides(partner, other, is_even())
     real, imag = unfold(left, right, mask)
@@ -519,15 +551,17 @@
     return jax.ShapeDtypeStruct(dims, dtype)
 
 
+def swap_pairs(array, start, tiles):
+    low = range(start, tiles - 1, 2)
+    return lax.ppermute(array, "tile", [(i, i + 1) for i in low] + [(i + 1, i) for i in low])
+
+
 def exchange(to_partner, to_other, tiles):
-    def pairs(start):
-        low = range(start, tiles - 1, 2)
-        return [(i, i + 1) for i in low] + [(i + 1, i) for i in low]
-
-    return (
-        lax.ppermute(to_partner, "tile", pairs(0)),
-        lax.ppermute(to_other, "tile", pairs(1)),
-    )
+    return swap_pairs(to_partner, 0, tiles), swap_pairs(to_other, 1, tiles)
+
+
+def inner_count(tiles):
+    return max(1, tiles // 4)
 
 
 def swap(array, mask, devices):
@@ -631,15 +665,19 @@
     phases = call(
         functools.partial(phase_kernel, tiles),
         "phase_table",
-        shape(angles, 2, tiles, beam, width),
+        shape(angles, 3, tiles, beam, width),
         [VMEM],
         (),
         angles * tiles * beam * width * 40,
     )(extra)
-    slabs, base, to_partner, to_other, keep, send = call(
+    inner = inner_count(tiles)
+    outer = tiles // inner
+    base, to_partner, to_other, keep, send, *slabs = call(
         second_kernel,
         "ptycho_second",
-        [shape(tiles, 4 * depth, width), shape(*block), flat, flat] + [shape(side, side)] * 2,
+        [shape(*block), flat, flat]
+        + [shape(side, side)] * 2
+        + [shape(outer, 4 * depth, width)] * inner,
         [HBM] * 2 + [SMEM] + [VMEM] * 12 + [ANY],
         places + [pltpu.VMEM(block, F32)] * 4 + [pltpu.VMEM((2, side, side), F32)] + work,
         flops,
@@ -647,9 +685,14 @@
         *(*slot_places, counts, base, rim, partner, other, target_in),
         *(probe_mine, probe_theirs, data_in, *tables, phases),
     )
-    slabs = lax.all_to_all(slabs, "tile", 0, 0, tiled=True)
+    slabs = slabs[:1] + [swap(array, mask + 1, devices) for mask, array in enumerate(slabs[1:])]
+    slabs = call(
+        merge_kernel, "slab_merge", [shape(inner, 4 * depth, width)] * outer, [VMEM] * inner
+    )(*slabs)
+    slabs = [slabs[0]] + [swap(array, (mask + 1) * inner, devices) for mask, array in enumerate(slabs[1:])]
     total = all_but_last(keep, send, rounds)
-    late = total
+    late, to_other = lax.optimization_barrier((total, to_other))
+    other = swap_pairs(to_other, 1, tiles)
     for mask in rounds[-1][: 1 if len(rounds[-1]) > 1 else 0]:
         late = call(sum_kernel, "probe_sum", shape(*late.shape), [VMEM] * 2)(
             late, swap(late, mask, devices)
@@ -659,21 +702,19 @@
         forward_kernel,
         "slab_spectrum",
         shape(2 * count, width),
-        [VMEM] * 3 + [ANY],
-        [pltpu.VMEM((count, 2 * width), F32)],
+        [VMEM] * 2 + [ANY] + [VMEM] * outer,
+        [pltpu.VMEM((count, 2 * width), F32), pltpu.VMEM((tiles, 4 * depth, width), F32)],
     )(
-        slabs,
         jnp.asarray(twiddles(tiles, width, -1.0, 1.0)),
         jnp.asarray(right_table(width, -1.0, 1.0)),
-        total,
+        late,
+        *slabs,
     )
     masks = list(range(angles))
     spectra = [spectrum] + [swap(spectrum, mask * tiles, devices) for mask in masks[1:]]
-    late, spectra[1], to_partner, to_other = lax.optimization_barrier(
-        (late, spectra[1], to_partner, to_other)
-    )
+    late, spectra[1], to_partner = lax.optimization_barrier((late, spectra[1], to_partner))
     terms = [late, swap(late, rounds[-1][min(1, len(rounds[-1]) - 1)], devices)]
-    partner, other = exchange(to_partner, to_other, tiles)
+    partner = swap_pairs(to_partner, 0, tiles)
     probe_mine = call(
         last_probe_kernel,
         "probe_last",
@@ -684,31 +725,31 @@
     probe_theirs = swap(probe_mine, tiles, devices)
     scale = 1.0 / (angles * tiles * width)
     group = max(size for size in (1, 2, 4, 10) if depth % size == 0)
-    tomo, token = call(
+    last = (base, partner, other, probe_mine, probe_theirs)
+    tomo, psi_new, probe_new = call(
         functools.partial(inverse_kernel, depth, masks),
         "slab_image",
-        [shape(2, depth, beam, tiles * width, dtype=BF16), shape(8, width)],
-        [VMEM] * (3 + angles) + [ANY],
+        [
+            shape(2, depth, beam, tiles * width, dtype=BF16),
+            shape(2, 1, rows_total, width),
+            shape(2, side, side),
+        ],
+        [VMEM] * (3 + angles + len(last)),
         [],
         depth * tiles * beam * 2 * 6 * width * 2 * width,
         grid=(depth // group,),
         out_specs=[
             pl.BlockSpec((2, group, beam, tiles * width), lambda row: (0, row, 0, 0)),
-            pl.BlockSpec((8, width), lambda row: (0, 0)),
+            pl.BlockSpec((2, 1, rows_total, width), lambda row: (0, 0, 0, 0)),
+            pl.BlockSpec((2, side, side), lambda row: (0, 0, 0)),
         ],
     )(
         phases,
         jnp.asarray(twiddles(tiles, width, 1.0, scale)),
         jnp.asarray(right_table(width, 1.0, 1.0)),
         *spectra,
-        probe_mine,
+        *last,
     )
-    psi_new, probe_new = call(
-        finish_kernel,
-        "field_probe",
-        [shape(2, 1, rows_total, width), shape(2, side, side)],
-        [VMEM] * 5 + [ANY],
-    )(base, partner, other, probe_mine, probe_theirs, token)
     return psi_new, probe_new, tomo
 
 

time: 81.5 us -> 79.6 us (0.977)
  starting transfers between devices: 31.5 us -> 33.6 us
  waiting for transfers between devices: 23.7 us -> 21.6 us
  Pallas kernels: 23.7 us -> 22 us
    all_to_all x1 -> x0, starting transfers between devices: 4.17 us -> none  [shards(): slabs = lax.all_to_all(slabs, 'tile', 0, 0, tiled=True)]
    ppermute x6, starting transfers between devices: 7.66 us -> 11.6 us  [swap_pairs(): lax.ppermute(array, 'tile', [(i, i + 1) for i in low] + [(i + 1, i) for i...]
    ppermute x18 -> x22, starting transfers between devices: 19.7 us -> 22 us  [swap(): lax.ppermute(array, ('angle', 'tile'), [(i, i ^ mask) for i in range(devi...]
    pallas_call x3, Pallas kernels: 7.64 us -> 6.08 us  [the longest x1 5.77 us: shards(): call(second_kernel, 'ptycho_second', [shape(*block), flat, flat] + [shape...]
    ppermute x18 -> x22, waiting for transfers between devices: 22.3 us -> 20.8 us  [swap(): lax.ppermute(array, ('angle', 'tile'), [(i, i ^ mask) for i in range(devi...]
    all_to_all x1 -> x0, waiting for transfers between devices: 1.34 us -> none  [shards(): slabs = lax.all_to_all(slabs, 'tile', 0, 0, tiled=True)]
  transfers between devices with their start and end apart: 25 -> 28, of which waited for: 12 -> 11; matrix products, arithmetic and copies ran while one was open for 0% -> 0% of each run, Pallas kernels for 11% -> 3%
where the time goes in v4:
time: 79.6 us; the launch traced here: 79.3 us
  starting transfers between devices  33.6 us (42%)
  Pallas kernels  22 us (28%)
  waiting for transfers between devices  21.6 us (27%)
  between operations  2.2 us (3%)
    ppermute x22, starting transfers between devices, swap(): lax.ppermute(array, ('angle', 'tile'), [(i, i ^ mask) for i in range(devi...  22 us
    ppermute x22, waiting for transfers between devices, swap(): lax.ppermute(array, ('angle', 'tile'), [(i, i ^ mask) for i in range(devi...  20.8 us
    ppermute x6, starting transfers between devices, swap_pairs(): lax.ppermute(array, 'tile', [(i, i + 1) for i in low] + [(i + 1, i) for i...  11.6 us
    pallas_call x1, Pallas kernels, shards(): call(functools.partial(inverse_kernel, depth, masks), 'slab_image', [shap...  6.49 us
    pallas_call x1, Pallas kernels, shards(): call(second_kernel, 'ptycho_second', [shape(*block), flat, flat] + [shape...  5.77 us
    pallas_call x1, Pallas kernels, shards(): call(first_kernel, 'ptycho_first', [shape(*block)] * 4 + [half] * 2, [HBM...  5.64 us
    pallas_call x1, Pallas kernels, shards(): call(stage_kernel, 'stage_operands', [pltpu.VMEM(x.shape, x.dtype) for x...  1.89 us
  transfers between devices with their start and end apart: 28, of which 11 were waited for; matrix products, arithmetic and copies ran while one was open for 0% of the time, Pallas kernels for 3%

profile of v4, /device:TPU:0, one launch (start us, length us, event | category | flops | bytes accessed | tf_op | source)
XLA Modules:
  0.0 79.3 jit_solution(11749329095307534596)
XLA Ops:
  0.6 1.0 %psi_pack.1 = (f32[160,128]{1,0:T(8,128)S(1)}, f32[160,128]{1,0:T(8,128)S(1)}) custom-call(f32[2,1,160,128]{3,2,1,0:T(8,128)} %psi.1), custom_call_target="tpu_custom_call" | custom-call | tf_op jit(solution)/shard_map/psi_pack/pallas_call | solution.py:608
  1.7 3.0 %collective-permute-start = (f32[160,128]{1,0:T(8,128)S(1)}, f32[160,128]{1,0:T(8,128)S(1)}, u32[]{:S(2)}, u32[]{:S(2)}) collective-permute-start(f32[160,128]{1,0:T(8,128)S(1)} %get-tuple-element.43), channel_id=1, source_target_pairs={{0,1},{2,3},{4,5},{6,7},{1,0},{3,2},{5,4},{7,6},{8,9},{10,11},{12,... | collective-permute-start | bytes 245768 | tf_op jit(solution)/shard_map/ppermute | solution.py:556
  4.7 0.7 collective-permute-start.1
  6.6 1.9 %stage_operands.1 = (f32[2,1,160,128]{3,2,1,0:T(8,128)S(1)}, f32[2,1,160,128]{3,2,1,0:T(8,128)S(1)}, f32[2,128,128]{2,1,0:T(8,128)S(1)}, f32[1,1,16,128,128]{4,3...) custom-call(f32[2,1,160,128]{3,2,1,0:T(8,128)} %psi.1, ...), custom_call_target="tpu_custom_call" | custom-call | bytes 3000000 | tf_op jit(solution)/shard_map/stage_operands/pallas_call | solution.py:620
  8.5 0.0 collective-permute-done.partner
  8.6 5.6 %ptycho_first.1 = (f32[2,160,128]{2,1,0:T(8,128)S(1)}, f32[2,160,128]{2,1,0:T(8,128)S(1)}, f32[2,160,128]{2,1,0:T(8,128)S(1)}, f32[2,160,128]{2,1,0:T(8,128)S(1)...) custom-call(s32[1,1,16]{2,1,0:T(1,128)} %pos_z.3, s32[1,1,16]{2,1,0:T(1,128)} %pos_x.3, s32[1,1]{1,0:T(1,128)S(6)} %copy.19.counts, ...), custom_call_target="tpu_custom_call" | custom-call | flops 3221225472 | tf_op jit(solution)/shard_map/ptycho_first/pallas_call | solution.py:634
  14.2 0.1 collective-permute-start.2
  14.3 1.2 %collective-permute-done.2.refs_1_ = f32[136,128]{1,0:T(8,128)S(1)} collective-permute-done((f32[136,128]{1,0:T(8,128)S(1)}, f32[136,128]{1,0:T(8,128)S(1)}, u32[]{:S(2)}, u32[]{:S(2)}) %collective-permute-start.2) | collective-permute-done | bytes 69664 | tf_op jit(solution)/shard_map/ppermute | solution.py:568
  15.5 5.3 %collective-permute-start.5 = (f32[136,128]{1,0:T(8,128)S(1)}, f32[136,128]{1,0:T(8,128)S(1)}, u32[]{:S(2)}, u32[]{:S(2)}) collective-permute-start(f32[136,128]{1,0:T(8,128)S(1)} %probe_sum.5.refs_0_), channel_id=1, source_target_pairs={{0,17},{1,16},{2,19},{3,18},{4,21},{5,20},{6,23},{7,22},{8,25},{9,... | collective-permute-start | bytes 208904 | tf_op jit(solution)/shard_map/ppermute | solution.py:568
  20.9 0.6 collective-permute-start.3
  21.5 1.9 %collective-permute-start.9 = (f32[2,160,128]{2,1,0:T(8,128)S(1)}, f32[2,160,128]{2,1,0:T(8,128)S(1)}, u32[]{:S(2)}, u32[]{:S(2)}) collective-permute-start(f32[2,160,128]{2,1,0:T(8,128)S(1)} %get-tuple-element.55), channel_id=1, source_target_pairs={{0,1},{2,3},{4,5},{6,7},{1,0},{3,2},{5,4},{7,6},{8,9},{10,11},{12,... | collective-permute-start | bytes 491528 | tf_op jit(solution)/shard_map/ppermute | solution.py:556
  23.4 0.7 collective-permute-start.10
  24.1 1.9 %collective-permute-done.4.refs_2_ = f32[136,128]{1,0:T(8,128)S(1)} collective-permute-done((f32[136,128]{1,0:T(8,128)S(1)}, f32[136,128]{1,0:T(8,128)S(1)}, u32[]{:S(2)}, u32[]{:S(2)}) %collective-permute-start.4) | collective-permute-done | bytes 69664 | tf_op jit(solution)/shard_map/ppermute | solution.py:568
  25.9 0.0 collective-permute-done.3.refs_1_
  26.0 4.1 %collective-permute-start.8 = (f32[136,128]{1,0:T(8,128)S(1)}, f32[136,128]{1,0:T(8,128)S(1)}, u32[]{:S(2)}, u32[]{:S(2)}) collective-permute-start(f32[136,128]{1,0:T(8,128)S(1)} %probe_sum.6.refs_0_), channel_id=1, source_target_pairs={{0,6},{1,7},{2,4},{3,5},{4,2},{5,3},{6,0},{7,1},{8,14},{9,15},{10,... | collective-permute-start | bytes 208904 | tf_op jit(solution)/shard_map/ppermute | solution.py:568
  30.1 0.0 collective-permute-start.7
  30.1 0.6 collective-permute-start.6
  30.7 5.4 %collective-permute-done.8.refs_3_ = f32[136,128]{1,0:T(8,128)S(1)} collective-permute-done((f32[136,128]{1,0:T(8,128)S(1)}, f32[136,128]{1,0:T(8,128)S(1)}, u32[]{:S(2)}, u32[]{:S(2)}) %collective-permute-start.8) | collective-permute-done | bytes 69664 | tf_op jit(solution)/shard_map/ppermute | solution.py:568
  36.1 1.9 %collective-permute-done.7.refs_2_ = f32[136,128]{1,0:T(8,128)S(1)} collective-permute-done((f32[136,128]{1,0:T(8,128)S(1)}, f32[136,128]{1,0:T(8,128)S(1)}, u32[]{:S(2)}, u32[]{:S(2)}) %collective-permute-start.7) | collective-permute-done | bytes 69664 | tf_op jit(solution)/shard_map/ppermute | solution.py:568
  38.0 0.1 collective-permute-start.11
  38.1 0.7 phase_table.1.rest_4_.phases
  38.8 0.0 collective-permute-done.10.other
  38.8 0.5 collective-permute-done.11.probe_theirs
  39.3 5.8 %ptycho_second.1 = (f32[2,160,128]{2,1,0:T(8,128)S(1)}, f32[160,128]{1,0:T(8,128)S(1)}, f32[160,128]{1,0:T(8,128)S(1)}, f32[128,128]{1,0:T(8,128)S(1)}, f32[128,...) custom-call(s32[1,1,16]{2,1,0:T(1,128)} %pos_z.3, s32[1,1,16]{2,1,0:T(1,128)} %pos_x.3, ...), custom_call_target="tpu_custom_call" | custom-call | flops 3221225472 | tf_op jit(solution)/shard_map/ptycho_second/pallas_call | solution.py:675
  45.1 0.1 collective-permute-start.17
  45.2 0.2 collective-permute-start.12
  45.4 1.1 %collective-permute-done.12.refs_1_ = f32[128,128]{1,0:T(8,128)S(1)} collective-permute-done((f32[128,128]{1,0:T(8,128)S(1)}, f32[128,128]{1,0:T(8,128)S(1)}, u32[]{:S(2)}, u32[]{:S(2)}) %collective-permute-start.12) | collective-permute-done | bytes 65568 | tf_op jit(solution)/shard_map/ppermute | solution.py:568
  46.5 3.0 %collective-permute-start.15 = (f32[128,128]{1,0:T(8,128)S(1)}, f32[128,128]{1,0:T(8,128)S(1)}, u32[]{:S(2)}, u32[]{:S(2)}) collective-permute-start(f32[128,128]{1,0:T(8,128)S(1)} %probe_sum.7.refs_0_), channel_id=1, source_target_pairs={{0,17},{1,16},{2,19},{3,18},{4,21},{5,20},{6,23},{7,22},{8,25},{9,... | collective-permute-start | bytes 196616 | tf_op jit(solution)/shard_map/ppermute | solution.py:568
  49.5 0.1 collective-permute-start.14
  49.6 0.6 collective-permute-start.13
  50.2 2.0 %collective-permute-done.17.refs_1_ = f32[4,80,128]{2,1,0:T(8,128)S(1)} collective-permute-done((f32[4,80,128]{2,1,0:T(8,128)S(1)}, f32[4,80,128]{2,1,0:T(8,128)S(1)}, u32[]{:S(2)}, u32[]{:S(2)}) %collective-permute-start.17) | collective-permute-done | bytes 163872 | tf_op jit(solution)/shard_map/ppermute | solution.py:568
  52.2 0.1 collective-permute-start.18
  52.3 1.8 %collective-permute-start.19 = (f32[2,80,128]{2,1,0:T(8,128)S(1)}, f32[2,80,128]{2,1,0:T(8,128)S(1)}, u32[]{:S(2)}, u32[]{:S(2)}) collective-permute-start(f32[2,80,128]{2,1,0:T(8,128)S(1)} %get-tuple-element.66), channel_id=1, source_target_pairs={{0,4},{1,5},{2,6},{3,7},{4,0},{5,1},{6,2},{7,3},{8,12},{9,13},{10,... | collective-permute-start | bytes 245768 | tf_op jit(solution)/shard_map/ppermute | solution.py:568
  54.1 0.5 collective-permute-done.15.refs_3_
  54.6 2.1 %collective-permute-start.20 = (f32[2,80,128]{2,1,0:T(8,128)S(1)}, f32[2,80,128]{2,1,0:T(8,128)S(1)}, u32[]{:S(2)}, u32[]{:S(2)}) collective-permute-start(f32[2,80,128]{2,1,0:T(8,128)S(1)} %get-tuple-element.67), channel_id=1, source_target_pairs={{0,6},{1,7},{2,4},{3,5},{4,2},{5,3},{6,0},{7,1},{8,14},{9,15},{10,... | collective-permute-start | bytes 245768 | tf_op jit(solution)/shard_map/ppermute | solution.py:568
  56.7 0.1 collective-permute-start.16
  56.8 4.8 %collective-permute-done.16.refs_1_ = f32[128,128]{1,0:T(8,128)S(1)} collective-permute-done((f32[128,128]{1,0:T(8,128)S(1)}, f32[128,128]{1,0:T(8,128)S(1)}, u32[]{:S(2)}, u32[]{:S(2)}) %collective-permute-start.16) | collective-permute-done | bytes 65568 | tf_op jit(solution)/shard_map/ppermute | solution.py:568
  61.7 0.3 slab_spectrum.1.rest_0_
  61.9 0.1 collective-permute-start.21
  62.0 1.4 %collective-permute-start.23 = (f32[320,128]{1,0:T(8,128)S(1)}, f32[320,128]{1,0:T(8,128)S(1)}, u32[]{:S(2)}, u32[]{:S(2)}) collective-permute-start(f32[320,128]{1,0:T(8,128)S(1)} %slab_spectrum.1.rest_0_), channel_id=1, source_target_pairs={{0,24},{1,25},{2,26},{3,27},{4,28},{5,29},{6,30},{7,31},{8,16},{9,... | collective-permute-start | bytes 491528 | tf_op jit(solution)/shard_map/ppermute | solution.py:568
  63.4 0.7 collective-permute-start.22
  64.2 0.9 %collective-permute-start.26 = (f32[128,128]{1,0:T(8,128)S(1)}, f32[128,128]{1,0:T(8,128)S(1)}, u32[]{:S(2)}, u32[]{:S(2)}) collective-permute-start(f32[128,128]{1,0:T(8,128)S(1)} %probe_sum.9._.refs_0_), channel_id=1, source_target_pairs={{0,4},{1,5},{2,6},{3,7},{4,0},{5,1},{6,2},{7,3},{8,12},{9,13},{10,... | collective-permute-start | bytes 196616 | tf_op jit(solution)/shard_map/ppermute | solution.py:568
  65.0 0.8 %collective-permute-start.25 = (f32[160,128]{1,0:T(8,128)S(1)}, f32[160,128]{1,0:T(8,128)S(1)}, u32[]{:S(2)}, u32[]{:S(2)}) collective-permute-start(f32[160,128]{1,0:T(8,128)S(1)} %get-tuple-element.72), channel_id=1, source_target_pairs={{1,2},{3,4},{5,6},{2,1},{4,3},{6,5},{9,10},{11,12},{13,14},{10,9},... | collective-permute-start | bytes 245768 | tf_op jit(solution)/shard_map/ppermute | solution.py:556
  65.9 4.5 %collective-permute-start.24 = (f32[160,128]{1,0:T(8,128)S(1)}, f32[160,128]{1,0:T(8,128)S(1)}, u32[]{:S(2)}, u32[]{:S(2)}) collective-permute-start(f32[160,128]{1,0:T(8,128)S(1)} %get-tuple-element.71), channel_id=1, source_target_pairs={{0,1},{2,3},{4,5},{6,7},{1,0},{3,2},{5,4},{7,6},{8,9},{10,11},{12,... | collective-permute-start | bytes 245768 | tf_op jit(solution)/shard_map/ppermute | solution.py:556
  70.4 0.1 collective-permute-start.27
  70.5 1.6 %collective-permute-done.22.rest_2_ = f32[320,128]{1,0:T(8,128)S(1)} collective-permute-done((f32[320,128]{1,0:T(8,128)S(1)}, f32[320,128]{1,0:T(8,128)S(1)}, u32[]{:S(2)}, u32[]{:S(2)}) %collective-permute-start.22) | collective-permute-done | bytes 163872 | tf_op jit(solution)/shard_map/ppermute | solution.py:568
  72.1 0.7 collective-permute-done.24.rest_5_
  72.9 6.5 %slab_image.1 = (bf16[2,20,32,1024]{3,2,1,0:T(8,128)(2,1)}, f32[2,1,160,128]{3,2,1,0:T(8,128)}, f32[2,128,128]{2,1,0:T(8,128)}) custom-call(f32[4,3,8,32,128]{4,3,2,1,0:T(8,128)S(1)} %phase_table.1.rest_4_.phases, f32[2,8,128]{2,1,0:T(8,128)S(1)} %copy-done.3, bf16[768,256]{1,0:T(8,128)(2,1)S(1)} %copy-done.2, f32[320,128]{1,0:T(8,128)S(1)} %slab_spectrum.1.rest_0_, ...), custom_call_target="tpu_custom_call" | custom-call | flops 2013265920 | tf_op jit(solution)/shard_map/slab_image/pallas_call | solution.py:729
  (31 shorter events, 0.2 us)
Async XLA Ops:
  1.7 6.9 %collective-permute-start = (f32[160,128]{1,0:T(8,128)S(1)}, f32[160,128]{1,0:T(8,128)S(1)}, u32[]{:S(2)}, u32[]{:S(2)}) collective-permute-start(f32[160,128]{1,0:T(8,128)S(1)} %get-tuple-element.43), channel_id=1, source_target_pairs={{0,1},{2,3},{4,5},{6,7},{1,0},{3,2},{5,4},{7,6},{8,9},{10,11},{12,... | collective-permute-start | bytes 245768 | tf_op jit(solution)/shard_map/ppermute | solution.py:556
  4.7 3.9 %collective-permute-start.1 = (f32[160,128]{1,0:T(8,128)S(1)}, f32[160,128]{1,0:T(8,128)S(1)}, u32[]{:S(2)}, u32[]{:S(2)}) collective-permute-start(f32[160,128]{1,0:T(8,128)S(1)} %get-tuple-element.44), channel_id=1, source_target_pairs={{1,2},{3,4},{5,6},{2,1},{4,3},{6,5},{9,10},{11,12},{13,14},{10,9},... | collective-permute-start | bytes 245768 | tf_op jit(solution)/shard_map/ppermute | solution.py:556
  14.2 1.3 %collective-permute-start.2 = (f32[136,128]{1,0:T(8,128)S(1)}, f32[136,128]{1,0:T(8,128)S(1)}, u32[]{:S(2)}, u32[]{:S(2)}) collective-permute-start(f32[136,128]{1,0:T(8,128)S(1)} %get-tuple-element.51), channel_id=1, source_target_pairs={{0,8},{1,9},{2,10},{3,11},{4,12},{5,13},{6,14},{7,15},{8,0},{9,1},... | collective-permute-start | bytes 208904 | tf_op jit(solution)/shard_map/ppermute | solution.py:568
  15.5 8.5 %collective-permute-start.5 = (f32[136,128]{1,0:T(8,128)S(1)}, f32[136,128]{1,0:T(8,128)S(1)}, u32[]{:S(2)}, u32[]{:S(2)}) collective-permute-start(f32[136,128]{1,0:T(8,128)S(1)} %probe_sum.5.refs_0_), channel_id=1, source_target_pairs={{0,17},{1,16},{2,19},{3,18},{4,21},{5,20},{6,23},{7,22},{8,25},{9,... | collective-permute-start | bytes 208904 | tf_op jit(solution)/shard_map/ppermute | solution.py:568
  20.9 5.1 %collective-permute-start.4 = (f32[136,128]{1,0:T(8,128)S(1)}, f32[136,128]{1,0:T(8,128)S(1)}, u32[]{:S(2)}, u32[]{:S(2)}) collective-permute-start(f32[136,128]{1,0:T(8,128)S(1)} %probe_sum.5.refs_0_), channel_id=1, source_target_pairs={{0,1},{1,0},{2,3},{3,2},{4,5},{5,4},{6,7},{7,6},{8,9},{9,8},{10,11... | collective-permute-start | bytes 208904 | tf_op jit(solution)/shard_map/ppermute | solution.py:568
  20.9 5.1 %collective-permute-start.3 = (f32[136,128]{1,0:T(8,128)S(1)}, f32[136,128]{1,0:T(8,128)S(1)}, u32[]{:S(2)}, u32[]{:S(2)}) collective-permute-start(f32[136,128]{1,0:T(8,128)S(1)} %probe_sum.5.refs_0_), channel_id=1, source_target_pairs={{0,16},{1,17},{2,18},{3,19},{4,20},{5,21},{6,22},{7,23},{8,24},{9,... | collective-permute-start | bytes 208904 | tf_op jit(solution)/shard_map/ppermute | solution.py:568
  21.5 17.3 %collective-permute-start.9 = (f32[2,160,128]{2,1,0:T(8,128)S(1)}, f32[2,160,128]{2,1,0:T(8,128)S(1)}, u32[]{:S(2)}, u32[]{:S(2)}) collective-permute-start(f32[2,160,128]{2,1,0:T(8,128)S(1)} %get-tuple-element.55), channel_id=1, source_target_pairs={{0,1},{2,3},{4,5},{6,7},{1,0},{3,2},{5,4},{7,6},{8,9},{10,11},{12,... | collective-permute-start | bytes 491528 | tf_op jit(solution)/shard_map/ppermute | solution.py:556
  23.4 15.4 %collective-permute-start.10 = (f32[2,160,128]{2,1,0:T(8,128)S(1)}, f32[2,160,128]{2,1,0:T(8,128)S(1)}, u32[]{:S(2)}, u32[]{:S(2)}) collective-permute-start(f32[2,160,128]{2,1,0:T(8,128)S(1)} %get-tuple-element.56), channel_id=1, source_target_pairs={{1,2},{3,4},{5,6},{2,1},{4,3},{6,5},{9,10},{11,12},{13,14},{10,9},... | collective-permute-start | bytes 491528 | tf_op jit(solution)/shard_map/ppermute | solution.py:556
  26.0 10.1 %collective-permute-start.8 = (f32[136,128]{1,0:T(8,128)S(1)}, f32[136,128]{1,0:T(8,128)S(1)}, u32[]{:S(2)}, u32[]{:S(2)}) collective-permute-start(f32[136,128]{1,0:T(8,128)S(1)} %probe_sum.6.refs_0_), channel_id=1, source_target_pairs={{0,6},{1,7},{2,4},{3,5},{4,2},{5,3},{6,0},{7,1},{8,14},{9,15},{10,... | collective-permute-start | bytes 208904 | tf_op jit(solution)/shard_map/ppermute | solution.py:568
  30.1 7.9 %collective-permute-start.7 = (f32[136,128]{1,0:T(8,128)S(1)}, f32[136,128]{1,0:T(8,128)S(1)}, u32[]{:S(2)}, u32[]{:S(2)}) collective-permute-start(f32[136,128]{1,0:T(8,128)S(1)} %probe_sum.6.refs_0_), channel_id=1, source_target_pairs={{0,4},{1,5},{2,6},{3,7},{4,0},{5,1},{6,2},{7,3},{8,12},{9,13},{10,... | collective-permute-start | bytes 208904 | tf_op jit(solution)/shard_map/ppermute | solution.py:568
  30.1 7.9 %collective-permute-start.6 = (f32[136,128]{1,0:T(8,128)S(1)}, f32[136,128]{1,0:T(8,128)S(1)}, u32[]{:S(2)}, u32[]{:S(2)}) collective-permute-start(f32[136,128]{1,0:T(8,128)S(1)} %probe_sum.6.refs_0_), channel_id=1, source_target_pairs={{0,2},{1,3},{2,0},{3,1},{4,6},{5,7},{6,4},{7,5},{8,10},{9,11},{10,... | collective-permute-start | bytes 208904 | tf_op jit(solution)/shard_map/ppermute | solution.py:568
  38.0 1.3 %collective-permute-start.11 = (f32[128,128]{1,0:T(8,128)S(1)}, f32[128,128]{1,0:T(8,128)S(1)}, u32[]{:S(2)}, u32[]{:S(2)}) collective-permute-start(f32[128,128]{1,0:T(8,128)S(1)} %get-tuple-element.57.probe_mine), channel_id=1, source_target_pairs={{0,8},{1,9},{2,10},{3,11},{4,12},{5,13},{6,14},{7,15},{8,0},{9,1},... | collective-permute-start | bytes 196616 | tf_op jit(solution)/shard_map/ppermute | solution.py:568
  39.3 22.3 %copy-start = (bf16[768,256]{1,0:T(8,128)(2,1)S(1)}, bf16[768,256]{1,0:T(8,128)(2,1)}, u32[]{:S(2)}) copy-start(bf16[768,256]{1,0:T(8,128)(2,1)} %constant.21.clone.table) | copy-start | bytes 1179652
  39.3 22.3 %copy-start.1 = (f32[2,8,128]{2,1,0:T(8,128)S(1)}, f32[2,8,128]{2,1,0:T(8,128)}, u32[]{:S(2)}) copy-start(f32[2,8,128]{2,1,0:T(8,128)} %constant.20.clone.turn) | copy-start | bytes 24580
  39.3 33.5 %copy-start.2 = (bf16[768,256]{1,0:T(8,128)(2,1)S(1)}, bf16[768,256]{1,0:T(8,128)(2,1)}, u32[]{:S(2)}) copy-start(bf16[768,256]{1,0:T(8,128)(2,1)} %constant.23.clone.table) | copy-start | bytes 1179652
  39.3 33.5 %copy-start.3 = (f32[2,8,128]{2,1,0:T(8,128)S(1)}, f32[2,8,128]{2,1,0:T(8,128)}, u32[]{:S(2)}) copy-start(f32[2,8,128]{2,1,0:T(8,128)} %constant.22.clone.turn) | copy-start | bytes 24580
  45.1 7.1 %collective-permute-start.17 = (f32[4,80,128]{2,1,0:T(8,128)S(1)}, f32[4,80,128]{2,1,0:T(8,128)S(1)}, u32[]{:S(2)}, u32[]{:S(2)}) collective-permute-start(f32[4,80,128]{2,1,0:T(8,128)S(1)} %get-tuple-element.63), channel_id=1, source_target_pairs={{0,1},{1,0},{2,3},{3,2},{4,5},{5,4},{6,7},{7,6},{8,9},{9,8},{10,11... | collective-permute-start | bytes 491528 | tf_op jit(solution)/shard_map/ppermute | solution.py:568
  45.2 1.3 %collective-permute-start.12 = (f32[128,128]{1,0:T(8,128)S(1)}, f32[128,128]{1,0:T(8,128)S(1)}, u32[]{:S(2)}, u32[]{:S(2)}) collective-permute-start(f32[128,128]{1,0:T(8,128)S(1)} %get-tuple-element.59), channel_id=1, source_target_pairs={{0,8},{1,9},{2,10},{3,11},{4,12},{5,13},{6,14},{7,15},{8,0},{9,1},... | collective-permute-start | bytes 196616 | tf_op jit(solution)/shard_map/ppermute | solution.py:568
  46.5 8.1 %collective-permute-start.15 = (f32[128,128]{1,0:T(8,128)S(1)}, f32[128,128]{1,0:T(8,128)S(1)}, u32[]{:S(2)}, u32[]{:S(2)}) collective-permute-start(f32[128,128]{1,0:T(8,128)S(1)} %probe_sum.7.refs_0_), channel_id=1, source_target_pairs={{0,17},{1,16},{2,19},{3,18},{4,21},{5,20},{6,23},{7,22},{8,25},{9,... | collective-permute-start | bytes 196616 | tf_op jit(solution)/shard_map/ppermute | solution.py:568
  49.5 7.1 %collective-permute-start.14 = (f32[128,128]{1,0:T(8,128)S(1)}, f32[128,128]{1,0:T(8,128)S(1)}, u32[]{:S(2)}, u32[]{:S(2)}) collective-permute-start(f32[128,128]{1,0:T(8,128)S(1)} %probe_sum.7.refs_0_), channel_id=1, source_target_pairs={{0,1},{1,0},{2,3},{3,2},{4,5},{5,4},{6,7},{7,6},{8,9},{9,8},{10,11... | collective-permute-start | bytes 196616 | tf_op jit(solution)/shard_map/ppermute | solution.py:568
  49.6 7.1 %collective-permute-start.13 = (f32[128,128]{1,0:T(8,128)S(1)}, f32[128,128]{1,0:T(8,128)S(1)}, u32[]{:S(2)}, u32[]{:S(2)}) collective-permute-start(f32[128,128]{1,0:T(8,128)S(1)} %probe_sum.7.refs_0_), channel_id=1, source_target_pairs={{0,16},{1,17},{2,18},{3,19},{4,20},{5,21},{6,22},{7,23},{8,24},{9,... | collective-permute-start | bytes 196616 | tf_op jit(solution)/shard_map/ppermute | solution.py:568
  52.2 9.4 %collective-permute-start.18 = (f32[2,80,128]{2,1,0:T(8,128)S(1)}, f32[2,80,128]{2,1,0:T(8,128)S(1)}, u32[]{:S(2)}, u32[]{:S(2)}) collective-permute-start(f32[2,80,128]{2,1,0:T(8,128)S(1)} %get-tuple-element.65), channel_id=1, source_target_pairs={{0,2},{1,3},{2,0},{3,1},{4,6},{5,7},{6,4},{7,5},{8,10},{9,11},{10,... | collective-permute-start | bytes 245768 | tf_op jit(solution)/shard_map/ppermute | solution.py:568
  52.3 9.3 %collective-permute-start.19 = (f32[2,80,128]{2,1,0:T(8,128)S(1)}, f32[2,80,128]{2,1,0:T(8,128)S(1)}, u32[]{:S(2)}, u32[]{:S(2)}) collective-permute-start(f32[2,80,128]{2,1,0:T(8,128)S(1)} %get-tuple-element.66), channel_id=1, source_target_pairs={{0,4},{1,5},{2,6},{3,7},{4,0},{5,1},{6,2},{7,3},{8,12},{9,13},{10,... | collective-permute-start | bytes 245768 | tf_op jit(solution)/shard_map/ppermute | solution.py:568
  54.6 7.0 %collective-permute-start.20 = (f32[2,80,128]{2,1,0:T(8,128)S(1)}, f32[2,80,128]{2,1,0:T(8,128)S(1)}, u32[]{:S(2)}, u32[]{:S(2)}) collective-permute-start(f32[2,80,128]{2,1,0:T(8,128)S(1)} %get-tuple-element.67), channel_id=1, source_target_pairs={{0,6},{1,7},{2,4},{3,5},{4,2},{5,3},{6,0},{7,1},{8,14},{9,15},{10,... | collective-permute-start | bytes 245768 | tf_op jit(solution)/shard_map/ppermute | solution.py:568
  56.7 4.9 %collective-permute-start.16 = (f32[128,128]{1,0:T(8,128)S(1)}, f32[128,128]{1,0:T(8,128)S(1)}, u32[]{:S(2)}, u32[]{:S(2)}) collective-permute-start(f32[128,128]{1,0:T(8,128)S(1)} %probe_sum.8.refs_0_), channel_id=1, source_target_pairs={{0,2},{1,3},{2,0},{3,1},{4,6},{5,7},{6,4},{7,5},{8,10},{9,11},{10,... | collective-permute-start | bytes 196616 | tf_op jit(solution)/shard_map/ppermute | solution.py:568
  61.9 2.2 %collective-permute-start.21 = (f32[320,128]{1,0:T(8,128)S(1)}, f32[320,128]{1,0:T(8,128)S(1)}, u32[]{:S(2)}, u32[]{:S(2)}) collective-permute-start(f32[320,128]{1,0:T(8,128)S(1)} %slab_spectrum.1.rest_0_), channel_id=1, source_target_pairs={{0,8},{1,9},{2,10},{3,11},{4,12},{5,13},{6,14},{7,15},{8,0},{9,1},... | collective-permute-start | bytes 491528 | tf_op jit(solution)/shard_map/ppermute | solution.py:568
  62.0 8.5 %collective-permute-start.23 = (f32[320,128]{1,0:T(8,128)S(1)}, f32[320,128]{1,0:T(8,128)S(1)}, u32[]{:S(2)}, u32[]{:S(2)}) collective-permute-start(f32[320,128]{1,0:T(8,128)S(1)} %slab_spectrum.1.rest_0_), channel_id=1, source_target_pairs={{0,24},{1,25},{2,26},{3,27},{4,28},{5,29},{6,30},{7,31},{8,16},{9,... | collective-permute-start | bytes 491528 | tf_op jit(solution)/shard_map/ppermute | solution.py:568
  63.4 8.7 %collective-permute-start.22 = (f32[320,128]{1,0:T(8,128)S(1)}, f32[320,128]{1,0:T(8,128)S(1)}, u32[]{:S(2)}, u32[]{:S(2)}) collective-permute-start(f32[320,128]{1,0:T(8,128)S(1)} %slab_spectrum.1.rest_0_), channel_id=1, source_target_pairs={{0,16},{1,17},{2,18},{3,19},{4,20},{5,21},{6,22},{7,23},{8,24},{9,... | collective-permute-start | bytes 491528 | tf_op jit(solution)/shard_map/ppermute | solution.py:568
  64.2 6.3 %collective-permute-start.26 = (f32[128,128]{1,0:T(8,128)S(1)}, f32[128,128]{1,0:T(8,128)S(1)}, u32[]{:S(2)}, u32[]{:S(2)}) collective-permute-start(f32[128,128]{1,0:T(8,128)S(1)} %probe_sum.9._.refs_0_), channel_id=1, source_target_pairs={{0,4},{1,5},{2,6},{3,7},{4,0},{5,1},{6,2},{7,3},{8,12},{9,13},{10,... | collective-permute-start | bytes 196616 | tf_op jit(solution)/shard_map/ppermute | solution.py:568
  65.0 5.5 %collective-permute-start.25 = (f32[160,128]{1,0:T(8,128)S(1)}, f32[160,128]{1,0:T(8,128)S(1)}, u32[]{:S(2)}, u32[]{:S(2)}) collective-permute-start(f32[160,128]{1,0:T(8,128)S(1)} %get-tuple-element.72), channel_id=1, source_target_pairs={{1,2},{3,4},{5,6},{2,1},{4,3},{6,5},{9,10},{11,12},{13,14},{10,9},... | collective-permute-start | bytes 245768 | tf_op jit(solution)/shard_map/ppermute | solution.py:556
  65.9 7.0 %collective-permute-start.24 = (f32[160,128]{1,0:T(8,128)S(1)}, f32[160,128]{1,0:T(8,128)S(1)}, u32[]{:S(2)}, u32[]{:S(2)}) collective-permute-start(f32[160,128]{1,0:T(8,128)S(1)} %get-tuple-element.71), channel_id=1, source_target_pairs={{0,1},{2,3},{4,5},{6,7},{1,0},{3,2},{5,4},{7,6},{8,9},{10,11},{12,... | collective-permute-start | bytes 245768 | tf_op jit(solution)/shard_map/ppermute | solution.py:556
  70.4 2.4 %collective-permute-start.27 = (f32[128,128]{1,0:T(8,128)S(1)}, f32[128,128]{1,0:T(8,128)S(1)}, u32[]{:S(2)}, u32[]{:S(2)}) collective-permute-start(f32[128,128]{1,0:T(8,128)S(1)} %probe_last.1.rest_7_), channel_id=1, source_target_pairs={{0,8},{1,9},{2,10},{3,11},{4,12},{5,13},{6,14},{7,15},{8,0},{9,1},... | collective-permute-start | bytes 196616 | tf_op jit(solution)/shard_map/ppermute | solution.py:568

commit v5 on v4

--- a/solution.py
+++ b/solution.py
@@ -313,7 +313,7 @@
     row = lax.broadcasted_iota(jnp.int32, (8, side), 0)
     lane = lax.broadcasted_iota(jnp.int32, (8, side), 1)
     angle, tile = lax.axis_index("angle"), lax.axis_index("tile")
-    mine = (row == 1) & (lane == angle) & (tile == 0)
+    mine = (row == 1) & (lane == angle) & (tile % inner_count(lax.axis_size("tile")) == 0)
     extra = jnp.where(row == 0, count.astype(F32), jnp.where(mine, shears[0], 0.0))
     core = angle % 2
     for out, part in ((keep_out, core), (send_out, 1 - core)):
@@ -328,7 +328,7 @@
     refs[-1][...] = terms[0]
 
 
-def probe_kernel(probe, *refs):
+def probe_kernel(_, probe, *refs):
     total, probe_out, extra_out = refs[-1], refs[-3], refs[-2]
     sum_kernel(*refs[:-3], total)
     side = probe.shape[-1]
@@ -440,14 +440,14 @@
     spectrum_out[count : 2 * count] = spectrum[:, width:]
 
 
-def phase_kernel(tiles, extra, table_out):
+def phase_kernel(tiles, sums, table_out):
     angles, _, _, beam, width = table_out.shape
     total = tiles * width
     first = lax.axis_index("angle") * beam - (beam * lax.axis_size("angle")) // 2
     offsets = (lax.broadcasted_iota(jnp.int32, (beam, width), 0) + first).astype(F32)
     column = lax.broadcasted_iota(jnp.int32, (beam, width), 1)
     for angle in range(angles):
-        shear = extra[1:2, angle : angle + 1]
+        shear = sums[sums.shape[0] - 7 : sums.shape[0] - 6, angle : angle + 1]
         for block in range(tiles):
             frequency = block + tiles * column
             signed = jnp.where(frequency < total // 2, frequency, frequency - total).astype(F32)
@@ -470,17 +470,18 @@
 
 def inverse_kernel(depth, masks, phases, turn, table, *rest):
     spectra = rest[: len(masks)]
-    last, (image_out, psi_out, probe_out) = rest[len(masks) : -3], rest[-3:]
+    last, outs = rest[len(masks) : -7], rest[-7:-4]
+    (image, psi, probe), sems = rest[-4:-1], rest[-1]
     _, _, tiles, beam, width = phases.shape
     angles = [lax.axis_index("angle") ^ mask for mask in masks]
-    group = image_out.shape[1]
-
-    @pl.when(pl.program_id(0) == 0)
-    def _():
-        finish(*last, psi_out, probe_out)
-
-    wide = math.gcd(group, 2)
-    first = pl.program_id(0) * group
+    finish(*last, psi, probe)
+    copies = [
+        pltpu.make_async_copy(psi, outs[1], sems.at[0]),
+        pltpu.make_async_copy(probe, outs[2], sems.at[1]),
+    ]
+    for copy in copies:
+        copy.start()
+    wide = math.gcd(depth, 2)
     count = tiles * depth
 
     def sum_angles(start, _):
@@ -488,7 +489,7 @@
         for block in range(tiles):
             tables = [[phases[angle, which, block] for which in range(3)] for angle in angles]
             for member in range(wide):
-                at = block * depth + first + start + member
+                at = block * depth + start + member
                 sums = None
                 for spectrum, three in zip(spectra, tables):
                     real = spectrum[pl.ds(at, 1), :]
@@ -502,19 +503,25 @@
         return [dot(jnp.concatenate([high, low, high], 1), table[...]) for high, low in splits]
 
     def store(start, images):
-        for member, image in enumerate(images):
+        for member, one in enumerate(images):
             blocks = []
             for block in range(tiles):
-                real = image[block * beam : (block + 1) * beam, :width]
-                imag = image[block * beam : (block + 1) * beam, width:]
+                real = one[block * beam : (block + 1) * beam, :width]
+                imag = one[block * beam : (block + 1) * beam, width:]
                 cosine, sine = turn[0, block : block + 1], turn[1, block : block + 1]
                 blocks.append((real * cosine - imag * sine, real * sine + imag * cosine))
             for index, (real, imag) in enumerate(butterfly(blocks, 1)):
                 columns = slice(index * width, (index + 1) * width)
-                image_out[0, start + member, :, columns] = real.astype(BF16)
-                image_out[1, start + member, :, columns] = imag.astype(BF16)
-
-    side_by_side([sum_angles, transform, store], group, wide)
+                image[0, start + member, :, columns] = real.astype(BF16)
+                image[1, start + member, :, columns] = imag.astype(BF16)
+        rows = pl.ds(start, wide)
+        copy = pltpu.make_async_copy(image.at[:, rows], outs[0].at[:, rows], sems.at[2 + start // wide])
+        copy.start()
+        copies.append(copy)
+
+    side_by_side([sum_angles, transform, store], depth, wide)
+    for copy in copies:
+        copy.wait()
 
 
 def finish(base, partner, other, probe_mine, probe_theirs, psi_out, probe_out):
@@ -652,16 +659,9 @@
     def last_round(total, rounds):
         return [total] + [swap(total, mask, devices) for mask in rounds[-1]]
 
-    terms = last_round(all_but_last(keep, send, rounds), rounds)
+    nearly = all_but_last(keep, send, rounds)
+    terms = last_round(nearly, rounds)
     partner, other = exchange(to_partner, to_other, tiles)
-    probe_mine, extra = call(
-        probe_kernel,
-        "probe_step",
-        [shape(side, side), shape(8, side)],
-        [VMEM] * (1 + len(terms)),
-        [pltpu.VMEM((side + 8, side), F32)],
-    )(probe_in, *terms)
-    probe_theirs = swap(probe_mine, tiles, devices)
     phases = call(
         functools.partial(phase_kernel, tiles),
         "phase_table",
@@ -669,7 +669,15 @@
         [VMEM],
         (),
         angles * tiles * beam * width * 40,
-    )(extra)
+    )(nearly)
+    probe_mine, extra = call(
+        probe_kernel,
+        "probe_step",
+        [shape(side, side), shape(8, side)],
+        [ANY] + [VMEM] * (1 + len(terms)),
+        [pltpu.VMEM((side + 8, side), F32)],
+    )(phases, probe_in, *terms)
+    probe_theirs = swap(probe_mine, tiles, devices)
     inner = inner_count(tiles)
     outer = tiles // inner
     base, to_partner, to_other, keep, send, *slabs = call(
@@ -724,7 +732,6 @@
     )(probe_mine, extra, *terms)
     probe_theirs = swap(probe_mine, tiles, devices)
     scale = 1.0 / (angles * tiles * width)
-    group = max(size for size in (1, 2, 4, 10) if depth % size == 0)
     last = (base, partner, other, probe_mine, probe_theirs)
     tomo, psi_new, probe_new = call(
         functools.partial(inverse_kernel, depth, masks),
@@ -735,14 +742,14 @@
             shape(2, side, side),
         ],
         [VMEM] * (3 + angles + len(last)),
-        [],
+        [
+            pltpu.VMEM((2, depth, beam, tiles * width), BF16),
+            pltpu.VMEM((2, 1, rows_total, width), F32),
+            pltpu.VMEM((2, side, side), F32),
+            pltpu.SemaphoreType.DMA((2 + depth // math.gcd(depth, 2),)),
+        ],
         depth * tiles * beam * 2 * 6 * width * 2 * width,
-        grid=(depth // group,),
-        out_specs=[
-            pl.BlockSpec((2, group, beam, tiles * width), lambda row: (0, row, 0, 0)),
-            pl.BlockSpec((2, 1, rows_total, width), lambda row: (0, 0, 0, 0)),
-            pl.BlockSpec((2, side, side), lambda row: (0, 0, 0)),
-        ],
+        out_specs=[HBM] * 3,
     )(
         phases,
         jnp.asarray(twiddles(tiles, width, 1.0, scale)),

time: 79.6 us -> 79.2 us (level)
  no operation moved by 1% of the time
where the time goes in v5:
time: 79.2 us; the launch traced here: 78.9 us
  starting transfers between devices  33.6 us (42%)
  waiting for transfers between devices  21.5 us (27%)
  Pallas kernels  21.4 us (27%)
  between operations  2.36 us (3%)
    ppermute x22, starting transfers between devices, swap(): lax.ppermute(array, ('angle', 'tile'), [(i, i ^ mask) for i in range(devi...  22.2 us
    ppermute x22, waiting for transfers between devices, swap(): lax.ppermute(array, ('angle', 'tile'), [(i, i ^ mask) for i in range(devi...  20.7 us
    ppermute x6, starting transfers between devices, swap_pairs(): lax.ppermute(array, 'tile', [(i, i + 1) for i in low] + [(i + 1, i) for i...  11.4 us
    pallas_call x1, Pallas kernels, shards(): call(functools.partial(inverse_kernel, depth, masks), 'slab_image', [shap...  5.95 us
    pallas_call x1, Pallas kernels, shards(): call(second_kernel, 'ptycho_second', [shape(*block), flat, flat] + [shape...  5.78 us
    pallas_call x1, Pallas kernels, shards(): call(first_kernel, 'ptycho_first', [shape(*block)] * 4 + [half] * 2, [HBM...  5.63 us
    pallas_call x1, Pallas kernels, shards(): call(stage_kernel, 'stage_operands', [pltpu.VMEM(x.shape, x.dtype) for x...  1.89 us
  transfers between devices with their start and end apart: 28, of which 11 were waited for; matrix products, arithmetic and copies ran while one was open for 0% of the time, Pallas kernels for 3%

profile of v5, /device:TPU:0, one launch (start us, length us, event | category | flops | bytes accessed | tf_op | source)
XLA Modules:
  0.0 78.9 jit_solution(12538325380274119034)
XLA Ops:
  0.6 1.0 %psi_pack.1 = (f32[160,128]{1,0:T(8,128)S(1)}, f32[160,128]{1,0:T(8,128)S(1)}) custom-call(f32[2,1,160,128]{3,2,1,0:T(8,128)} %psi.1), custom_call_target="tpu_custom_call" | custom-call | tf_op jit(solution)/shard_map/psi_pack/pallas_call | solution.py:615
  1.7 3.0 %collective-permute-start = (f32[160,128]{1,0:T(8,128)S(1)}, f32[160,128]{1,0:T(8,128)S(1)}, u32[]{:S(2)}, u32[]{:S(2)}) collective-permute-start(f32[160,128]{1,0:T(8,128)S(1)} %get-tuple-element.42), channel_id=1, source_target_pairs={{0,1},{2,3},{4,5},{6,7},{1,0},{3,2},{5,4},{7,6},{8,9},{10,11},{12,... | collective-permute-start | bytes 245768 | tf_op jit(solution)/shard_map/ppermute | solution.py:563
  4.7 0.7 collective-permute-start.1
  6.6 1.9 %stage_operands.1 = (f32[2,1,160,128]{3,2,1,0:T(8,128)S(1)}, f32[2,1,160,128]{3,2,1,0:T(8,128)S(1)}, f32[2,128,128]{2,1,0:T(8,128)S(1)}, f32[1,1,16,128,128]{4,3...) custom-call(f32[2,1,160,128]{3,2,1,0:T(8,128)} %psi.1, ...), custom_call_target="tpu_custom_call" | custom-call | bytes 3000000 | tf_op jit(solution)/shard_map/stage_operands/pallas_call | solution.py:627
  8.5 0.0 collective-permute-done.partner
  8.5 0.0 collective-permute-done.1.other
  8.6 5.6 %ptycho_first.1 = (f32[2,160,128]{2,1,0:T(8,128)S(1)}, f32[2,160,128]{2,1,0:T(8,128)S(1)}, f32[2,160,128]{2,1,0:T(8,128)S(1)}, f32[2,160,128]{2,1,0:T(8,128)S(1)...) custom-call(s32[1,1,16]{2,1,0:T(1,128)} %pos_z.3, s32[1,1,16]{2,1,0:T(1,128)} %pos_x.3, s32[1,1]{1,0:T(1,128)S(6)} %copy.19.counts, ...), custom_call_target="tpu_custom_call" | custom-call | flops 3221225472 | tf_op jit(solution)/shard_map/ptycho_first/pallas_call | solution.py:641
  14.2 0.1 collective-permute-start.2
  14.3 1.2 %collective-permute-done.2.refs_1_ = f32[136,128]{1,0:T(8,128)S(1)} collective-permute-done((f32[136,128]{1,0:T(8,128)S(1)}, f32[136,128]{1,0:T(8,128)S(1)}, u32[]{:S(2)}, u32[]{:S(2)}) %collective-permute-start.2) | collective-permute-done | bytes 69664 | tf_op jit(solution)/shard_map/ppermute | solution.py:575
  15.5 5.3 %collective-permute-start.5 = (f32[136,128]{1,0:T(8,128)S(1)}, f32[136,128]{1,0:T(8,128)S(1)}, u32[]{:S(2)}, u32[]{:S(2)}) collective-permute-start(f32[136,128]{1,0:T(8,128)S(1)} %probe_sum.5.refs_0_), channel_id=1, source_target_pairs={{0,17},{1,16},{2,19},{3,18},{4,21},{5,20},{6,23},{7,22},{8,25},{9,... | collective-permute-start | bytes 208904 | tf_op jit(solution)/shard_map/ppermute | solution.py:575
  20.9 0.6 collective-permute-start.3
  21.5 1.9 %collective-permute-start.6 = (f32[2,160,128]{2,1,0:T(8,128)S(1)}, f32[2,160,128]{2,1,0:T(8,128)S(1)}, u32[]{:S(2)}, u32[]{:S(2)}) collective-permute-start(f32[2,160,128]{2,1,0:T(8,128)S(1)} %get-tuple-element.54), channel_id=1, source_target_pairs={{0,1},{2,3},{4,5},{6,7},{1,0},{3,2},{5,4},{7,6},{8,9},{10,11},{12,... | collective-permute-start | bytes 491528 | tf_op jit(solution)/shard_map/ppermute | solution.py:563
  23.4 0.7 collective-permute-start.7
  24.1 0.0 collective-permute-done.5.refs_3_
  24.1 1.9 %collective-permute-done.4.refs_2_ = f32[136,128]{1,0:T(8,128)S(1)} collective-permute-done((f32[136,128]{1,0:T(8,128)S(1)}, f32[136,128]{1,0:T(8,128)S(1)}, u32[]{:S(2)}, u32[]{:S(2)}) %collective-permute-start.4) | collective-permute-done | bytes 69664 | tf_op jit(solution)/shard_map/ppermute | solution.py:575
  26.0 0.0 collective-permute-done.3.refs_1_
  26.0 4.1 %collective-permute-start.10 = (f32[136,128]{1,0:T(8,128)S(1)}, f32[136,128]{1,0:T(8,128)S(1)}, u32[]{:S(2)}, u32[]{:S(2)}) collective-permute-start(f32[136,128]{1,0:T(8,128)S(1)} %probe_sum.6.sums.refs_0_), channel_id=1, source_target_pairs={{0,6},{1,7},{2,4},{3,5},{4,2},{5,3},{6,0},{7,1},{8,14},{9,15},{10,... | collective-permute-start | bytes 208904 | tf_op jit(solution)/shard_map/ppermute | solution.py:575
  30.1 0.6 collective-permute-start.8
  30.8 0.7 phase_table.1._.rest_4_.phases
  31.5 4.6 %collective-permute-done.10.refs_3_ = f32[136,128]{1,0:T(8,128)S(1)} collective-permute-done((f32[136,128]{1,0:T(8,128)S(1)}, f32[136,128]{1,0:T(8,128)S(1)}, u32[]{:S(2)}, u32[]{:S(2)}) %collective-permute-start.10) | collective-permute-done | bytes 69664 | tf_op jit(solution)/shard_map/ppermute | solution.py:575
  36.1 1.9 %collective-permute-done.9.refs_2_ = f32[136,128]{1,0:T(8,128)S(1)} collective-permute-done((f32[136,128]{1,0:T(8,128)S(1)}, f32[136,128]{1,0:T(8,128)S(1)}, u32[]{:S(2)}, u32[]{:S(2)}) %collective-permute-start.9) | collective-permute-done | bytes 69664 | tf_op jit(solution)/shard_map/ppermute | solution.py:575
  38.0 0.1 collective-permute-start.11
  38.1 1.2 %collective-permute-done.11.probe_theirs = f32[128,128]{1,0:T(8,128)S(1)} collective-permute-done((f32[128,128]{1,0:T(8,128)S(1)}, f32[128,128]{1,0:T(8,128)S(1)}, u32[]{:S(2)}, u32[]{:S(2)}) %collective-permute-start.11) | collective-permute-done | bytes 65568 | tf_op jit(solution)/shard_map/ppermute | solution.py:575
  39.3 5.8 %ptycho_second.1 = (f32[2,160,128]{2,1,0:T(8,128)S(1)}, f32[160,128]{1,0:T(8,128)S(1)}, f32[160,128]{1,0:T(8,128)S(1)}, f32[128,128]{1,0:T(8,128)S(1)}, f32[128,...) custom-call(s32[1,1,16]{2,1,0:T(1,128)} %pos_z.3, s32[1,1,16]{2,1,0:T(1,128)} %pos_x.3, ...), custom_call_target="tpu_custom_call" | custom-call | flops 3221225472 | tf_op jit(solution)/shard_map/ptycho_second/pallas_call | solution.py:683
  45.1 0.1 collective-permute-start.17
  45.2 0.2 collective-permute-start.12
  45.4 1.1 %collective-permute-done.12.refs_1_ = f32[128,128]{1,0:T(8,128)S(1)} collective-permute-done((f32[128,128]{1,0:T(8,128)S(1)}, f32[128,128]{1,0:T(8,128)S(1)}, u32[]{:S(2)}, u32[]{:S(2)}) %collective-permute-start.12) | collective-permute-done | bytes 65568 | tf_op jit(solution)/shard_map/ppermute | solution.py:575
  46.5 2.9 %collective-permute-start.15 = (f32[128,128]{1,0:T(8,128)S(1)}, f32[128,128]{1,0:T(8,128)S(1)}, u32[]{:S(2)}, u32[]{:S(2)}) collective-permute-start(f32[128,128]{1,0:T(8,128)S(1)} %probe_sum.7.refs_0_), channel_id=1, source_target_pairs={{0,17},{1,16},{2,19},{3,18},{4,21},{5,20},{6,23},{7,22},{8,25},{9,... | collective-permute-start | bytes 196616 | tf_op jit(solution)/shard_map/ppermute | solution.py:575
  49.4 0.1 collective-permute-start.14
  49.5 0.6 collective-permute-start.13
  50.1 2.1 %collective-permute-done.17.refs_1_ = f32[4,80,128]{2,1,0:T(8,128)S(1)} collective-permute-done((f32[4,80,128]{2,1,0:T(8,128)S(1)}, f32[4,80,128]{2,1,0:T(8,128)S(1)}, u32[]{:S(2)}, u32[]{:S(2)}) %collective-permute-start.17) | collective-permute-done | bytes 163872 | tf_op jit(solution)/shard_map/ppermute | solution.py:575
  52.2 0.1 collective-permute-start.18
  52.3 1.8 %collective-permute-start.19 = (f32[2,80,128]{2,1,0:T(8,128)S(1)}, f32[2,80,128]{2,1,0:T(8,128)S(1)}, u32[]{:S(2)}, u32[]{:S(2)}) collective-permute-start(f32[2,80,128]{2,1,0:T(8,128)S(1)} %get-tuple-element.65), channel_id=1, source_target_pairs={{0,4},{1,5},{2,6},{3,7},{4,0},{5,1},{6,2},{7,3},{8,12},{9,13},{10,... | collective-permute-start | bytes 245768 | tf_op jit(solution)/shard_map/ppermute | solution.py:575
  54.1 0.4 collective-permute-done.15.refs_3_
  54.5 2.2 %collective-permute-start.20 = (f32[2,80,128]{2,1,0:T(8,128)S(1)}, f32[2,80,128]{2,1,0:T(8,128)S(1)}, u32[]{:S(2)}, u32[]{:S(2)}) collective-permute-start(f32[2,80,128]{2,1,0:T(8,128)S(1)} %get-tuple-element.66), channel_id=1, source_target_pairs={{0,6},{1,7},{2,4},{3,5},{4,2},{5,3},{6,0},{7,1},{8,14},{9,15},{10,... | collective-permute-start | bytes 245768 | tf_op jit(solution)/shard_map/ppermute | solution.py:575
  56.7 0.1 collective-permute-start.16
  56.8 4.7 %collective-permute-done.16.refs_1_ = f32[128,128]{1,0:T(8,128)S(1)} collective-permute-done((f32[128,128]{1,0:T(8,128)S(1)}, f32[128,128]{1,0:T(8,128)S(1)}, u32[]{:S(2)}, u32[]{:S(2)}) %collective-permute-start.16) | collective-permute-done | bytes 65568 | tf_op jit(solution)/shard_map/ppermute | solution.py:575
  61.6 0.3 slab_spectrum.1.rest_0_
  61.8 0.1 collective-permute-start.21
  61.9 1.5 %collective-permute-start.23 = (f32[320,128]{1,0:T(8,128)S(1)}, f32[320,128]{1,0:T(8,128)S(1)}, u32[]{:S(2)}, u32[]{:S(2)}) collective-permute-start(f32[320,128]{1,0:T(8,128)S(1)} %slab_spectrum.1.rest_0_), channel_id=1, source_target_pairs={{0,24},{1,25},{2,26},{3,27},{4,28},{5,29},{6,30},{7,31},{8,16},{9,... | collective-permute-start | bytes 491528 | tf_op jit(solution)/shard_map/ppermute | solution.py:575
  63.4 0.6 collective-permute-start.22
  64.1 1.0 %collective-permute-start.26 = (f32[128,128]{1,0:T(8,128)S(1)}, f32[128,128]{1,0:T(8,128)S(1)}, u32[]{:S(2)}, u32[]{:S(2)}) collective-permute-start(f32[128,128]{1,0:T(8,128)S(1)} %probe_sum.9._.refs_0_), channel_id=1, source_target_pairs={{0,4},{1,5},{2,6},{3,7},{4,0},{5,1},{6,2},{7,3},{8,12},{9,13},{10,... | collective-permute-start | bytes 196616 | tf_op jit(solution)/shard_map/ppermute | solution.py:575
  65.1 0.8 %collective-permute-start.25 = (f32[160,128]{1,0:T(8,128)S(1)}, f32[160,128]{1,0:T(8,128)S(1)}, u32[]{:S(2)}, u32[]{:S(2)}) collective-permute-start(f32[160,128]{1,0:T(8,128)S(1)} %get-tuple-element.71), channel_id=1, source_target_pairs={{1,2},{3,4},{5,6},{2,1},{4,3},{6,5},{9,10},{11,12},{13,14},{10,9},... | collective-permute-start | bytes 245768 | tf_op jit(solution)/shard_map/ppermute | solution.py:563
  65.9 4.4 %collective-permute-start.24 = (f32[160,128]{1,0:T(8,128)S(1)}, f32[160,128]{1,0:T(8,128)S(1)}, u32[]{:S(2)}, u32[]{:S(2)}) collective-permute-start(f32[160,128]{1,0:T(8,128)S(1)} %get-tuple-element.70), channel_id=1, source_target_pairs={{0,1},{2,3},{4,5},{6,7},{1,0},{3,2},{5,4},{7,6},{8,9},{10,11},{12,... | collective-permute-start | bytes 245768 | tf_op jit(solution)/shard_map/ppermute | solution.py:563
  70.3 0.1 collective-permute-start.27
  70.4 1.6 %collective-permute-done.22.rest_2_ = f32[320,128]{1,0:T(8,128)S(1)} collective-permute-done((f32[320,128]{1,0:T(8,128)S(1)}, f32[320,128]{1,0:T(8,128)S(1)}, u32[]{:S(2)}, u32[]{:S(2)}) %collective-permute-start.22) | collective-permute-done | bytes 163872 | tf_op jit(solution)/shard_map/ppermute | solution.py:575
  72.0 0.7 collective-permute-done.24.rest_5_
  72.7 5.9 %slab_image.1 = (bf16[2,20,32,1024]{3,2,1,0:T(8,128)(2,1)}, f32[2,1,160,128]{3,2,1,0:T(8,128)}, f32[2,128,128]{2,1,0:T(8,128)}) custom-call(f32[4,3,8,32,128]{4,3,2,1,0:T(8,128)S(1)} %phase_table.1._.rest_4_.phases, f32[2,8,128]{2,1,0:T(8,128)S(1)} %copy-done.3, bf16[768,256]{1,0:T(8,128)(2,1)S(1)} %copy-done.2, f32[320,128]{1,0:T(8,128)S(1)} %slab_spectrum.1.rest_0_, ...), custom_call_target="tpu_custom_call" | custom-call | flops 2013265920 | tf_op jit(solution)/shard_map/slab_image/pallas_call | solution.py:736
  (31 shorter events, 0.2 us)
Async XLA Ops:
  1.7 6.9 %collective-permute-start = (f32[160,128]{1,0:T(8,128)S(1)}, f32[160,128]{1,0:T(8,128)S(1)}, u32[]{:S(2)}, u32[]{:S(2)}) collective-permute-start(f32[160,128]{1,0:T(8,128)S(1)} %get-tuple-element.42), channel_id=1, source_target_pairs={{0,1},{2,3},{4,5},{6,7},{1,0},{3,2},{5,4},{7,6},{8,9},{10,11},{12,... | collective-permute-start | bytes 245768 | tf_op jit(solution)/shard_map/ppermute | solution.py:563
  4.7 3.9 %collective-permute-start.1 = (f32[160,128]{1,0:T(8,128)S(1)}, f32[160,128]{1,0:T(8,128)S(1)}, u32[]{:S(2)}, u32[]{:S(2)}) collective-permute-start(f32[160,128]{1,0:T(8,128)S(1)} %get-tuple-element.43), channel_id=1, source_target_pairs={{1,2},{3,4},{5,6},{2,1},{4,3},{6,5},{9,10},{11,12},{13,14},{10,9},... | collective-permute-start | bytes 245768 | tf_op jit(solution)/shard_map/ppermute | solution.py:563
  14.2 1.3 %collective-permute-start.2 = (f32[136,128]{1,0:T(8,128)S(1)}, f32[136,128]{1,0:T(8,128)S(1)}, u32[]{:S(2)}, u32[]{:S(2)}) collective-permute-start(f32[136,128]{1,0:T(8,128)S(1)} %get-tuple-element.51), channel_id=1, source_target_pairs={{0,8},{1,9},{2,10},{3,11},{4,12},{5,13},{6,14},{7,15},{8,0},{9,1},... | collective-permute-start | bytes 208904 | tf_op jit(solution)/shard_map/ppermute | solution.py:575
  15.5 8.5 %collective-permute-start.5 = (f32[136,128]{1,0:T(8,128)S(1)}, f32[136,128]{1,0:T(8,128)S(1)}, u32[]{:S(2)}, u32[]{:S(2)}) collective-permute-start(f32[136,128]{1,0:T(8,128)S(1)} %probe_sum.5.refs_0_), channel_id=1, source_target_pairs={{0,17},{1,16},{2,19},{3,18},{4,21},{5,20},{6,23},{7,22},{8,25},{9,... | collective-permute-start | bytes 208904 | tf_op jit(solution)/shard_map/ppermute | solution.py:575
  20.9 5.1 %collective-permute-start.4 = (f32[136,128]{1,0:T(8,128)S(1)}, f32[136,128]{1,0:T(8,128)S(1)}, u32[]{:S(2)}, u32[]{:S(2)}) collective-permute-start(f32[136,128]{1,0:T(8,128)S(1)} %probe_sum.5.refs_0_), channel_id=1, source_target_pairs={{0,1},{1,0},{2,3},{3,2},{4,5},{5,4},{6,7},{7,6},{8,9},{9,8},{10,11... | collective-permute-start | bytes 208904 | tf_op jit(solution)/shard_map/ppermute | solution.py:575
  20.9 5.1 %collective-permute-start.3 = (f32[136,128]{1,0:T(8,128)S(1)}, f32[136,128]{1,0:T(8,128)S(1)}, u32[]{:S(2)}, u32[]{:S(2)}) collective-permute-start(f32[136,128]{1,0:T(8,128)S(1)} %probe_sum.5.refs_0_), channel_id=1, source_target_pairs={{0,16},{1,17},{2,18},{3,19},{4,20},{5,21},{6,22},{7,23},{8,24},{9,... | collective-permute-start | bytes 208904 | tf_op jit(solution)/shard_map/ppermute | solution.py:575
  21.5 16.5 %collective-permute-start.6 = (f32[2,160,128]{2,1,0:T(8,128)S(1)}, f32[2,160,128]{2,1,0:T(8,128)S(1)}, u32[]{:S(2)}, u32[]{:S(2)}) collective-permute-start(f32[2,160,128]{2,1,0:T(8,128)S(1)} %get-tuple-element.54), channel_id=1, source_target_pairs={{0,1},{2,3},{4,5},{6,7},{1,0},{3,2},{5,4},{7,6},{8,9},{10,11},{12,... | collective-permute-start | bytes 491528 | tf_op jit(solution)/shard_map/ppermute | solution.py:563
  23.4 14.7 %collective-permute-start.7 = (f32[2,160,128]{2,1,0:T(8,128)S(1)}, f32[2,160,128]{2,1,0:T(8,128)S(1)}, u32[]{:S(2)}, u32[]{:S(2)}) collective-permute-start(f32[2,160,128]{2,1,0:T(8,128)S(1)} %get-tuple-element.55), channel_id=1, source_target_pairs={{1,2},{3,4},{5,6},{2,1},{4,3},{6,5},{9,10},{11,12},{13,14},{10,9},... | collective-permute-start | bytes 491528 | tf_op jit(solution)/shard_map/ppermute | solution.py:563
  26.0 10.1 %collective-permute-start.10 = (f32[136,128]{1,0:T(8,128)S(1)}, f32[136,128]{1,0:T(8,128)S(1)}, u32[]{:S(2)}, u32[]{:S(2)}) collective-permute-start(f32[136,128]{1,0:T(8,128)S(1)} %probe_sum.6.sums.refs_0_), channel_id=1, source_target_pairs={{0,6},{1,7},{2,4},{3,5},{4,2},{5,3},{6,0},{7,1},{8,14},{9,15},{10,... | collective-permute-start | bytes 208904 | tf_op jit(solution)/shard_map/ppermute | solution.py:575
  30.1 7.8 %collective-permute-start.9 = (f32[136,128]{1,0:T(8,128)S(1)}, f32[136,128]{1,0:T(8,128)S(1)}, u32[]{:S(2)}, u32[]{:S(2)}) collective-permute-start(f32[136,128]{1,0:T(8,128)S(1)} %probe_sum.6.sums.refs_0_), channel_id=1, source_target_pairs={{0,4},{1,5},{2,6},{3,7},{4,0},{5,1},{6,2},{7,3},{8,12},{9,13},{10,... | collective-permute-start | bytes 208904 | tf_op jit(solution)/shard_map/ppermute | solution.py:575
  30.1 7.8 %collective-permute-start.8 = (f32[136,128]{1,0:T(8,128)S(1)}, f32[136,128]{1,0:T(8,128)S(1)}, u32[]{:S(2)}, u32[]{:S(2)}) collective-permute-start(f32[136,128]{1,0:T(8,128)S(1)} %probe_sum.6.sums.refs_0_), channel_id=1, source_target_pairs={{0,2},{1,3},{2,0},{3,1},{4,6},{5,7},{6,4},{7,5},{8,10},{9,11},{10,... | collective-permute-start | bytes 208904 | tf_op jit(solution)/shard_map/ppermute | solution.py:575
  38.0 1.3 %collective-permute-start.11 = (f32[128,128]{1,0:T(8,128)S(1)}, f32[128,128]{1,0:T(8,128)S(1)}, u32[]{:S(2)}, u32[]{:S(2)}) collective-permute-start(f32[128,128]{1,0:T(8,128)S(1)} %get-tuple-element.56.probe_mine), channel_id=1, source_target_pairs={{0,8},{1,9},{2,10},{3,11},{4,12},{5,13},{6,14},{7,15},{8,0},{9,1},... | collective-permute-start | bytes 196616 | tf_op jit(solution)/shard_map/ppermute | solution.py:575
  39.3 22.2 %copy-start = (bf16[768,256]{1,0:T(8,128)(2,1)S(1)}, bf16[768,256]{1,0:T(8,128)(2,1)}, u32[]{:S(2)}) copy-start(bf16[768,256]{1,0:T(8,128)(2,1)} %constant.21.clone.table) | copy-start | bytes 1179652
  39.3 22.2 %copy-start.1 = (f32[2,8,128]{2,1,0:T(8,128)S(1)}, f32[2,8,128]{2,1,0:T(8,128)}, u32[]{:S(2)}) copy-start(f32[2,8,128]{2,1,0:T(8,128)} %constant.20.clone.turn) | copy-start | bytes 24580
  39.3 33.4 %copy-start.2 = (bf16[768,256]{1,0:T(8,128)(2,1)S(1)}, bf16[768,256]{1,0:T(8,128)(2,1)}, u32[]{:S(2)}) copy-start(bf16[768,256]{1,0:T(8,128)(2,1)} %constant.23.clone.table) | copy-start | bytes 1179652
  39.3 33.4 %copy-start.3 = (f32[2,8,128]{2,1,0:T(8,128)S(1)}, f32[2,8,128]{2,1,0:T(8,128)}, u32[]{:S(2)}) copy-start(f32[2,8,128]{2,1,0:T(8,128)} %constant.22.clone.turn) | copy-start | bytes 24580
  45.1 7.1 %collective-permute-start.17 = (f32[4,80,128]{2,1,0:T(8,128)S(1)}, f32[4,80,128]{2,1,0:T(8,128)S(1)}, u32[]{:S(2)}, u32[]{:S(2)}) collective-permute-start(f32[4,80,128]{2,1,0:T(8,128)S(1)} %get-tuple-element.62), channel_id=1, source_target_pairs={{0,1},{1,0},{2,3},{3,2},{4,5},{5,4},{6,7},{7,6},{8,9},{9,8},{10,11... | collective-permute-start | bytes 491528 | tf_op jit(solution)/shard_map/ppermute | solution.py:575
  45.2 1.3 %collective-permute-start.12 = (f32[128,128]{1,0:T(8,128)S(1)}, f32[128,128]{1,0:T(8,128)S(1)}, u32[]{:S(2)}, u32[]{:S(2)}) collective-permute-start(f32[128,128]{1,0:T(8,128)S(1)} %get-tuple-element.58), channel_id=1, source_target_pairs={{0,8},{1,9},{2,10},{3,11},{4,12},{5,13},{6,14},{7,15},{8,0},{9,1},... | collective-permute-start | bytes 196616 | tf_op jit(solution)/shard_map/ppermute | solution.py:575
  46.5 8.0 %collective-permute-start.15 = (f32[128,128]{1,0:T(8,128)S(1)}, f32[128,128]{1,0:T(8,128)S(1)}, u32[]{:S(2)}, u32[]{:S(2)}) collective-permute-start(f32[128,128]{1,0:T(8,128)S(1)} %probe_sum.7.refs_0_), channel_id=1, source_target_pairs={{0,17},{1,16},{2,19},{3,18},{4,21},{5,20},{6,23},{7,22},{8,25},{9,... | collective-permute-start | bytes 196616 | tf_op jit(solution)/shard_map/ppermute | solution.py:575
  49.4 7.3 %collective-permute-start.14 = (f32[128,128]{1,0:T(8,128)S(1)}, f32[128,128]{1,0:T(8,128)S(1)}, u32[]{:S(2)}, u32[]{:S(2)}) collective-permute-start(f32[128,128]{1,0:T(8,128)S(1)} %probe_sum.7.refs_0_), channel_id=1, source_target_pairs={{0,1},{1,0},{2,3},{3,2},{4,5},{5,4},{6,7},{7,6},{8,9},{9,8},{10,11... | collective-permute-start | bytes 196616 | tf_op jit(solution)/shard_map/ppermute | solution.py:575
  49.5 7.2 %collective-permute-start.13 = (f32[128,128]{1,0:T(8,128)S(1)}, f32[128,128]{1,0:T(8,128)S(1)}, u32[]{:S(2)}, u32[]{:S(2)}) collective-permute-start(f32[128,128]{1,0:T(8,128)S(1)} %probe_sum.7.refs_0_), channel_id=1, source_target_pairs={{0,16},{1,17},{2,18},{3,19},{4,20},{5,21},{6,22},{7,23},{8,24},{9,... | collective-permute-start | bytes 196616 | tf_op jit(solution)/shard_map/ppermute | solution.py:575
  52.2 9.3 %collective-permute-start.18 = (f32[2,80,128]{2,1,0:T(8,128)S(1)}, f32[2,80,128]{2,1,0:T(8,128)S(1)}, u32[]{:S(2)}, u32[]{:S(2)}) collective-permute-start(f32[2,80,128]{2,1,0:T(8,128)S(1)} %get-tuple-element.64), channel_id=1, source_target_pairs={{0,2},{1,3},{2,0},{3,1},{4,6},{5,7},{6,4},{7,5},{8,10},{9,11},{10,... | collective-permute-start | bytes 245768 | tf_op jit(solution)/shard_map/ppermute | solution.py:575
  52.3 9.2 %collective-permute-start.19 = (f32[2,80,128]{2,1,0:T(8,128)S(1)}, f32[2,80,128]{2,1,0:T(8,128)S(1)}, u32[]{:S(2)}, u32[]{:S(2)}) collective-permute-start(f32[2,80,128]{2,1,0:T(8,128)S(1)} %get-tuple-element.65), channel_id=1, source_target_pairs={{0,4},{1,5},{2,6},{3,7},{4,0},{5,1},{6,2},{7,3},{8,12},{9,13},{10,... | collective-permute-start | bytes 245768 | tf_op jit(solution)/shard_map/ppermute | solution.py:575
  54.5 7.0 %collective-permute-start.20 = (f32[2,80,128]{2,1,0:T(8,128)S(1)}, f32[2,80,128]{2,1,0:T(8,128)S(1)}, u32[]{:S(2)}, u32[]{:S(2)}) collective-permute-start(f32[2,80,128]{2,1,0:T(8,128)S(1)} %get-tuple-element.66), channel_id=1, source_target_pairs={{0,6},{1,7},{2,4},{3,5},{4,2},{5,3},{6,0},{7,1},{8,14},{9,15},{10,... | collective-permute-start | bytes 245768 | tf_op jit(solution)/shard_map/ppermute | solution.py:575
  56.7 4.8 %collective-permute-start.16 = (f32[128,128]{1,0:T(8,128)S(1)}, f32[128,128]{1,0:T(8,128)S(1)}, u32[]{:S(2)}, u32[]{:S(2)}) collective-permute-start(f32[128,128]{1,0:T(8,128)S(1)} %probe_sum.8.refs_0_), channel_id=1, source_target_pairs={{0,2},{1,3},{2,0},{3,1},{4,6},{5,7},{6,4},{7,5},{8,10},{9,11},{10,... | collective-permute-start | bytes 196616 | tf_op jit(solution)/shard_map/ppermute | solution.py:575
  61.8 2.2 %collective-permute-start.21 = (f32[320,128]{1,0:T(8,128)S(1)}, f32[320,128]{1,0:T(8,128)S(1)}, u32[]{:S(2)}, u32[]{:S(2)}) collective-permute-start(f32[320,128]{1,0:T(8,128)S(1)} %slab_spectrum.1.rest_0_), channel_id=1, source_target_pairs={{0,8},{1,9},{2,10},{3,11},{4,12},{5,13},{6,14},{7,15},{8,0},{9,1},... | collective-permute-start | bytes 491528 | tf_op jit(solution)/shard_map/ppermute | solution.py:575
  61.9 8.5 %collective-permute-start.23 = (f32[320,128]{1,0:T(8,128)S(1)}, f32[320,128]{1,0:T(8,128)S(1)}, u32[]{:S(2)}, u32[]{:S(2)}) collective-permute-start(f32[320,128]{1,0:T(8,128)S(1)} %slab_spectrum.1.rest_0_), channel_id=1, source_target_pairs={{0,24},{1,25},{2,26},{3,27},{4,28},{5,29},{6,30},{7,31},{8,16},{9,... | collective-permute-start | bytes 491528 | tf_op jit(solution)/shard_map/ppermute | solution.py:575
  63.4 8.6 %collective-permute-start.22 = (f32[320,128]{1,0:T(8,128)S(1)}, f32[320,128]{1,0:T(8,128)S(1)}, u32[]{:S(2)}, u32[]{:S(2)}) collective-permute-start(f32[320,128]{1,0:T(8,128)S(1)} %slab_spectrum.1.rest_0_), channel_id=1, source_target_pairs={{0,16},{1,17},{2,18},{3,19},{4,20},{5,21},{6,22},{7,23},{8,24},{9,... | collective-permute-start | bytes 491528 | tf_op jit(solution)/shard_map/ppermute | solution.py:575
  64.1 6.3 %collective-permute-start.26 = (f32[128,128]{1,0:T(8,128)S(1)}, f32[128,128]{1,0:T(8,128)S(1)}, u32[]{:S(2)}, u32[]{:S(2)}) collective-permute-start(f32[128,128]{1,0:T(8,128)S(1)} %probe_sum.9._.refs_0_), channel_id=1, source_target_pairs={{0,4},{1,5},{2,6},{3,7},{4,0},{5,1},{6,2},{7,3},{8,12},{9,13},{10,... | collective-permute-start | bytes 196616 | tf_op jit(solution)/shard_map/ppermute | solution.py:575
  65.1 5.3 %collective-permute-start.25 = (f32[160,128]{1,0:T(8,128)S(1)}, f32[160,128]{1,0:T(8,128)S(1)}, u32[]{:S(2)}, u32[]{:S(2)}) collective-permute-start(f32[160,128]{1,0:T(8,128)S(1)} %get-tuple-element.71), channel_id=1, source_target_pairs={{1,2},{3,4},{5,6},{2,1},{4,3},{6,5},{9,10},{11,12},{13,14},{10,9},... | collective-permute-start | bytes 245768 | tf_op jit(solution)/shard_map/ppermute | solution.py:563
  65.9 6.8 %collective-permute-start.24 = (f32[160,128]{1,0:T(8,128)S(1)}, f32[160,128]{1,0:T(8,128)S(1)}, u32[]{:S(2)}, u32[]{:S(2)}) collective-permute-start(f32[160,128]{1,0:T(8,128)S(1)} %get-tuple-element.70), channel_id=1, source_target_pairs={{0,1},{2,3},{4,5},{6,7},{1,0},{3,2},{5,4},{7,6},{8,9},{10,11},{12,... | collective-permute-start | bytes 245768 | tf_op jit(solution)/shard_map/ppermute | solution.py:563
  70.3 2.4 %collective-permute-start.27 = (f32[128,128]{1,0:T(8,128)S(1)}, f32[128,128]{1,0:T(8,128)S(1)}, u32[]{:S(2)}, u32[]{:S(2)}) collective-permute-start(f32[128,128]{1,0:T(8,128)S(1)} %probe_last.1.rest_7_), channel_id=1, source_target_pairs={{0,8},{1,9},{2,10},{3,11},{4,12},{5,13},{6,14},{7,15},{8,0},{9,1},... | collective-permute-start | bytes 196616 | tf_op jit(solution)/shard_map/ppermute | solution.py:575

commit v6 on v5

--- a/solution.py
+++ b/solution.py
@@ -470,17 +470,11 @@
 
 def inverse_kernel(depth, masks, phases, turn, table, *rest):
     spectra = rest[: len(masks)]
-    last, outs = rest[len(masks) : -7], rest[-7:-4]
-    (image, psi, probe), sems = rest[-4:-1], rest[-1]
+    image_out, token, image, sems = rest[-4:]
+    token[...] = jnp.zeros_like(token)
     _, _, tiles, beam, width = phases.shape
     angles = [lax.axis_index("angle") ^ mask for mask in masks]
-    finish(*last, psi, probe)
-    copies = [
-        pltpu.make_async_copy(psi, outs[1], sems.at[0]),
-        pltpu.make_async_copy(probe, outs[2], sems.at[1]),
-    ]
-    for copy in copies:
-        copy.start()
+    copies = []
     wide = math.gcd(depth, 2)
     count = tiles * depth
 
@@ -515,7 +509,7 @@
                 image[0, start + member, :, columns] = real.astype(BF16)
                 image[1, start + member, :, columns] = imag.astype(BF16)
         rows = pl.ds(start, wide)
-        copy = pltpu.make_async_copy(image.at[:, rows], outs[0].at[:, rows], sems.at[2 + start // wide])
+        copy = pltpu.make_async_copy(image.at[:, rows], image_out.at[:, rows], sems.at[start // wide])
         copy.start()
         copies.append(copy)
 
@@ -524,7 +518,7 @@
         copy.wait()
 
 
-def finish(base, partner, other, probe_mine, probe_theirs, psi_out, probe_out):
+def finish_kernel(base, partner, other, probe_mine, probe_theirs, _, psi_out, probe_out):
     mask = lane_mask(base.shape[1:], base.shape[-1] // 2)
     left, right = packed_sides(partner, other, is_even())
     real, imag = unfold(left, right, mask)
@@ -732,31 +726,30 @@
     )(probe_mine, extra, *terms)
     probe_theirs = swap(probe_mine, tiles, devices)
     scale = 1.0 / (angles * tiles * width)
-    last = (base, partner, other, probe_mine, probe_theirs)
-    tomo, psi_new, probe_new = call(
+    tomo, token = call(
         functools.partial(inverse_kernel, depth, masks),
         "slab_image",
-        [
-            shape(2, depth, beam, tiles * width, dtype=BF16),
-            shape(2, 1, rows_total, width),
-            shape(2, side, side),
-        ],
-        [VMEM] * (3 + angles + len(last)),
+        [shape(2, depth, beam, tiles * width, dtype=BF16), shape(8, width)],
+        [VMEM] * (3 + angles) + [ANY],
         [
             pltpu.VMEM((2, depth, beam, tiles * width), BF16),
-            pltpu.VMEM((2, 1, rows_total, width), F32),
-            pltpu.VMEM((2, side, side), F32),
-            pltpu.SemaphoreType.DMA((2 + depth // math.gcd(depth, 2),)),
+            pltpu.SemaphoreType.DMA((depth // math.gcd(depth, 2),)),
         ],
         depth * tiles * beam * 2 * 6 * width * 2 * width,
-        out_specs=[HBM] * 3,
+        out_specs=[HBM, VMEM],
     )(
         phases,
         jnp.asarray(twiddles(tiles, width, 1.0, scale)),
         jnp.asarray(right_table(width, 1.0, 1.0)),
         *spectra,
-        *last,
+        probe_mine,
     )
+    psi_new, probe_new = call(
+        finish_kernel,
+        "field_probe",
+        [shape(2, 1, rows_total, width), shape(2, side, side)],
+        [VMEM] * 5 + [ANY],
+    )(base, partner, other, probe_mine, probe_theirs, token)
     return psi_new, probe_new, tomo
 
 

time: 79.2 us -> 79 us (level)
  transfers between devices with their start and end apart: 28 -> 28, of which waited for: 11 -> 10; matrix products, arithmetic and copies ran while one was open for 0% -> 0% of each run, Pallas kernels for 3% -> 11%
where the time goes in v6:
time: 79 us; the launch traced here: 78.7 us
  starting transfers between devices  33.5 us (42%)
  Pallas kernels  22.1 us (28%)
  waiting for transfers between devices  20.8 us (26%)
  between operations  2.22 us (3%)
    ppermute x22, starting transfers between devices, swap(): lax.ppermute(array, ('angle', 'tile'), [(i, i ^ mask) for i in range(devi...  21.9 us
    ppermute x22, waiting for transfers between devices, swap(): lax.ppermute(array, ('angle', 'tile'), [(i, i ^ mask) for i in range(devi...  20.8 us
    ppermute x6, starting transfers between devices, swap_pairs(): lax.ppermute(array, 'tile', [(i, i + 1) for i in low] + [(i + 1, i) for i...  11.6 us
    pallas_call x1, Pallas kernels, shards(): call(functools.partial(inverse_kernel, depth, masks), 'slab_image', [shap...  5.86 us
    pallas_call x1, Pallas kernels, shards(): call(second_kernel, 'ptycho_second', [shape(*block), flat, flat] + [shape...  5.78 us
    pallas_call x1, Pallas kernels, shards(): call(first_kernel, 'ptycho_first', [shape(*block)] * 4 + [half] * 2, [HBM...  5.67 us
    pallas_call x1, Pallas kernels, shards(): call(stage_kernel, 'stage_operands', [pltpu.VMEM(x.shape, x.dtype) for x...  1.89 us
  transfers between devices with their start and end apart: 28, of which 10 were waited for; matrix products, arithmetic and copies ran while one was open for 0% of the time, Pallas kernels for 11%

profile of v6, /device:TPU:0, one launch (start us, length us, event | category | flops | bytes accessed | tf_op | source)
XLA Modules:
  0.0 78.7 jit_solution(2475749753803229019)
XLA Ops:
  0.6 1.0 %psi_pack.1 = (f32[160,128]{1,0:T(8,128)S(1)}, f32[160,128]{1,0:T(8,128)S(1)}) custom-call(f32[2,1,160,128]{3,2,1,0:T(8,128)} %psi.1), custom_call_target="tpu_custom_call" | custom-call | tf_op jit(solution)/shard_map/psi_pack/pallas_call | solution.py:609
  1.7 3.0 %collective-permute-start = (f32[160,128]{1,0:T(8,128)S(1)}, f32[160,128]{1,0:T(8,128)S(1)}, u32[]{:S(2)}, u32[]{:S(2)}) collective-permute-start(f32[160,128]{1,0:T(8,128)S(1)} %get-tuple-element.43), channel_id=1, source_target_pairs={{0,1},{2,3},{4,5},{6,7},{1,0},{3,2},{5,4},{7,6},{8,9},{10,11},{12,... | collective-permute-start | bytes 245768 | tf_op jit(solution)/shard_map/ppermute | solution.py:557
  4.7 0.7 collective-permute-start.1
  6.6 1.9 %stage_operands.1 = (f32[2,1,160,128]{3,2,1,0:T(8,128)S(1)}, f32[2,1,160,128]{3,2,1,0:T(8,128)S(1)}, f32[2,128,128]{2,1,0:T(8,128)S(1)}, f32[1,1,16,128,128]{4,3...) custom-call(f32[2,1,160,128]{3,2,1,0:T(8,128)} %psi.1, ...), custom_call_target="tpu_custom_call" | custom-call | bytes 3000000 | tf_op jit(solution)/shard_map/stage_operands/pallas_call | solution.py:621
  8.5 0.0 collective-permute-done.partner
  8.6 5.7 %ptycho_first.1 = (f32[2,160,128]{2,1,0:T(8,128)S(1)}, f32[2,160,128]{2,1,0:T(8,128)S(1)}, f32[2,160,128]{2,1,0:T(8,128)S(1)}, f32[2,160,128]{2,1,0:T(8,128)S(1)...) custom-call(s32[1,1,16]{2,1,0:T(1,128)} %pos_z.3, s32[1,1,16]{2,1,0:T(1,128)} %pos_x.3, s32[1,1]{1,0:T(1,128)S(6)} %copy.19.counts, ...), custom_call_target="tpu_custom_call" | custom-call | flops 3221225472 | tf_op jit(solution)/shard_map/ptycho_first/pallas_call | solution.py:635
  14.2 0.1 collective-permute-start.4
  14.3 1.2 %collective-permute-done.4.refs_1_ = f32[136,128]{1,0:T(8,128)S(1)} collective-permute-done((f32[136,128]{1,0:T(8,128)S(1)}, f32[136,128]{1,0:T(8,128)S(1)}, u32[]{:S(2)}, u32[]{:S(2)}) %collective-permute-start.4) | collective-permute-done | bytes 69664 | tf_op jit(solution)/shard_map/ppermute | solution.py:569
  15.6 5.3 %collective-permute-start.7 = (f32[136,128]{1,0:T(8,128)S(1)}, f32[136,128]{1,0:T(8,128)S(1)}, u32[]{:S(2)}, u32[]{:S(2)}) collective-permute-start(f32[136,128]{1,0:T(8,128)S(1)} %probe_sum.5.refs_0_), channel_id=1, source_target_pairs={{0,17},{1,16},{2,19},{3,18},{4,21},{5,20},{6,23},{7,22},{8,25},{9,... | collective-permute-start | bytes 208904 | tf_op jit(solution)/shard_map/ppermute | solution.py:569
  20.8 0.6 collective-permute-start.5
  21.5 1.9 %collective-permute-start.2 = (f32[2,160,128]{2,1,0:T(8,128)S(1)}, f32[2,160,128]{2,1,0:T(8,128)S(1)}, u32[]{:S(2)}, u32[]{:S(2)}) collective-permute-start(f32[2,160,128]{2,1,0:T(8,128)S(1)} %get-tuple-element.53), channel_id=1, source_target_pairs={{0,1},{2,3},{4,5},{6,7},{1,0},{3,2},{5,4},{7,6},{8,9},{10,11},{12,... | collective-permute-start | bytes 491528 | tf_op jit(solution)/shard_map/ppermute | solution.py:557
  23.4 0.7 collective-permute-start.3
  24.1 0.0 collective-permute-done.7.refs_3_
  24.1 1.8 %collective-permute-done.6.refs_2_ = f32[136,128]{1,0:T(8,128)S(1)} collective-permute-done((f32[136,128]{1,0:T(8,128)S(1)}, f32[136,128]{1,0:T(8,128)S(1)}, u32[]{:S(2)}, u32[]{:S(2)}) %collective-permute-start.6) | collective-permute-done | bytes 69664 | tf_op jit(solution)/shard_map/ppermute | solution.py:569
  25.9 0.0 collective-permute-done.5.refs_1_
  25.9 4.2 %collective-permute-start.10 = (f32[136,128]{1,0:T(8,128)S(1)}, f32[136,128]{1,0:T(8,128)S(1)}, u32[]{:S(2)}, u32[]{:S(2)}) collective-permute-start(f32[136,128]{1,0:T(8,128)S(1)} %probe_sum.6.sums.refs_0_), channel_id=1, source_target_pairs={{0,6},{1,7},{2,4},{3,5},{4,2},{5,3},{6,0},{7,1},{8,14},{9,15},{10,... | collective-permute-start | bytes 208904 | tf_op jit(solution)/shard_map/ppermute | solution.py:569
  30.1 0.6 collective-permute-start.8
  30.8 0.7 phase_table.1._.rest_4_.phases
  31.5 4.6 %collective-permute-done.10.refs_3_ = f32[136,128]{1,0:T(8,128)S(1)} collective-permute-done((f32[136,128]{1,0:T(8,128)S(1)}, f32[136,128]{1,0:T(8,128)S(1)}, u32[]{:S(2)}, u32[]{:S(2)}) %collective-permute-start.10) | collective-permute-done | bytes 69664 | tf_op jit(solution)/shard_map/ppermute | solution.py:569
  36.1 1.9 %collective-permute-done.9.refs_2_ = f32[136,128]{1,0:T(8,128)S(1)} collective-permute-done((f32[136,128]{1,0:T(8,128)S(1)}, f32[136,128]{1,0:T(8,128)S(1)}, u32[]{:S(2)}, u32[]{:S(2)}) %collective-permute-start.9) | collective-permute-done | bytes 69664 | tf_op jit(solution)/shard_map/ppermute | solution.py:569
  38.0 0.1 collective-permute-start.11
  38.1 0.0 collective-permute-done.3.other
  38.1 1.2 %collective-permute-done.11.probe_theirs = f32[128,128]{1,0:T(8,128)S(1)} collective-permute-done((f32[128,128]{1,0:T(8,128)S(1)}, f32[128,128]{1,0:T(8,128)S(1)}, u32[]{:S(2)}, u32[]{:S(2)}) %collective-permute-start.11) | collective-permute-done | bytes 65568 | tf_op jit(solution)/shard_map/ppermute | solution.py:569
  39.3 5.8 %ptycho_second.1 = (f32[2,160,128]{2,1,0:T(8,128)S(1)}, f32[160,128]{1,0:T(8,128)S(1)}, f32[160,128]{1,0:T(8,128)S(1)}, f32[128,128]{1,0:T(8,128)S(1)}, f32[128,...) custom-call(s32[1,1,16]{2,1,0:T(1,128)} %pos_z.3, s32[1,1,16]{2,1,0:T(1,128)} %pos_x.3, ...), custom_call_target="tpu_custom_call" | custom-call | flops 3221225472 | tf_op jit(solution)/shard_map/ptycho_second/pallas_call | solution.py:677
  45.1 0.1 collective-permute-start.17
  45.2 0.2 collective-permute-start.12
  45.4 1.1 %collective-permute-done.12.refs_1_ = f32[128,128]{1,0:T(8,128)S(1)} collective-permute-done((f32[128,128]{1,0:T(8,128)S(1)}, f32[128,128]{1,0:T(8,128)S(1)}, u32[]{:S(2)}, u32[]{:S(2)}) %collective-permute-start.12) | collective-permute-done | bytes 65568 | tf_op jit(solution)/shard_map/ppermute | solution.py:569
  46.5 2.9 %collective-permute-start.15 = (f32[128,128]{1,0:T(8,128)S(1)}, f32[128,128]{1,0:T(8,128)S(1)}, u32[]{:S(2)}, u32[]{:S(2)}) collective-permute-start(f32[128,128]{1,0:T(8,128)S(1)} %probe_sum.7.refs_0_), channel_id=1, source_target_pairs={{0,17},{1,16},{2,19},{3,18},{4,21},{5,20},{6,23},{7,22},{8,25},{9,... | collective-permute-start | bytes 196616 | tf_op jit(solution)/shard_map/ppermute | solution.py:569
  49.4 0.1 collective-permute-start.14
  49.5 0.6 collective-permute-start.13
  50.1 2.1 %collective-permute-done.17.refs_1_ = f32[4,80,128]{2,1,0:T(8,128)S(1)} collective-permute-done((f32[4,80,128]{2,1,0:T(8,128)S(1)}, f32[4,80,128]{2,1,0:T(8,128)S(1)}, u32[]{:S(2)}, u32[]{:S(2)}) %collective-permute-start.17) | collective-permute-done | bytes 163872 | tf_op jit(solution)/shard_map/ppermute | solution.py:569
  52.3 0.1 collective-permute-start.18
  52.3 1.7 %collective-permute-start.19 = (f32[2,80,128]{2,1,0:T(8,128)S(1)}, f32[2,80,128]{2,1,0:T(8,128)S(1)}, u32[]{:S(2)}, u32[]{:S(2)}) collective-permute-start(f32[2,80,128]{2,1,0:T(8,128)S(1)} %get-tuple-element.67), channel_id=1, source_target_pairs={{0,4},{1,5},{2,6},{3,7},{4,0},{5,1},{6,2},{7,3},{8,12},{9,13},{10,... | collective-permute-start | bytes 245768 | tf_op jit(solution)/shard_map/ppermute | solution.py:569
  54.0 0.5 collective-permute-done.15.refs_3_
  54.5 2.2 %collective-permute-start.20 = (f32[2,80,128]{2,1,0:T(8,128)S(1)}, f32[2,80,128]{2,1,0:T(8,128)S(1)}, u32[]{:S(2)}, u32[]{:S(2)}) collective-permute-start(f32[2,80,128]{2,1,0:T(8,128)S(1)} %get-tuple-element.68), channel_id=1, source_target_pairs={{0,6},{1,7},{2,4},{3,5},{4,2},{5,3},{6,0},{7,1},{8,14},{9,15},{10,... | collective-permute-start | bytes 245768 | tf_op jit(solution)/shard_map/ppermute | solution.py:569
  56.7 0.1 collective-permute-start.16
  56.8 4.7 %collective-permute-done.16.refs_1_ = f32[128,128]{1,0:T(8,128)S(1)} collective-permute-done((f32[128,128]{1,0:T(8,128)S(1)}, f32[128,128]{1,0:T(8,128)S(1)}, u32[]{:S(2)}, u32[]{:S(2)}) %collective-permute-start.16) | collective-permute-done | bytes 65568 | tf_op jit(solution)/shard_map/ppermute | solution.py:569
  61.6 0.3 slab_spectrum.1.rest_0_
  61.9 0.1 collective-permute-start.21
  61.9 1.4 %collective-permute-start.27 = (f32[320,128]{1,0:T(8,128)S(1)}, f32[320,128]{1,0:T(8,128)S(1)}, u32[]{:S(2)}, u32[]{:S(2)}) collective-permute-start(f32[320,128]{1,0:T(8,128)S(1)} %slab_spectrum.1.rest_0_), channel_id=1, source_target_pairs={{0,24},{1,25},{2,26},{3,27},{4,28},{5,29},{6,30},{7,31},{8,16},{9,... | collective-permute-start | bytes 491528 | tf_op jit(solution)/shard_map/ppermute | solution.py:569
  63.3 0.8 collective-permute-start.26
  64.1 0.9 %collective-permute-start.24 = (f32[128,128]{1,0:T(8,128)S(1)}, f32[128,128]{1,0:T(8,128)S(1)}, u32[]{:S(2)}, u32[]{:S(2)}) collective-permute-start(f32[128,128]{1,0:T(8,128)S(1)} %probe_sum.9._.refs_0_), channel_id=1, source_target_pairs={{0,4},{1,5},{2,6},{3,7},{4,0},{5,1},{6,2},{7,3},{8,12},{9,13},{10,... | collective-permute-start | bytes 196616 | tf_op jit(solution)/shard_map/ppermute | solution.py:569
  65.0 0.8 %collective-permute-start.23 = (f32[160,128]{1,0:T(8,128)S(1)}, f32[160,128]{1,0:T(8,128)S(1)}, u32[]{:S(2)}, u32[]{:S(2)}) collective-permute-start(f32[160,128]{1,0:T(8,128)S(1)} %get-tuple-element.71), channel_id=1, source_target_pairs={{1,2},{3,4},{5,6},{2,1},{4,3},{6,5},{9,10},{11,12},{13,14},{10,9},... | collective-permute-start | bytes 245768 | tf_op jit(solution)/shard_map/ppermute | solution.py:557
  65.8 4.5 %collective-permute-start.22 = (f32[160,128]{1,0:T(8,128)S(1)}, f32[160,128]{1,0:T(8,128)S(1)}, u32[]{:S(2)}, u32[]{:S(2)}) collective-permute-start(f32[160,128]{1,0:T(8,128)S(1)} %get-tuple-element.70), channel_id=1, source_target_pairs={{0,1},{2,3},{4,5},{6,7},{1,0},{3,2},{5,4},{7,6},{8,9},{10,11},{12,... | collective-permute-start | bytes 245768 | tf_op jit(solution)/shard_map/ppermute | solution.py:557
  70.4 0.1 collective-permute-start.25
  70.5 1.6 %collective-permute-done.26.rest_2_ = f32[320,128]{1,0:T(8,128)S(1)} collective-permute-done((f32[320,128]{1,0:T(8,128)S(1)}, f32[320,128]{1,0:T(8,128)S(1)}, u32[]{:S(2)}, u32[]{:S(2)}) %collective-permute-start.26) | collective-permute-done | bytes 163872 | tf_op jit(solution)/shard_map/ppermute | solution.py:569
  72.0 5.9 %slab_image.1 = (bf16[2,20,32,1024]{3,2,1,0:T(8,128)(2,1)}, f32[8,128]{1,0:T(8,128)S(1)}) custom-call(f32[4,3,8,32,128]{4,3,2,1,0:T(8,128)S(1)} %phase_table.1._.rest_4_.phases, f32[2,8,128]{2,1,0:T(8,128)S(1)} %copy-done.3, bf16[768,256]{1,0:T(8,128)(2,1)S(1)} %copy-done.2, f32[320,128]{1,0:T(8,128)S(1)} %slab_spectrum.1.rest_0_, ...), custom_call_target="tpu_custom_call" | custom-call | flops 2013265920 | tf_op jit(solution)/shard_map/slab_image/pallas_call | solution.py:729
  77.9 0.8 field_probe.1
  (32 shorter events, 0.2 us)
Async XLA Ops:
  1.7 6.9 %collective-permute-start = (f32[160,128]{1,0:T(8,128)S(1)}, f32[160,128]{1,0:T(8,128)S(1)}, u32[]{:S(2)}, u32[]{:S(2)}) collective-permute-start(f32[160,128]{1,0:T(8,128)S(1)} %get-tuple-element.43), channel_id=1, source_target_pairs={{0,1},{2,3},{4,5},{6,7},{1,0},{3,2},{5,4},{7,6},{8,9},{10,11},{12,... | collective-permute-start | bytes 245768 | tf_op jit(solution)/shard_map/ppermute | solution.py:557
  4.7 3.9 %collective-permute-start.1 = (f32[160,128]{1,0:T(8,128)S(1)}, f32[160,128]{1,0:T(8,128)S(1)}, u32[]{:S(2)}, u32[]{:S(2)}) collective-permute-start(f32[160,128]{1,0:T(8,128)S(1)} %get-tuple-element.44), channel_id=1, source_target_pairs={{1,2},{3,4},{5,6},{2,1},{4,3},{6,5},{9,10},{11,12},{13,14},{10,9},... | collective-permute-start | bytes 245768 | tf_op jit(solution)/shard_map/ppermute | solution.py:557
  14.2 1.3 %collective-permute-start.4 = (f32[136,128]{1,0:T(8,128)S(1)}, f32[136,128]{1,0:T(8,128)S(1)}, u32[]{:S(2)}, u32[]{:S(2)}) collective-permute-start(f32[136,128]{1,0:T(8,128)S(1)} %get-tuple-element.56), channel_id=1, source_target_pairs={{0,8},{1,9},{2,10},{3,11},{4,12},{5,13},{6,14},{7,15},{8,0},{9,1},... | collective-permute-start | bytes 208904 | tf_op jit(solution)/shard_map/ppermute | solution.py:569
  15.6 8.5 %collective-permute-start.7 = (f32[136,128]{1,0:T(8,128)S(1)}, f32[136,128]{1,0:T(8,128)S(1)}, u32[]{:S(2)}, u32[]{:S(2)}) collective-permute-start(f32[136,128]{1,0:T(8,128)S(1)} %probe_sum.5.refs_0_), channel_id=1, source_target_pairs={{0,17},{1,16},{2,19},{3,18},{4,21},{5,20},{6,23},{7,22},{8,25},{9,... | collective-permute-start | bytes 208904 | tf_op jit(solution)/shard_map/ppermute | solution.py:569
  20.8 5.1 %collective-permute-start.6 = (f32[136,128]{1,0:T(8,128)S(1)}, f32[136,128]{1,0:T(8,128)S(1)}, u32[]{:S(2)}, u32[]{:S(2)}) collective-permute-start(f32[136,128]{1,0:T(8,128)S(1)} %probe_sum.5.refs_0_), channel_id=1, source_target_pairs={{0,1},{1,0},{2,3},{3,2},{4,5},{5,4},{6,7},{7,6},{8,9},{9,8},{10,11... | collective-permute-start | bytes 208904 | tf_op jit(solution)/shard_map/ppermute | solution.py:569
  20.8 5.1 %collective-permute-start.5 = (f32[136,128]{1,0:T(8,128)S(1)}, f32[136,128]{1,0:T(8,128)S(1)}, u32[]{:S(2)}, u32[]{:S(2)}) collective-permute-start(f32[136,128]{1,0:T(8,128)S(1)} %probe_sum.5.refs_0_), channel_id=1, source_target_pairs={{0,16},{1,17},{2,18},{3,19},{4,20},{5,21},{6,22},{7,23},{8,24},{9,... | collective-permute-start | bytes 208904 | tf_op jit(solution)/shard_map/ppermute | solution.py:569
  21.5 16.6 %collective-permute-start.2 = (f32[2,160,128]{2,1,0:T(8,128)S(1)}, f32[2,160,128]{2,1,0:T(8,128)S(1)}, u32[]{:S(2)}, u32[]{:S(2)}) collective-permute-start(f32[2,160,128]{2,1,0:T(8,128)S(1)} %get-tuple-element.53), channel_id=1, source_target_pairs={{0,1},{2,3},{4,5},{6,7},{1,0},{3,2},{5,4},{7,6},{8,9},{10,11},{12,... | collective-permute-start | bytes 491528 | tf_op jit(solution)/shard_map/ppermute | solution.py:557
  23.4 14.7 %collective-permute-start.3 = (f32[2,160,128]{2,1,0:T(8,128)S(1)}, f32[2,160,128]{2,1,0:T(8,128)S(1)}, u32[]{:S(2)}, u32[]{:S(2)}) collective-permute-start(f32[2,160,128]{2,1,0:T(8,128)S(1)} %get-tuple-element.54), channel_id=1, source_target_pairs={{1,2},{3,4},{5,6},{2,1},{4,3},{6,5},{9,10},{11,12},{13,14},{10,9},... | collective-permute-start | bytes 491528 | tf_op jit(solution)/shard_map/ppermute | solution.py:557
  25.9 10.2 %collective-permute-start.10 = (f32[136,128]{1,0:T(8,128)S(1)}, f32[136,128]{1,0:T(8,128)S(1)}, u32[]{:S(2)}, u32[]{:S(2)}) collective-permute-start(f32[136,128]{1,0:T(8,128)S(1)} %probe_sum.6.sums.refs_0_), channel_id=1, source_target_pairs={{0,6},{1,7},{2,4},{3,5},{4,2},{5,3},{6,0},{7,1},{8,14},{9,15},{10,... | collective-permute-start | bytes 208904 | tf_op jit(solution)/shard_map/ppermute | solution.py:569
  30.1 7.8 %collective-permute-start.9 = (f32[136,128]{1,0:T(8,128)S(1)}, f32[136,128]{1,0:T(8,128)S(1)}, u32[]{:S(2)}, u32[]{:S(2)}) collective-permute-start(f32[136,128]{1,0:T(8,128)S(1)} %probe_sum.6.sums.refs_0_), channel_id=1, source_target_pairs={{0,4},{1,5},{2,6},{3,7},{4,0},{5,1},{6,2},{7,3},{8,12},{9,13},{10,... | collective-permute-start | bytes 208904 | tf_op jit(solution)/shard_map/ppermute | solution.py:569
  30.1 7.8 %collective-permute-start.8 = (f32[136,128]{1,0:T(8,128)S(1)}, f32[136,128]{1,0:T(8,128)S(1)}, u32[]{:S(2)}, u32[]{:S(2)}) collective-permute-start(f32[136,128]{1,0:T(8,128)S(1)} %probe_sum.6.sums.refs_0_), channel_id=1, source_target_pairs={{0,2},{1,3},{2,0},{3,1},{4,6},{5,7},{6,4},{7,5},{8,10},{9,11},{10,... | collective-permute-start | bytes 208904 | tf_op jit(solution)/shard_map/ppermute | solution.py:569
  38.0 1.3 %collective-permute-start.11 = (f32[128,128]{1,0:T(8,128)S(1)}, f32[128,128]{1,0:T(8,128)S(1)}, u32[]{:S(2)}, u32[]{:S(2)}) collective-permute-start(f32[128,128]{1,0:T(8,128)S(1)} %get-tuple-element.57.probe_mine), channel_id=1, source_target_pairs={{0,8},{1,9},{2,10},{3,11},{4,12},{5,13},{6,14},{7,15},{8,0},{9,1},... | collective-permute-start | bytes 196616 | tf_op jit(solution)/shard_map/ppermute | solution.py:569
  39.3 22.2 %copy-start = (bf16[768,256]{1,0:T(8,128)(2,1)S(1)}, bf16[768,256]{1,0:T(8,128)(2,1)}, u32[]{:S(2)}) copy-start(bf16[768,256]{1,0:T(8,128)(2,1)} %constant.21.clone.table) | copy-start | bytes 1179652
  39.3 22.3 %copy-start.1 = (f32[2,8,128]{2,1,0:T(8,128)S(1)}, f32[2,8,128]{2,1,0:T(8,128)}, u32[]{:S(2)}) copy-start(f32[2,8,128]{2,1,0:T(8,128)} %constant.20.clone.turn) | copy-start | bytes 24580
  39.3 32.7 %copy-start.2 = (bf16[768,256]{1,0:T(8,128)(2,1)S(1)}, bf16[768,256]{1,0:T(8,128)(2,1)}, u32[]{:S(2)}) copy-start(bf16[768,256]{1,0:T(8,128)(2,1)} %constant.23.clone.table) | copy-start | bytes 1179652
  39.3 32.7 %copy-start.3 = (f32[2,8,128]{2,1,0:T(8,128)S(1)}, f32[2,8,128]{2,1,0:T(8,128)}, u32[]{:S(2)}) copy-start(f32[2,8,128]{2,1,0:T(8,128)} %constant.22.clone.turn) | copy-start | bytes 24580
  45.1 7.1 %collective-permute-start.17 = (f32[4,80,128]{2,1,0:T(8,128)S(1)}, f32[4,80,128]{2,1,0:T(8,128)S(1)}, u32[]{:S(2)}, u32[]{:S(2)}) collective-permute-start(f32[4,80,128]{2,1,0:T(8,128)S(1)} %get-tuple-element.64), channel_id=1, source_target_pairs={{0,1},{1,0},{2,3},{3,2},{4,5},{5,4},{6,7},{7,6},{8,9},{9,8},{10,11... | collective-permute-start | bytes 491528 | tf_op jit(solution)/shard_map/ppermute | solution.py:569
  45.2 1.3 %collective-permute-start.12 = (f32[128,128]{1,0:T(8,128)S(1)}, f32[128,128]{1,0:T(8,128)S(1)}, u32[]{:S(2)}, u32[]{:S(2)}) collective-permute-start(f32[128,128]{1,0:T(8,128)S(1)} %get-tuple-element.60), channel_id=1, source_target_pairs={{0,8},{1,9},{2,10},{3,11},{4,12},{5,13},{6,14},{7,15},{8,0},{9,1},... | collective-permute-start | bytes 196616 | tf_op jit(solution)/shard_map/ppermute | solution.py:569
  46.5 8.0 %collective-permute-start.15 = (f32[128,128]{1,0:T(8,128)S(1)}, f32[128,128]{1,0:T(8,128)S(1)}, u32[]{:S(2)}, u32[]{:S(2)}) collective-permute-start(f32[128,128]{1,0:T(8,128)S(1)} %probe_sum.7.refs_0_), channel_id=1, source_target_pairs={{0,17},{1,16},{2,19},{3,18},{4,21},{5,20},{6,23},{7,22},{8,25},{9,... | collective-permute-start | bytes 196616 | tf_op jit(solution)/shard_map/ppermute | solution.py:569
  49.4 7.3 %collective-permute-start.14 = (f32[128,128]{1,0:T(8,128)S(1)}, f32[128,128]{1,0:T(8,128)S(1)}, u32[]{:S(2)}, u32[]{:S(2)}) collective-permute-start(f32[128,128]{1,0:T(8,128)S(1)} %probe_sum.7.refs_0_), channel_id=1, source_target_pairs={{0,1},{1,0},{2,3},{3,2},{4,5},{5,4},{6,7},{7,6},{8,9},{9,8},{10,11... | collective-permute-start | bytes 196616 | tf_op jit(solution)/shard_map/ppermute | solution.py:569
  49.5 7.2 %collective-permute-start.13 = (f32[128,128]{1,0:T(8,128)S(1)}, f32[128,128]{1,0:T(8,128)S(1)}, u32[]{:S(2)}, u32[]{:S(2)}) collective-permute-start(f32[128,128]{1,0:T(8,128)S(1)} %probe_sum.7.refs_0_), channel_id=1, source_target_pairs={{0,16},{1,17},{2,18},{3,19},{4,20},{5,21},{6,22},{7,23},{8,24},{9,... | collective-permute-start | bytes 196616 | tf_op jit(solution)/shard_map/ppermute | solution.py:569
  52.3 9.3 %collective-permute-start.18 = (f32[2,80,128]{2,1,0:T(8,128)S(1)}, f32[2,80,128]{2,1,0:T(8,128)S(1)}, u32[]{:S(2)}, u32[]{:S(2)}) collective-permute-start(f32[2,80,128]{2,1,0:T(8,128)S(1)} %get-tuple-element.66), channel_id=1, source_target_pairs={{0,2},{1,3},{2,0},{3,1},{4,6},{5,7},{6,4},{7,5},{8,10},{9,11},{10,... | collective-permute-start | bytes 245768 | tf_op jit(solution)/shard_map/ppermute | solution.py:569
  52.3 9.2 %collective-permute-start.19 = (f32[2,80,128]{2,1,0:T(8,128)S(1)}, f32[2,80,128]{2,1,0:T(8,128)S(1)}, u32[]{:S(2)}, u32[]{:S(2)}) collective-permute-start(f32[2,80,128]{2,1,0:T(8,128)S(1)} %get-tuple-element.67), channel_id=1, source_target_pairs={{0,4},{1,5},{2,6},{3,7},{4,0},{5,1},{6,2},{7,3},{8,12},{9,13},{10,... | collective-permute-start | bytes 245768 | tf_op jit(solution)/shard_map/ppermute | solution.py:569
  54.5 7.0 %collective-permute-start.20 = (f32[2,80,128]{2,1,0:T(8,128)S(1)}, f32[2,80,128]{2,1,0:T(8,128)S(1)}, u32[]{:S(2)}, u32[]{:S(2)}) collective-permute-start(f32[2,80,128]{2,1,0:T(8,128)S(1)} %get-tuple-element.68), channel_id=1, source_target_pairs={{0,6},{1,7},{2,4},{3,5},{4,2},{5,3},{6,0},{7,1},{8,14},{9,15},{10,... | collective-permute-start | bytes 245768 | tf_op jit(solution)/shard_map/ppermute | solution.py:569
  56.7 4.8 %collective-permute-start.16 = (f32[128,128]{1,0:T(8,128)S(1)}, f32[128,128]{1,0:T(8,128)S(1)}, u32[]{:S(2)}, u32[]{:S(2)}) collective-permute-start(f32[128,128]{1,0:T(8,128)S(1)} %probe_sum.8.refs_0_), channel_id=1, source_target_pairs={{0,2},{1,3},{2,0},{3,1},{4,6},{5,7},{6,4},{7,5},{8,10},{9,11},{10,... | collective-permute-start | bytes 196616 | tf_op jit(solution)/shard_map/ppermute | solution.py:569
  61.9 2.2 %collective-permute-start.21 = (f32[320,128]{1,0:T(8,128)S(1)}, f32[320,128]{1,0:T(8,128)S(1)}, u32[]{:S(2)}, u32[]{:S(2)}) collective-permute-start(f32[320,128]{1,0:T(8,128)S(1)} %slab_spectrum.1.rest_0_), channel_id=1, source_target_pairs={{0,8},{1,9},{2,10},{3,11},{4,12},{5,13},{6,14},{7,15},{8,0},{9,1},... | collective-permute-start | bytes 491528 | tf_op jit(solution)/shard_map/ppermute | solution.py:569
  61.9 8.5 %collective-permute-start.27 = (f32[320,128]{1,0:T(8,128)S(1)}, f32[320,128]{1,0:T(8,128)S(1)}, u32[]{:S(2)}, u32[]{:S(2)}) collective-permute-start(f32[320,128]{1,0:T(8,128)S(1)} %slab_spectrum.1.rest_0_), channel_id=1, source_target_pairs={{0,24},{1,25},{2,26},{3,27},{4,28},{5,29},{6,30},{7,31},{8,16},{9,... | collective-permute-start | bytes 491528 | tf_op jit(solution)/shard_map/ppermute | solution.py:569
  63.3 8.7 %collective-permute-start.26 = (f32[320,128]{1,0:T(8,128)S(1)}, f32[320,128]{1,0:T(8,128)S(1)}, u32[]{:S(2)}, u32[]{:S(2)}) collective-permute-start(f32[320,128]{1,0:T(8,128)S(1)} %slab_spectrum.1.rest_0_), channel_id=1, source_target_pairs={{0,16},{1,17},{2,18},{3,19},{4,20},{5,21},{6,22},{7,23},{8,24},{9,... | collective-permute-start | bytes 491528 | tf_op jit(solution)/shard_map/ppermute | solution.py:569
  64.1 6.3 %collective-permute-start.24 = (f32[128,128]{1,0:T(8,128)S(1)}, f32[128,128]{1,0:T(8,128)S(1)}, u32[]{:S(2)}, u32[]{:S(2)}) collective-permute-start(f32[128,128]{1,0:T(8,128)S(1)} %probe_sum.9._.refs_0_), channel_id=1, source_target_pairs={{0,4},{1,5},{2,6},{3,7},{4,0},{5,1},{6,2},{7,3},{8,12},{9,13},{10,... | collective-permute-start | bytes 196616 | tf_op jit(solution)/shard_map/ppermute | solution.py:569
  65.0 12.9 %collective-permute-start.23 = (f32[160,128]{1,0:T(8,128)S(1)}, f32[160,128]{1,0:T(8,128)S(1)}, u32[]{:S(2)}, u32[]{:S(2)}) collective-permute-start(f32[160,128]{1,0:T(8,128)S(1)} %get-tuple-element.71), channel_id=1, source_target_pairs={{1,2},{3,4},{5,6},{2,1},{4,3},{6,5},{9,10},{11,12},{13,14},{10,9},... | collective-permute-start | bytes 245768 | tf_op jit(solution)/shard_map/ppermute | solution.py:557
  65.8 12.1 %collective-permute-start.22 = (f32[160,128]{1,0:T(8,128)S(1)}, f32[160,128]{1,0:T(8,128)S(1)}, u32[]{:S(2)}, u32[]{:S(2)}) collective-permute-start(f32[160,128]{1,0:T(8,128)S(1)} %get-tuple-element.70), channel_id=1, source_target_pairs={{0,1},{2,3},{4,5},{6,7},{1,0},{3,2},{5,4},{7,6},{8,9},{10,11},{12,... | collective-permute-start | bytes 245768 | tf_op jit(solution)/shard_map/ppermute | solution.py:557
  70.4 7.6 %collective-permute-start.25 = (f32[128,128]{1,0:T(8,128)S(1)}, f32[128,128]{1,0:T(8,128)S(1)}, u32[]{:S(2)}, u32[]{:S(2)}) collective-permute-start(f32[128,128]{1,0:T(8,128)S(1)} %probe_last.1.rest_4_.probe_mine), channel_id=1, source_target_pairs={{0,8},{1,9},{2,10},{3,11},{4,12},{5,13},{6,14},{7,15},{8,0},{9,1},... | collective-permute-start | bytes 196616 | tf_op jit(solution)/shard_map/ppermute | solution.py:569
